TPU v7x, 256 devices: a whole 4x4x8 slice. The times are simulated.
256 devices in a mesh: req: 64 (over y_lo, x, z), tp: 4 (over y_hi, core).
Axes of the slice: x: 4, y: 4 (y_hi: 2, y_lo: 2; y = y_hi * 2 + y_lo), z: 8, core: 2. Of those that a mesh axis runs over, the one named last changes fastest.
Arguments:
- queries: bfloat16 [4096, 4, 4096], P('req', None, 'tp'), may hold values from -64 to 64
- prefix_keys: bfloat16 [4096, 512], P('req', 'tp'), may hold values from -6 to 6
- prefix_values: bfloat16 [4096, 512], P('req', 'tp'), may hold values from -6 to 6
- suffix_keys: bfloat16 [4096, 64, 512], P('req', None, 'tp'), may hold values from -9 to 9
- suffix_values: bfloat16 [4096, 64, 512], P('req', None, 'tp'), may hold values from -6 to 6
- new_keys: bfloat16 [4096, 4, 512], P('req', None, 'tp'), may hold values from -15 to 15
- new_values: bfloat16 [4096, 4, 512], P('req', None, 'tp'), may hold values from -6 to 6
- suffix_lengths: int32 [4096], P('req'), may hold values from 1 to 64, as said below
- out_weight: bfloat16 [4096, 4096], P('tp'), may hold values from -0.09375 to 0.09375
Outputs:
- attended: bfloat16 [4096, 4, 4096], P('req')
Inputs may be any that keep to these rules, and one draw needn't show every extreme that they name: `suffix_lengths`: some request has all 64 slots live.
All inputs are finite; a program needn't handle non-finite values.
Results may differ from a plain program's by a relative error of at most 0.015.
Values may be sent and summed in bfloat16 or wider, within the bound.
No kernel may reach another device: no remote copies, remote signals or barrier semaphores. Data moves between devices by JAX's collectives and lax.ppermute only.
A program may use at most 128 MiB of HBM per device.

v0:
```python
import math

import jax
import jax.numpy as jnp
from jax import lax
from jax.sharding import PartitionSpec as P

NH = 32
KVH = 4
HD = 128


def local(
    queries,
    prefix_keys,
    prefix_values,
    suffix_keys,
    suffix_values,
    new_keys,
    new_values,
    suffix_lengths,
    out_weight,
):
    rows = queries.shape[0]
    steps = queries.shape[1]
    group = NH // KVH
    kv_local = prefix_keys.shape[1] // HD
    slots = suffix_keys.shape[1]
    scale = 1.0 / math.sqrt(HD)
    query_five = queries.reshape(rows, steps, kv_local, group, HD)
    suf_keys = suffix_keys.reshape(rows, slots, kv_local, HD)
    suf_vals = suffix_values.reshape(rows, slots, kv_local, HD)
    fresh_keys = new_keys.reshape(rows, steps, kv_local, HD)
    fresh_vals = new_values.reshape(rows, steps, kv_local, HD)
    results = []
    for step in range(steps):
        chosen = query_five[:, step : step + 1]
        query_rows = chosen.transpose(2, 0, 1, 3, 4).reshape(kv_local, -1, HD)
        count = query_rows.shape[1]
        best = jnp.full((kv_local, count), -jnp.inf, jnp.float32)
        total = jnp.zeros((kv_local, count), jnp.float32)
        accum = jnp.zeros((kv_local, count, HD), jnp.float32)
        keys = lax.all_gather(prefix_keys, "req", axis=0, tiled=True).reshape(-1, kv_local, HD)
        vals = lax.all_gather(prefix_values, "req", axis=0, tiled=True).reshape(-1, kv_local, HD)
        scores = (
            jnp.einsum("kmd,nkd->kmn", query_rows, keys, preferred_element_type=jnp.float32) * scale
        )
        top = jnp.max(scores, axis=-1)
        fade = jnp.exp(best - top)
        weights = jnp.exp(scores - top[..., None])
        total = total * fade + jnp.sum(weights, axis=-1)
        accum = accum * fade[..., None] + jnp.einsum(
            "kmn,nkd->kmd", weights.astype(jnp.bfloat16), vals, preferred_element_type=jnp.float32
        )
        width = chosen.shape[1]
        finish_best = top.reshape(kv_local, rows, width, group)
        finish_total = total.reshape(kv_local, rows, width, group)
        finish_accum = accum.reshape(kv_local, rows, width, group, HD)
        s_suf = (
            jnp.einsum("rtkgd,rskd->krtgs", chosen, suf_keys, preferred_element_type=jnp.float32)
            * scale
        )
        live = jnp.arange(slots)[None, :] < suffix_lengths[:, None]
        s_suf = jnp.where(live[None, :, None, None, :], s_suf, -jnp.inf)
        s_new = (
            jnp.einsum("rtkgd,rukd->krtgu", chosen, fresh_keys, preferred_element_type=jnp.float32)
            * scale
        )
        step_ids = step + jnp.arange(width)
        causal = jnp.arange(steps)[None, :] <= step_ids[:, None]
        s_new = jnp.where(causal[None, None, :, None, :], s_new, -jnp.inf)
        finish_top = jnp.maximum(
            finish_best, jnp.maximum(jnp.max(s_suf, axis=-1), jnp.max(s_new, axis=-1))
        )
        finish_fade = jnp.exp(finish_best - finish_top)
        w_suf = jnp.exp(s_suf - finish_top[..., None])
        w_new = jnp.exp(s_new - finish_top[..., None])
        finish_total = (
            finish_total * finish_fade + jnp.sum(w_suf, axis=-1) + jnp.sum(w_new, axis=-1)
        )
        finish_accum = finish_accum * finish_fade[..., None]
        finish_accum = finish_accum + jnp.einsum(
            "krtgs,rskd->krtgd",
            w_suf.astype(jnp.bfloat16),
            suf_vals,
            preferred_element_type=jnp.float32,
        )
        finish_accum = finish_accum + jnp.einsum(
            "krtgu,rukd->krtgd",
            w_new.astype(jnp.bfloat16),
            fresh_vals,
            preferred_element_type=jnp.float32,
        )
        finish_heads_out = (finish_accum / finish_total[..., None]).astype(jnp.bfloat16)
        heads_out = finish_heads_out.transpose(1, 2, 0, 3, 4).reshape(
            rows * width, kv_local * group * HD
        )
        terms = jnp.dot(heads_out, out_weight, preferred_element_type=jnp.float32)
        results.append(lax.psum(terms.astype(jnp.bfloat16), "tp").reshape(rows, 1, -1))
    attended = jnp.concatenate(results, axis=1)
    return attended


def solution(mesh):
    in_specs = (
        P("req", None, "tp"),
        P("req", "tp"),
        P("req", "tp"),
        P("req", None, "tp"),
        P("req", None, "tp"),
        P("req", None, "tp"),
        P("req", None, "tp"),
        P("req"),
        P("tp", None),
    )
    out_specs = P("req", None, None)
    return jax.shard_map(local, mesh=mesh, in_specs=in_specs, out_specs=out_specs, check_vma=False)
```

profile of v0, /device:TPU:1, one launch (start us, length us, event | category | flops | bytes accessed | tf_op | source)
XLA Modules:
  0.0 726.0 jit_solution(11719818191584809528)
XLA Ops:
  10.1 2.0 fusion.150
  12.0 2.0 fusion.148
  14.0 2.0 fusion.146
  15.9 2.0 fusion.144
  21.4 245.1 %all-gather.3.cloned.1.call-done = bf16[4096,128]{1,0:T(8,128)(2,1)} async-done(((bf16[64,128]{1,0:T(8,128)(2,1)}), bf16[4096,128]{1,0:T(8,128)(2,1)}) %all-gather.3.cloned.1.call-update) | async-done | bytes 1048592 | tf_op jit(solution)/shard_map/all_gather | solution.py:43
  266.5 2.6 multiply_reduce_fusion.3
  269.2 3.2 copy-done.2
  272.4 1.5 fusion
  275.3 1.5 fusion.2
  276.8 4.5 multiply_reduce_fusion.1
  281.2 4.5 multiply_reduce_fusion
  287.1 275.6 %all-gather.5.cloned.1.call-done = bf16[4096,128]{1,0:T(8,128)(2,1)} async-done(((bf16[64,128]{1,0:T(8,128)(2,1)}), bf16[4096,128]{1,0:T(8,128)(2,1)}) %all-gather.5.cloned.1.call-update) | async-done | bytes 1048592 | tf_op jit(solution)/shard_map/all_gather | solution.py:44
  562.7 5.5 fusion.34
  568.8 5.3 fusion.43
  574.9 2.4 fusion.8
  577.6 2.4 fusion.9
  582.8 5.3 fusion.52
  588.9 5.9 fusion.10
  595.2 1.7 fusion.6
  597.1 5.3 fusion.61
  603.1 5.7 fusion.11
  608.9 105.9 %all-reduce.3.cloned.1.call-done = (bf16[64,1,4096]{2,0,1:T(8,128)(2,1)}, bf16[64,1,4096]{2,0,1:T(8,128)(2,1)}, bf16[64,1,4096]{2,0,1:T(8,128)(2,1)}, bf16[64,1,4096]{2,0,1:T(8,128)(2,1)}) async-done(((bf16[64,1,4096]{2,0,1:T(8,128)(2,1)}, bf16[64,1,4096]{2,0,1:T(8,128)(2,1)}, bf16[64,1,4096]{2,0,1:T(8,128)(2,1)}, bf16[64,1,4096]{2,0,1:T(8,128)(2,1)}), (bf16[64,1,4096]{2,0,1:T(8,128)(2,1)}, ...) | async-done | bytes 2097168 | tf_op jit(solution)/shard_map/psum | solution.py:99
  714.7 1.8 pad_maximum_fusion
  716.5 2.9 copy.13
  (82 shorter events, 16.0 us)
Async XLA Ops:
  6.5 561.7 %copy-start = (bf16[64,64,128]{2,1,0:T(8,128)(2,1)S(1)}, bf16[64,64,128]{2,1,0:T(8,128)(2,1)}, u32[]{:S(2)}) copy-start(bf16[64,64,128]{2,1,0:T(8,128)(2,1)} %param.13) | copy-start | bytes 3145732
  6.5 14.7 %copy-start.5 = (bf16[64,4,128]{2,1,0:T(4,128)(2,1)S(1)}, bf16[64,4,128]{2,1,0:T(4,128)(2,1)}, u32[]{:S(2)}) copy-start(bf16[64,4,128]{2,1,0:T(4,128)(2,1)} %param.14) | copy-start | bytes 196612
  6.5 260.0 %all-gather.3.cloned.1.call-start = ((), (), s32[]{:S(2)}) async-start(), calls=%async_computation | async-start | bytes 1064960 | tf_op jit(solution)/shard_map/all_gather | solution.py:43
  7.3 555.4 %all-gather.5.cloned.1.call-start = ((), (), s32[]{:S(2)}) async-start(), calls=%async_computation.1 | async-start | bytes 1064960 | tf_op jit(solution)/shard_map/all_gather | solution.py:44
  8.0 706.7 %all-reduce.3.cloned.1.call-start = ((), (), s32[]{:S(2)}) async-start(), calls=%async_computation.2 | async-start | bytes 4194304 | tf_op jit(solution)/shard_map/psum | solution.py:99
  266.5 7.4 %copy-start.3 = (bf16[4096,128]{1,0:T(8,128)(2,1)S(1)}, bf16[4096,128]{1,0:T(8,128)(2,1)}, u32[]{:S(2)}) copy-start(bf16[4096,128]{1,0:T(8,128)(2,1)} %all-gather.3.cloned.1.call-done) | copy-start | bytes 3145732
  269.2 3.2 copy-start.2
  275.3 6.0 copy-start.1
  562.7 6.0 copy-start.4
  568.3 6.6 slice-start
  568.7 5.8 copy-start.6
  568.7 6.1 slice-start.1
  577.6 2.8 slice-start.4
  577.6 3.6 slice-start.5
  588.9 6.3 slice-start.2
  588.9 6.3 slice-start.3
Sparse Core Ops, SparseCore 0:
  9.1 257.3 all-gather.2
  268.3 294.3 all-gather.4
  609.0 105.6 all-reduce.2
where the time goes:
time: 726 us
  waiting for transfers between devices  628 us (87%)
  matrix products  65 us (9%)
  between operations  13.6 us (2%)
  other arithmetic  10.3 us (1%)
  local copies, waits for them, and re-layouts  9.02 us (1%)
    all_gather x1, waiting for transfers between devices, local(): lax.all_gather(prefix_values, 'req', axis=0, tiled=True)  276 us
    all_gather x1, waiting for transfers between devices, local(): lax.all_gather(prefix_keys, 'req', axis=0, tiled=True)  245 us
    psum x1, waiting for transfers between devices, local(): lax.psum(terms.astype(jnp.bfloat16), 'tp').reshape(rows, 1, -1)  106 us
    dot_general x4, matrix products, local(): jnp.einsum('kmn,nkd->kmd', weights.astype(jnp.bfloat16), vals, preferred_...  21.4 us
    dot_general x4, matrix products, local(): terms = jnp.dot(heads_out, out_weight, preferred_element_type=jnp.float32)  16.4 us
  transfers between devices with their start and end apart: 3, of which 3 were waited for; matrix products, arithmetic and copies ran while one was open for 4% of the time, Pallas kernels for 0%

commit v1 on v0

v1 whole, which is shorter than its diff:
```python
import math

import jax
import jax.numpy as jnp
from jax import lax
from jax.experimental import pallas as pl
from jax.experimental.pallas import tpu as pltpu
from jax.sharding import Mesh, PartitionSpec as P

HD = 128
GROUP = 8
STEPS = 4
SLOTS = 64
TOK = 16
PACK = TOK * GROUP
SCALE = math.log2(math.e) / math.sqrt(HD)
LOW = -1e30

E_PAIRS = [(i, i ^ 1) for i in range(8)]
O_PAIRS = [(i, (i + 1) % 8 if i % 2 else (i - 1) % 8) for i in range(8)]


def dot_t(a, b):
    return lax.dot_general(a, b, (((1,), (1,)), ((), ())), preferred_element_type=jnp.float32)


def dot(a, b):
    return jnp.dot(a, b, preferred_element_type=jnp.float32)


def with_ones(v):
    return jnp.concatenate([v, jnp.ones_like(v)], axis=1)


def row_max(s):
    return jnp.max(s, axis=1, keepdims=True)


def suffix_body(q_ref, sk_ref, sv_ref, nk_ref, nv_ref, bias_ref, qp_ref, m_ref, acc_ref):
    packs = q_ref.shape[0] // TOK
    keys = TOK // STEPS * SLOTS
    row = lax.broadcasted_iota(jnp.int32, (PACK, keys), 0)
    col = lax.broadcasted_iota(jnp.int32, (PACK, keys), 1)
    same = ((row >> 2) & 3) == (col >> 6)
    row_n = lax.broadcasted_iota(jnp.int32, (PACK, TOK), 0)
    col_n = lax.broadcasted_iota(jnp.int32, (PACK, TOK), 1)
    same_n = (((row_n >> 2) & 3) == (col_n >> 2)) & ((col_n & 3) <= (row_n & 3))
    for g in range(packs):
        block = q_ref[g * TOK : (g + 1) * TOK, :]
        q = jnp.concatenate([block[:, h * HD : (h + 1) * HD] for h in range(GROUP)], axis=0)
        rows = pl.ds(g * PACK, PACK)
        qp_ref[rows, :] = q
        k = sk_ref[g * keys : (g + 1) * keys, :]
        v = sv_ref[g * keys : (g + 1) * keys, :]
        s = dot_t(q, k) * SCALE + bias_ref[g]
        s = jnp.where(same, s, LOW)
        s_n = dot_t(q, nk_ref[g * TOK : (g + 1) * TOK, :]) * SCALE
        s_n = jnp.where(same_n, s_n, LOW)
        m = jnp.maximum(row_max(s), row_max(s_n))
        p = jnp.exp2(s - m).astype(jnp.bfloat16)
        p_n = jnp.exp2(s_n - m).astype(jnp.bfloat16)
        acc = dot(p, with_ones(v)) + dot(p_n, with_ones(nv_ref[g * TOK : (g + 1) * TOK, :]))
        m_ref[rows, :] = jnp.broadcast_to(m, (PACK, HD))
        acc_ref[rows, :] = acc


def suffix(q, sk, sv, nk, nv, bias):
    rows = q.shape[0] * GROUP
    grid = 4
    part = lambda a: pl.BlockSpec((a.shape[0] // grid,) + a.shape[1:], lambda i: (i,) + (0,) * (a.ndim - 1))
    outs = [
        jax.ShapeDtypeStruct((rows, HD), jnp.bfloat16),
        jax.ShapeDtypeStruct((rows, HD), jnp.float32),
        jax.ShapeDtypeStruct((rows, 2 * HD), jnp.float32),
    ]
    return pl.pallas_call(
        suffix_body,
        grid=(grid,),
        in_specs=[part(a) for a in (q, sk, sv, nk, nv, bias)],
        out_specs=[part(o) for o in outs],
        out_shape=outs,
        cost_estimate=pl.CostEstimate(flops=300_000_000, bytes_accessed=6_000_000, transcendentals=600_000),
        compiler_params=pltpu.CompilerParams(vmem_limit_bytes=24 * 1024 * 1024),
        name="suffix",
    )(q, sk, sv, nk, nv, bias)


def step(q, m, acc, kvs):
    parts = [dot_t(q, kv[:, :HD]) for kv in kvs]
    top = row_max(parts[0])
    for s in parts[1:]:
        top = jnp.maximum(top, row_max(s))
    new = jnp.maximum(m, top * SCALE)
    acc = acc * jnp.exp2(m - new)[:, :1]
    for s, kv in zip(parts, kvs):
        p = jnp.exp2(s * SCALE - new[:, :1]).astype(jnp.bfloat16)
        acc = acc + dot(p, with_ones(kv[:, HD:]))
    return new, acc


def prefix_body(n, *refs):
    q_ref, m_ref, acc_ref = refs[:3]
    m_out, acc_out = refs[3 + n :]
    new, acc = step(q_ref[...], m_ref[...], acc_ref[...], [r[...] for r in refs[3 : 3 + n]])
    m_out[...] = new
    acc_out[...] = acc


def final_body(n, *refs):
    q_ref, m_ref, acc_ref = refs[:3]
    out_ref = refs[3 + n]
    _, acc = step(q_ref[...], m_ref[...], acc_ref[...], [r[...] for r in refs[3 : 3 + n]])
    heads = (acc[:, :HD] / acc[:, HD:]).astype(jnp.bfloat16)
    for g in range(heads.shape[0] // PACK):
        for h in range(GROUP):
            first = g * PACK + h * TOK
            out_ref[g * TOK : (g + 1) * TOK, h * HD : (h + 1) * HD] = heads[first : first + TOK, :]


def prefix(q, m, acc, kvs, tile=256):
    rows = q.shape[0]
    part = lambda a: pl.BlockSpec((tile, a.shape[1]), lambda i: (i, 0))
    whole = lambda a: pl.BlockSpec(a.shape, lambda i: (0, 0))
    keys = sum(kv.shape[0] for kv in kvs)
    return pl.pallas_call(
        lambda *refs: prefix_body(len(kvs), *refs),
        grid=(rows // tile,),
        in_specs=[part(q), part(m), part(acc)] + [whole(kv) for kv in kvs],
        out_specs=[part(m), part(acc)],
        out_shape=[jax.ShapeDtypeStruct(m.shape, m.dtype), jax.ShapeDtypeStruct(acc.shape, acc.dtype)],
        cost_estimate=pl.CostEstimate(flops=rows * keys * HD * 8, bytes_accessed=7_000_000, transcendentals=rows * keys),
        compiler_params=pltpu.CompilerParams(vmem_limit_bytes=24 * 1024 * 1024),
        name="prefix",
    )(q, m, acc, *kvs)


def final(q, m, acc, kvs, chunk, chunks, tile=256):
    rows = q.shape[0] // chunks
    steps = rows // tile
    part = lambda a: pl.BlockSpec((tile, a.shape[1]), lambda i: (i + chunk * steps, 0))
    whole = lambda a: pl.BlockSpec(a.shape, lambda i: (0, 0))
    keys = sum(kv.shape[0] for kv in kvs)
    return pl.pallas_call(
        lambda *refs: final_body(len(kvs), *refs),
        grid=(steps,),
        in_specs=[part(q), part(m), part(acc)] + [whole(kv) for kv in kvs],
        out_specs=pl.BlockSpec((tile // GROUP, GROUP * HD), lambda i: (i, 0)),
        out_shape=jax.ShapeDtypeStruct((rows // GROUP, GROUP * HD), jnp.bfloat16),
        cost_estimate=pl.CostEstimate(flops=rows * keys * HD * 8, bytes_accessed=2_000_000, transcendentals=rows * keys),
        compiler_params=pltpu.CompilerParams(vmem_limit_bytes=24 * 1024 * 1024),
        name="final",
    )(q, m, acc, *kvs)


def local(queries, prefix_keys, prefix_values, suffix_keys, suffix_values, new_keys, new_values, suffix_lengths, out_weight):
    requests = queries.shape[0]
    tokens = requests * STEPS
    half = out_weight.shape[1] // 2
    core = lax.axis_index("core")
    even = lambda a: lax.ppermute(a, "z", E_PAIRS)
    odd = lambda a: lax.ppermute(a, "z", O_PAIRS)
    x1 = lambda a: lax.ppermute(a, "x", [(i, i ^ 1) for i in range(4)])
    x3 = lambda a: lax.ppermute(a, "x", [(i, i ^ 3) for i in range(4)])
    y = lambda a: lax.ppermute(a, "ylo", [(0, 1), (1, 0)])
    swap_core = lambda a: lax.ppermute(a, "core", [(0, 1), (1, 0)])
    swap_y = lambda a: lax.ppermute(a, "yhi", [(0, 1), (1, 0)])

    kv = jnp.concatenate([prefix_keys, prefix_values], axis=1)
    pair = jnp.concatenate([kv, even(kv)], axis=0)
    r2 = odd(pair)
    r3 = even(r2)
    r4 = odd(r3)
    line = jnp.concatenate([pair, r2, r3, r4], axis=0)
    b_x1, b_x3, b_y = x1(line), x3(line), y(line)
    b_yx1, b_yx3 = x1(b_y), x3(b_y)
    b_far = x1(b_x3)
    b_yfar = x3(b_yx1)

    weight_mine = lax.dynamic_slice(out_weight, (0, core * half), (out_weight.shape[0], half))
    weight_other = swap_core(lax.dynamic_slice(out_weight, (0, (1 - core) * half), (out_weight.shape[0], half)))

    flat = lambda a: a.reshape(-1, a.shape[-1])
    live = jnp.arange(SLOTS)[None, :] < suffix_lengths[:, None]
    bias = jnp.where(live, 0.0, LOW).astype(jnp.float32).reshape(tokens // TOK, 1, TOK // STEPS * SLOTS)
    q, m, acc = suffix(flat(queries), flat(suffix_keys), flat(suffix_values), flat(new_keys), flat(new_values), bias)
    m, acc = prefix(q, m, acc, [line])
    m, acc = prefix(q, m, acc, [b_x1, b_x3, b_y])
    m, acc = prefix(q, m, acc, [b_yx1, b_yx3])
    chunks = 4
    results = []
    for chunk in range(chunks):
        mine = final(q, m, acc, [b_far, b_yfar], chunk, chunks)
        other = swap_core(mine)
        terms = dot(mine, weight_mine) + dot(other, weight_other)
        total = (terms + swap_y(terms.astype(jnp.bfloat16)).astype(jnp.float32)).astype(jnp.bfloat16)
        rest = swap_core(total)
        left = jnp.where(core == 0, total, rest)
        right = jnp.where(core == 0, rest, total)
        results.append(jnp.concatenate([left, right], axis=1).reshape(requests // chunks, STEPS, 2 * half))
    return jnp.concatenate(results, axis=0)


def solution(mesh):
    fine = Mesh(mesh.devices.reshape(2, 4, 8, 2, 2), ("ylo", "x", "z", "yhi", "core"))
    req, tp = ("ylo", "x", "z"), ("yhi", "core")
    in_specs = (
        P(req, None, tp),
        P(req, tp),
        P(req, tp),
        P(req, None, tp),
        P(req, None, tp),
        P(req, None, tp),
        P(req, None, tp),
        P(req),
        P(tp, None),
    )
    return jax.shard_map(local, mesh=fine, in_specs=in_specs, out_specs=P(req, None, None), check_vma=False)
```

time: 726 us -> 115 us (0.16)
  waiting for transfers between devices: 628 us -> 14.3 us
  matrix products: 65 us -> 15.5 us
  starting transfers between devices: 0.08 us -> 37.4 us
  Pallas kernels: 0 us -> 36.4 us
  between operations: 13.6 us -> 0.41 us
    all_gather x2 -> x0, waiting for transfers between devices: 521 us -> none  [the longest x1 276 us: local(): lax.all_gather(prefix_values, 'req', axis=0, tiled=True)]
    psum x1 -> x0, waiting for transfers between devices: 106 us -> none  [local(): lax.psum(terms.astype(jnp.bfloat16), 'tp').reshape(rows, 1, -1)]
    dot_general x28 -> x8, matrix products: 65 us -> 15.5 us  [dot(): return jnp.dot(a, b, preferred_element_type=jnp.float32)]
    ppermute x0 -> x24, starting transfers between devices: none -> 37.4 us  [the longest x9 16.3 us: local(): swap_core = lambda a: lax.ppermute(a, 'core', [(0, 1), (1, 0)])]
    pallas_call x0 -> x8, Pallas kernels: none -> 36.4 us  [the longest x3 23.9 us: prefix(): pl.pallas_call(lambda *refs: prefix_body(len(kvs), *refs), grid=(rows //...]
    ppermute x0 -> x24, waiting for transfers between devices: none -> 14.3 us  [the longest x2 5.86 us: local(): even = lambda a: lax.ppermute(a, 'z', E_PAIRS)]
    reduce_sum x12 -> x0, other arithmetic: 7.59 us -> none  [the longest x4 6.23 us: local(): total = total * fade + jnp.sum(weights, axis=-1)]
  transfers between devices with their start and end apart: 3 -> 24, of which waited for: 3 -> 7; matrix products, arithmetic and copies ran while one was open for 4% -> 15% of each run, Pallas kernels for 0% -> 32%
where the time goes in v1:
time: 115 us; the launch traced here: 114 us
  starting transfers between devices  37.4 us (33%)
  Pallas kernels  36.4 us (32%)
  matrix products  15.5 us (13%)
  waiting for transfers between devices  14.3 us (12%)
  local copies, waits for them, and re-layouts  7.26 us (6%)
  other arithmetic  3.05 us (3%)
    pallas_call x3, Pallas kernels, prefix(): pl.pallas_call(lambda *refs: prefix_body(len(kvs), *refs), grid=(rows //...  23.9 us
    ppermute x9, starting transfers between devices, local(): swap_core = lambda a: lax.ppermute(a, 'core', [(0, 1), (1, 0)])  16.3 us
    dot_general x8, matrix products, dot(): return jnp.dot(a, b, preferred_element_type=jnp.float32)  15.5 us
    pallas_call x4, Pallas kernels, final(): pl.pallas_call(lambda *refs: final_body(len(kvs), *refs), grid=(steps,),...  8.14 us
    ppermute x2, starting transfers between devices, local(): odd = lambda a: lax.ppermute(a, 'z', O_PAIRS)  6.53 us
    ppermute x4, starting transfers between devices, local(): swap_y = lambda a: lax.ppermute(a, 'yhi', [(0, 1), (1, 0)])  6.29 us
    ppermute x2, waiting for transfers between devices, local(): even = lambda a: lax.ppermute(a, 'z', E_PAIRS)  5.86 us
    ppermute x3, starting transfers between devices, local(): x3 = lambda a: lax.ppermute(a, 'x', [(i, i ^ 3) for i in range(4)])  5.11 us
  transfers between devices with their start and end apart: 24, of which 7 were waited for; matrix products, arithmetic and copies ran while one was open for 15% of the time, Pallas kernels for 32%

profile of v1, /device:TPU:1, one launch (start us, length us, event | category | flops | bytes accessed | tf_op | source)
XLA Modules:
  0.0 114.3 jit_solution(12800475624592260902)
XLA Ops:
  0.0 4.9 %constant_dynamic-slice_fusion = bf16[1024,2048]{1,0:T(8,128)(2,1)} fusion(bf16[1024,4096]{1,0:T(8,128)(2,1)} %param.17, s32[]{:T(128)S(6)} %select_n.56), kind=kLoop, calls=%fused_computation.42 | loop fusion | bytes 8388612 | tf_op jit(solution)/shard_map/dynamic_slice | solution.py:180
  4.9 3.2 %collective-permute-start.12 = (bf16[1024,2048]{1,0:T(8,128)(2,1)}, bf16[1024,2048]{1,0:T(8,128)(2,1)}, u32[]{:S(2)}, u32[]{:S(2)}) collective-permute-start(bf16[1024,2048]{1,0:T(8,128)(2,1)} %constant_dynamic-slice_fusion), channel_id=1, source_target_pairs={{0,1},{1,0},{2,3},{3,2},{4,5},{5,4},{6,7},{7,6},{8,9},{9,8},{10,11... | collective-permute-start | bytes 12582920 | tf_op jit(solution)/shard_map/ppermute | solution.py:165
  8.3 2.8 %collective-permute-done = bf16[64,256]{1,0:T(8,128)(2,1)S(1)} collective-permute-done((bf16[64,256]{1,0:T(8,128)(2,1)S(1)}, bf16[64,256]{1,0:T(8,128)(2,1)S(1)}, u32[]{:S(2)}, u32[]{:S(2)}) %collective-permute-start) | collective-permute-done | bytes 32800 | tf_op jit(solution)/shard_map/ppermute | solution.py:160
  11.1 3.9 %collective-permute-start.1 = (bf16[128,256]{1,0:T(8,128)(2,1)S(1)}, bf16[128,256]{1,0:T(8,128)(2,1)S(1)}, u32[]{:S(2)}, u32[]{:S(2)}) collective-permute-start(bf16[128,256]{1,0:T(8,128)(2,1)S(1)} %pad_maximum_fusion.5), channel_id=1, source_target_pairs={{0,28},{4,8},{8,4},{12,16},{16,12},{20,24},{24,20},{28,0},{1,29},{... | collective-permute-start | bytes 196616 | tf_op jit(solution)/shard_map/ppermute | solution.py:161
  16.6 3.1 %collective-permute-done.2 = bf16[128,256]{1,0:T(8,128)(2,1)S(1)} collective-permute-done((bf16[128,256]{1,0:T(8,128)(2,1)S(1)}, bf16[128,256]{1,0:T(8,128)(2,1)S(1)}, u32[]{:S(2)}, u32[]{:S(2)}) %collective-permute-start.2) | collective-permute-done | bytes 65568 | tf_op jit(solution)/shard_map/ppermute | solution.py:160
  19.7 2.7 %collective-permute-start.3 = (bf16[128,256]{1,0:T(8,128)(2,1)S(1)}, bf16[128,256]{1,0:T(8,128)(2,1)S(1)}, u32[]{:S(2)}, u32[]{:S(2)}) collective-permute-start(bf16[128,256]{1,0:T(8,128)(2,1)S(1)} %collective-permute-done.2), channel_id=1, source_target_pairs={{0,28},{4,8},{8,4},{12,16},{16,12},{20,24},{24,20},{28,0},{1,29},{... | collective-permute-start | bytes 196616 | tf_op jit(solution)/shard_map/ppermute | solution.py:161
  26.9 2.6 %collective-permute-start.5 = (bf16[512,256]{1,0:T(8,128)(2,1)S(1)}, bf16[512,256]{1,0:T(8,128)(2,1)S(1)}, u32[]{:S(2)}, u32[]{:S(2)}) collective-permute-start(bf16[512,256]{1,0:T(8,128)(2,1)S(1)} %constant_dynamic-update-slice_fusion.2.refs_3_), channel_id=1, source_target_pairs={{0,96},{32,64},{64,32},{96,0},{1,97},{33,65},{65,33},{97,1},{2,98}... | collective-permute-start | bytes 786440 | tf_op jit(solution)/shard_map/ppermute | solution.py:163
  30.9 4.3 %suffix.1 = (bf16[2048,128]{1,0:T(8,128)(2,1)S(1)}, f32[2048,128]{1,0:T(8,128)S(1)}, f32[2048,256]{1,0:T(8,128)S(1)}) custom-call(bf16[256,1024]{1,0:T(8,128)(2,1)S(1)} %reshape.71.q_ref, bf16[4096,128]{1,0:T(8,128)(2,1)S(1)} %bitcast.16, bf16[4096,128]{1,0:T(8,128)(2,1)S(1)} %bitcast.17, bf16[256,128]{1,0:T(8,128)(2,1)S(1)} %bitcast.18, ...), custom_call_target="tpu_custom_call" | custom-call | flops 300000000 | bytes 6000000 | tf_op jit(solution)/shard_map/suffix/pallas_call | solution.py:76
  35.3 5.7 %prefix.3 = (f32[2048,128]{1,0:T(8,128)S(1)}, f32[2048,256]{1,0:T(8,128)S(1)}) custom-call(bf16[2048,128]{1,0:T(8,128)(2,1)S(1)} %get-tuple-element.14.refs_0_, f32[2048,128]{1,0:T(8,128)S(1)} %get-tuple-element.15.refs_1_, f32[2048,256]{1,0:T(8,128)S(1)} %get-tuple-element.16.refs_2_, bf16[512,256]{1,0:T(8,128)(2,1)S(1)} %constant_dynamic-update-slice_fusion.2.refs_3_), custom_call_target="tpu_custom_call" | custom-call | flops 1073741824 | bytes 7000000 | tf_op jit(solution)/shard_map/prefix/pallas_call | solution.py:125
  43.9 10.1 %prefix.4 = (f32[2048,128]{1,0:T(8,128)S(1)}, f32[2048,256]{1,0:T(8,128)S(1)}) custom-call(bf16[2048,128]{1,0:T(8,128)(2,1)S(1)} %get-tuple-element.14.refs_0_, f32[2048,128]{1,0:T(8,128)S(1)} %get-tuple-element.17.refs_1_, f32[2048,256]{1,0:T(8,128)S(1)} %get-tuple-element.18.refs_2_, bf16[512,256]{1,0:T(8,128)(2,1)S(1)} %collective-permute-done.4.refs_3_, ...), custom_call_target="tpu_custom_call" | custom-call | flops 3221225472 | bytes 7000000 | tf_op jit(solution)/shard_map/prefix/pallas_call | solution.py:125
  54.0 8.1 %prefix.5 = (f32[2048,128]{1,0:T(8,128)S(1)}, f32[2048,256]{1,0:T(8,128)S(1)}) custom-call(bf16[2048,128]{1,0:T(8,128)(2,1)S(1)} %get-tuple-element.14.refs_0_, f32[2048,128]{1,0:T(8,128)S(1)} %get-tuple-element.19.refs_1_, f32[2048,256]{1,0:T(8,128)S(1)} %get-tuple-element.20.refs_2_, bf16[512,256]{1,0:T(8,128)(2,1)S(1)} %collective-permute-done.7.refs_3_, ...), custom_call_target="tpu_custom_call" | custom-call | flops 2147483648 | bytes 7000000 | tf_op jit(solution)/shard_map/prefix/pallas_call | solution.py:125
  62.1 2.0 %final.7 = bf16[64,1024]{1,0:T(8,128)(2,1)S(1)} custom-call(bf16[2048,128]{1,0:T(8,128)(2,1)S(1)} %get-tuple-element.14.refs_0_, f32[2048,128]{1,0:T(8,128)S(1)} %get-tuple-element.21.refs_1_, f32[2048,256]{1,0:T(8,128)S(1)} %get-tuple-element.22.refs_2_, bf16[512,256]{1,0:T(8,128)(2,1)S(1)} %collective-permute-done.9.refs_3_, ...), custom_call_target="tpu_custom_call" | custom-call | flops 536870912 | bytes 2000000 | tf_op jit(solution)/shard_map/final/pallas_call | solution.py:143
  64.2 6.3 %collective-permute-start.21 = (bf16[64,1024]{1,0:T(8,128)(2,1)S(1)}, bf16[64,1024]{1,0:T(8,128)(2,1)S(1)}, u32[]{:S(2)}, u32[]{:S(2)}) collective-permute-start(bf16[64,1024]{1,0:T(8,128)(2,1)S(1)} %final.7), channel_id=1, source_target_pairs={{0,1},{1,0},{2,3},{3,2},{4,5},{5,4},{6,7},{7,6},{8,9},{9,8},{10,11... | collective-permute-start | bytes 393224 | tf_op jit(solution)/shard_map/ppermute | solution.py:165
  72.6 2.0 %final.5 = bf16[64,1024]{1,0:T(8,128)(2,1)S(1)} custom-call(bf16[2048,128]{1,0:T(8,128)(2,1)S(1)} %get-tuple-element.14.refs_0_, f32[2048,128]{1,0:T(8,128)S(1)} %get-tuple-element.21.refs_1_, f32[2048,256]{1,0:T(8,128)S(1)} %get-tuple-element.22.refs_2_, bf16[512,256]{1,0:T(8,128)(2,1)S(1)} %collective-permute-done.9.refs_3_, ...), custom_call_target="tpu_custom_call" | custom-call | flops 536870912 | bytes 2000000 | tf_op jit(solution)/shard_map/final/pallas_call | solution.py:143
  77.4 3.0 %fusion.31 = f32[64,2048]{1,0:T(8,128)S(1)} fusion(bf16[64,1024]{1,0:T(8,128)(2,1)S(1)} %collective-permute-done.21, bf16[1024,2048]{1,0:T(8,128)(2,1)} %collective-permute-done.12), kind=kOutput, calls=%fused_computation.51 | convolution fusion | flops 268435456 | bytes 4849664 | tf_op jit(solution)/shard_map/dot_general | solution.py:28
  81.3 3.0 %collective-permute-start.22 = (bf16[64,2048]{1,0:T(8,128)(2,1)S(1)}, bf16[64,2048]{1,0:T(8,128)(2,1)S(1)}, u32[]{:S(2)}, u32[]{:S(2)}) collective-permute-start(bf16[64,2048]{1,0:T(8,128)(2,1)S(1)} %get-tuple-element.35), channel_id=1, source_target_pairs={{0,2},{2,0},{1,3},{3,1},{4,6},{6,4},{5,7},{7,5},{8,10},{10,8},{9,1... | collective-permute-start | bytes 786440 | tf_op jit(solution)/shard_map/ppermute | solution.py:166
  84.3 3.0 %fusion.30 = f32[64,2048]{1,0:T(8,128)S(1)} fusion(bf16[64,1024]{1,0:T(8,128)(2,1)S(1)} %collective-permute-done.18, bf16[1024,2048]{1,0:T(8,128)(2,1)} %collective-permute-done.12), kind=kOutput, calls=%fused_computation.50 | convolution fusion | flops 268435456 | bytes 4849664 | tf_op jit(solution)/shard_map/dot_general | solution.py:28
  88.3 3.0 %fusion.29 = f32[64,2048]{1,0:T(8,128)S(1)} fusion(bf16[64,1024]{1,0:T(8,128)(2,1)S(1)} %collective-permute-done.15, bf16[1024,2048]{1,0:T(8,128)(2,1)} %collective-permute-done.12), kind=kOutput, calls=%fused_computation.49 | convolution fusion | flops 268435456 | bytes 4849664 | tf_op jit(solution)/shard_map/dot_general | solution.py:28
  92.3 3.0 %collective-permute-start.16 = (bf16[64,2048]{1,0:T(8,128)(2,1)S(1)}, bf16[64,2048]{1,0:T(8,128)(2,1)S(1)}, u32[]{:S(2)}, u32[]{:S(2)}) collective-permute-start(bf16[64,2048]{1,0:T(8,128)(2,1)S(1)} %get-tuple-element.39), channel_id=1, source_target_pairs={{0,2},{2,0},{1,3},{3,1},{4,6},{6,4},{5,7},{7,5},{8,10},{10,8},{9,1... | collective-permute-start | bytes 786440 | tf_op jit(solution)/shard_map/ppermute | solution.py:166
  95.2 3.0 %fusion.28 = f32[64,2048]{1,0:T(8,128)S(1)} fusion(bf16[64,1024]{1,0:T(8,128)(2,1)S(1)} %collective-permute-done.11, bf16[1024,2048]{1,0:T(8,128)(2,1)} %collective-permute-done.12), kind=kOutput, calls=%fused_computation.48 | convolution fusion | flops 268435456 | bytes 4849664 | tf_op jit(solution)/shard_map/dot_general | solution.py:28
  102.5 2.1 %collective-permute-start.17 = (bf16[64,2048]{1,0:T(8,128)(2,1)S(1)}, bf16[64,2048]{1,0:T(8,128)(2,1)S(1)}, u32[]{:S(2)}, u32[]{:S(2)}) collective-permute-start(bf16[64,2048]{1,0:T(8,128)(2,1)S(1)} %add_convert_fusion.2), channel_id=1, source_target_pairs={{0,1},{1,0},{2,3},{3,2},{4,5},{5,4},{6,7},{7,6},{8,9},{9,8},{10,11... | collective-permute-start | bytes 786440 | tf_op jit(solution)/shard_map/ppermute | solution.py:165
  104.7 3.1 %collective-permute-done.13 = bf16[64,2048]{1,0:T(8,128)(2,1)S(1)} collective-permute-done((bf16[64,2048]{1,0:T(8,128)(2,1)S(1)}, bf16[64,2048]{1,0:T(8,128)(2,1)S(1)}, u32[]{:S(2)}, u32[]{:S(2)}) %collective-permute-start.13) | collective-permute-done | bytes 262176 | tf_op jit(solution)/shard_map/ppermute | solution.py:166
  107.8 2.1 %collective-permute-start.14 = (bf16[64,2048]{1,0:T(8,128)(2,1)S(1)}, bf16[64,2048]{1,0:T(8,128)(2,1)S(1)}, u32[]{:S(2)}, u32[]{:S(2)}) collective-permute-start(bf16[64,2048]{1,0:T(8,128)(2,1)S(1)} %add_convert_fusion.3), channel_id=1, source_target_pairs={{0,1},{1,0},{2,3},{3,2},{4,5},{5,4},{6,7},{7,6},{8,9},{9,8},{10,11... | collective-permute-start | bytes 786440 | tf_op jit(solution)/shard_map/ppermute | solution.py:165
  111.8 2.5 %pad_maximum_fusion = bf16[64,4,4096]{2,1,0:T(4,128)(2,1)} fusion(bf16[16,4,4096]{2,1,0:T(4,128)(2,1)S(1)} %reshape.79, bf16[16,4,4096]{2,1,0:T(4,128)(2,1)S(1)} %reshape.78, bf16[16,4,4096]{2,1,0:T(4,128)(2,1)S(1)} %reshape.77, bf16[16,4,4096]{2,1,0:T(4,128)(2,1)S(1)} %reshape.76), kind=kLoop, calls=%fused_computation.12 | loop fusion | flops 3145728 | bytes 4194304 | tf_op jit(solution)/shard_map/concatenate | solution.py:200
  (89 shorter events, 24.5 us)
Async XLA Ops:
  4.9 72.4 %collective-permute-start.12 = (bf16[1024,2048]{1,0:T(8,128)(2,1)}, bf16[1024,2048]{1,0:T(8,128)(2,1)}, u32[]{:S(2)}, u32[]{:S(2)}) collective-permute-start(bf16[1024,2048]{1,0:T(8,128)(2,1)} %constant_dynamic-slice_fusion), channel_id=1, source_target_pairs={{0,1},{1,0},{2,3},{3,2},{4,5},{5,4},{6,7},{7,6},{8,9},{9,8},{10,11... | collective-permute-start | bytes 12582920 | tf_op jit(solution)/shard_map/ppermute | solution.py:165
  8.2 2.9 %collective-permute-start = (bf16[64,256]{1,0:T(8,128)(2,1)S(1)}, bf16[64,256]{1,0:T(8,128)(2,1)S(1)}, u32[]{:S(2)}, u32[]{:S(2)}) collective-permute-start(bf16[64,256]{1,0:T(8,128)(2,1)S(1)} %get-tuple-element.31), channel_id=1, source_target_pairs={{0,4},{4,0},{8,12},{12,8},{16,20},{20,16},{24,28},{28,24},{1,5},{5... | collective-permute-start | bytes 98312 | tf_op jit(solution)/shard_map/ppermute | solution.py:160
  11.1 5.5 %collective-permute-start.1 = (bf16[128,256]{1,0:T(8,128)(2,1)S(1)}, bf16[128,256]{1,0:T(8,128)(2,1)S(1)}, u32[]{:S(2)}, u32[]{:S(2)}) collective-permute-start(bf16[128,256]{1,0:T(8,128)(2,1)S(1)} %pad_maximum_fusion.5), channel_id=1, source_target_pairs={{0,28},{4,8},{8,4},{12,16},{16,12},{20,24},{24,20},{28,0},{1,29},{... | collective-permute-start | bytes 196616 | tf_op jit(solution)/shard_map/ppermute | solution.py:161
  16.6 3.1 %collective-permute-start.2 = (bf16[128,256]{1,0:T(8,128)(2,1)S(1)}, bf16[128,256]{1,0:T(8,128)(2,1)S(1)}, u32[]{:S(2)}, u32[]{:S(2)}) collective-permute-start(bf16[128,256]{1,0:T(8,128)(2,1)S(1)} %collective-permute-done.1), channel_id=1, source_target_pairs={{0,4},{4,0},{8,12},{12,8},{16,20},{20,16},{24,28},{28,24},{1,5},{5... | collective-permute-start | bytes 196616 | tf_op jit(solution)/shard_map/ppermute | solution.py:160
  19.7 4.3 %collective-permute-start.3 = (bf16[128,256]{1,0:T(8,128)(2,1)S(1)}, bf16[128,256]{1,0:T(8,128)(2,1)S(1)}, u32[]{:S(2)}, u32[]{:S(2)}) collective-permute-start(bf16[128,256]{1,0:T(8,128)(2,1)S(1)} %collective-permute-done.2), channel_id=1, source_target_pairs={{0,28},{4,8},{8,4},{12,16},{16,12},{20,24},{24,20},{28,0},{1,29},{... | collective-permute-start | bytes 196616 | tf_op jit(solution)/shard_map/ppermute | solution.py:161
  24.0 5.4 %collective-permute-start.6 = (bf16[512,256]{1,0:T(8,128)(2,1)S(1)}, bf16[512,256]{1,0:T(8,128)(2,1)S(1)}, u32[]{:S(2)}, u32[]{:S(2)}) collective-permute-start(bf16[512,256]{1,0:T(8,128)(2,1)S(1)} %constant_dynamic-update-slice_fusion.2.refs_3_), channel_id=1, source_target_pairs={{0,128},{128,0},{1,129},{129,1},{2,130},{130,2},{3,131},{131,3},{4... | collective-permute-start | bytes 786440 | tf_op jit(solution)/shard_map/ppermute | solution.py:164
  26.9 15.6 %collective-permute-start.5 = (bf16[512,256]{1,0:T(8,128)(2,1)S(1)}, bf16[512,256]{1,0:T(8,128)(2,1)S(1)}, u32[]{:S(2)}, u32[]{:S(2)}) collective-permute-start(bf16[512,256]{1,0:T(8,128)(2,1)S(1)} %constant_dynamic-update-slice_fusion.2.refs_3_), channel_id=1, source_target_pairs={{0,96},{32,64},{64,32},{96,0},{1,97},{33,65},{65,33},{97,1},{2,98}... | collective-permute-start | bytes 786440 | tf_op jit(solution)/shard_map/ppermute | solution.py:163
  29.4 14.5 %collective-permute-start.4 = (bf16[512,256]{1,0:T(8,128)(2,1)S(1)}, bf16[512,256]{1,0:T(8,128)(2,1)S(1)}, u32[]{:S(2)}, u32[]{:S(2)}) collective-permute-start(bf16[512,256]{1,0:T(8,128)(2,1)S(1)} %constant_dynamic-update-slice_fusion.2.refs_3_), channel_id=1, source_target_pairs={{0,32},{32,0},{64,96},{96,64},{1,33},{33,1},{65,97},{97,65},{2,34}... | collective-permute-start | bytes 786440 | tf_op jit(solution)/shard_map/ppermute | solution.py:162
  29.4 13.4 %collective-permute-start.7 = (bf16[512,256]{1,0:T(8,128)(2,1)S(1)}, bf16[512,256]{1,0:T(8,128)(2,1)S(1)}, u32[]{:S(2)}, u32[]{:S(2)}) collective-permute-start(bf16[512,256]{1,0:T(8,128)(2,1)S(1)} %collective-permute-done.6.refs_5_), channel_id=1, source_target_pairs={{0,32},{32,0},{64,96},{96,64},{1,33},{33,1},{65,97},{97,65},{2,34}... | collective-permute-start | bytes 786440 | tf_op jit(solution)/shard_map/ppermute | solution.py:162
  41.0 13.0 %collective-permute-start.8 = (bf16[512,256]{1,0:T(8,128)(2,1)S(1)}, bf16[512,256]{1,0:T(8,128)(2,1)S(1)}, u32[]{:S(2)}, u32[]{:S(2)}) collective-permute-start(bf16[512,256]{1,0:T(8,128)(2,1)S(1)} %collective-permute-done.6.refs_5_), channel_id=1, source_target_pairs={{0,96},{32,64},{64,32},{96,0},{1,97},{33,65},{65,33},{97,1},{2,98}... | collective-permute-start | bytes 786440 | tf_op jit(solution)/shard_map/ppermute | solution.py:163
  42.5 19.6 %collective-permute-start.9 = (bf16[512,256]{1,0:T(8,128)(2,1)S(1)}, bf16[512,256]{1,0:T(8,128)(2,1)S(1)}, u32[]{:S(2)}, u32[]{:S(2)}) collective-permute-start(bf16[512,256]{1,0:T(8,128)(2,1)S(1)} %collective-permute-done.5.refs_4_), channel_id=1, source_target_pairs={{0,32},{32,0},{64,96},{96,64},{1,33},{33,1},{65,97},{97,65},{2,34}... | collective-permute-start | bytes 786440 | tf_op jit(solution)/shard_map/ppermute | solution.py:162
  42.8 19.3 %collective-permute-start.10 = (bf16[512,256]{1,0:T(8,128)(2,1)S(1)}, bf16[512,256]{1,0:T(8,128)(2,1)S(1)}, u32[]{:S(2)}, u32[]{:S(2)}) collective-permute-start(bf16[512,256]{1,0:T(8,128)(2,1)S(1)} %collective-permute-done.7.refs_3_), channel_id=1, source_target_pairs={{0,96},{32,64},{64,32},{96,0},{1,97},{33,65},{65,33},{97,1},{2,98}... | collective-permute-start | bytes 786440 | tf_op jit(solution)/shard_map/ppermute | solution.py:163
  64.2 13.2 %collective-permute-start.21 = (bf16[64,1024]{1,0:T(8,128)(2,1)S(1)}, bf16[64,1024]{1,0:T(8,128)(2,1)S(1)}, u32[]{:S(2)}, u32[]{:S(2)}) collective-permute-start(bf16[64,1024]{1,0:T(8,128)(2,1)S(1)} %final.7), channel_id=1, source_target_pairs={{0,1},{1,0},{2,3},{3,2},{4,5},{5,4},{6,7},{7,6},{8,9},{9,8},{10,11... | collective-permute-start | bytes 393224 | tf_op jit(solution)/shard_map/ppermute | solution.py:165
  72.5 22.7 %collective-permute-start.11 = (bf16[64,1024]{1,0:T(8,128)(2,1)S(1)}, bf16[64,1024]{1,0:T(8,128)(2,1)S(1)}, u32[]{:S(2)}, u32[]{:S(2)}) collective-permute-start(bf16[64,1024]{1,0:T(8,128)(2,1)S(1)} %final.4), channel_id=1, source_target_pairs={{0,1},{1,0},{2,3},{3,2},{4,5},{5,4},{6,7},{7,6},{8,9},{9,8},{10,11... | collective-permute-start | bytes 393224 | tf_op jit(solution)/shard_map/ppermute | solution.py:165
  74.7 13.7 %collective-permute-start.15 = (bf16[64,1024]{1,0:T(8,128)(2,1)S(1)}, bf16[64,1024]{1,0:T(8,128)(2,1)S(1)}, u32[]{:S(2)}, u32[]{:S(2)}) collective-permute-start(bf16[64,1024]{1,0:T(8,128)(2,1)S(1)} %final.5), channel_id=1, source_target_pairs={{0,1},{1,0},{2,3},{3,2},{4,5},{5,4},{6,7},{7,6},{8,9},{9,8},{10,11... | collective-permute-start | bytes 393224 | tf_op jit(solution)/shard_map/ppermute | solution.py:165
  77.2 7.0 %collective-permute-start.18 = (bf16[64,1024]{1,0:T(8,128)(2,1)S(1)}, bf16[64,1024]{1,0:T(8,128)(2,1)S(1)}, u32[]{:S(2)}, u32[]{:S(2)}) collective-permute-start(bf16[64,1024]{1,0:T(8,128)(2,1)S(1)} %final.6), channel_id=1, source_target_pairs={{0,1},{1,0},{2,3},{3,2},{4,5},{5,4},{6,7},{7,6},{8,9},{9,8},{10,11... | collective-permute-start | bytes 393224 | tf_op jit(solution)/shard_map/ppermute | solution.py:165
  81.3 18.0 %collective-permute-start.22 = (bf16[64,2048]{1,0:T(8,128)(2,1)S(1)}, bf16[64,2048]{1,0:T(8,128)(2,1)S(1)}, u32[]{:S(2)}, u32[]{:S(2)}) collective-permute-start(bf16[64,2048]{1,0:T(8,128)(2,1)S(1)} %get-tuple-element.35), channel_id=1, source_target_pairs={{0,2},{2,0},{1,3},{3,1},{4,6},{6,4},{5,7},{7,5},{8,10},{10,8},{9,1... | collective-permute-start | bytes 786440 | tf_op jit(solution)/shard_map/ppermute | solution.py:166
  88.2 12.9 %collective-permute-start.19 = (bf16[64,2048]{1,0:T(8,128)(2,1)S(1)}, bf16[64,2048]{1,0:T(8,128)(2,1)S(1)}, u32[]{:S(2)}, u32[]{:S(2)}) collective-permute-start(bf16[64,2048]{1,0:T(8,128)(2,1)S(1)} %get-tuple-element.37), channel_id=1, source_target_pairs={{0,2},{2,0},{1,3},{3,1},{4,6},{6,4},{5,7},{7,5},{8,10},{10,8},{9,1... | collective-permute-start | bytes 786440 | tf_op jit(solution)/shard_map/ppermute | solution.py:166
  92.3 10.2 %collective-permute-start.16 = (bf16[64,2048]{1,0:T(8,128)(2,1)S(1)}, bf16[64,2048]{1,0:T(8,128)(2,1)S(1)}, u32[]{:S(2)}, u32[]{:S(2)}) collective-permute-start(bf16[64,2048]{1,0:T(8,128)(2,1)S(1)} %get-tuple-element.39), channel_id=1, source_target_pairs={{0,2},{2,0},{1,3},{3,1},{4,6},{6,4},{5,7},{7,5},{8,10},{10,8},{9,1... | collective-permute-start | bytes 786440 | tf_op jit(solution)/shard_map/ppermute | solution.py:166
  99.1 8.6 %collective-permute-start.13 = (bf16[64,2048]{1,0:T(8,128)(2,1)S(1)}, bf16[64,2048]{1,0:T(8,128)(2,1)S(1)}, u32[]{:S(2)}, u32[]{:S(2)}) collective-permute-start(bf16[64,2048]{1,0:T(8,128)(2,1)S(1)} %get-tuple-element.41), channel_id=1, source_target_pairs={{0,2},{2,0},{1,3},{3,1},{4,6},{6,4},{5,7},{7,5},{8,10},{10,8},{9,1... | collective-permute-start | bytes 786440 | tf_op jit(solution)/shard_map/ppermute | solution.py:166
  99.4 10.5 %collective-permute-start.23 = (bf16[64,2048]{1,0:T(8,128)(2,1)S(1)}, bf16[64,2048]{1,0:T(8,128)(2,1)S(1)}, u32[]{:S(2)}, u32[]{:S(2)}) collective-permute-start(bf16[64,2048]{1,0:T(8,128)(2,1)S(1)} %add_convert_fusion), channel_id=1, source_target_pairs={{0,1},{1,0},{2,3},{3,2},{4,5},{5,4},{6,7},{7,6},{8,9},{9,8},{10,11... | collective-permute-start | bytes 786440 | tf_op jit(solution)/shard_map/ppermute | solution.py:165
  101.1 8.7 %collective-permute-start.20 = (bf16[64,2048]{1,0:T(8,128)(2,1)S(1)}, bf16[64,2048]{1,0:T(8,128)(2,1)S(1)}, u32[]{:S(2)}, u32[]{:S(2)}) collective-permute-start(bf16[64,2048]{1,0:T(8,128)(2,1)S(1)} %add_convert_fusion.1), channel_id=1, source_target_pairs={{0,1},{1,0},{2,3},{3,2},{4,5},{5,4},{6,7},{7,6},{8,9},{9,8},{10,11... | collective-permute-start | bytes 786440 | tf_op jit(solution)/shard_map/ppermute | solution.py:165
  102.5 7.7 %collective-permute-start.17 = (bf16[64,2048]{1,0:T(8,128)(2,1)S(1)}, bf16[64,2048]{1,0:T(8,128)(2,1)S(1)}, u32[]{:S(2)}, u32[]{:S(2)}) collective-permute-start(bf16[64,2048]{1,0:T(8,128)(2,1)S(1)} %add_convert_fusion.2), channel_id=1, source_target_pairs={{0,1},{1,0},{2,3},{3,2},{4,5},{5,4},{6,7},{7,6},{8,9},{9,8},{10,11... | collective-permute-start | bytes 786440 | tf_op jit(solution)/shard_map/ppermute | solution.py:165
  107.8 3.2 %collective-permute-start.14 = (bf16[64,2048]{1,0:T(8,128)(2,1)S(1)}, bf16[64,2048]{1,0:T(8,128)(2,1)S(1)}, u32[]{:S(2)}, u32[]{:S(2)}) collective-permute-start(bf16[64,2048]{1,0:T(8,128)(2,1)S(1)} %add_convert_fusion.3), channel_id=1, source_target_pairs={{0,1},{1,0},{2,3},{3,2},{4,5},{5,4},{6,7},{7,6},{8,9},{9,8},{10,11... | collective-permute-start | bytes 786440 | tf_op jit(solution)/shard_map/ppermute | solution.py:165
  (9 other events, 181.1 us)

commit v2 on v1

v2 whole, which is shorter than its diff:
```python
import math

import jax
import jax.numpy as jnp
from jax import lax
from jax.experimental import pallas as pl
from jax.experimental.pallas import tpu as pltpu
from jax.sharding import Mesh, PartitionSpec as P

HD = 128
GROUP = 8
STEPS = 4
SLOTS = 64
TOK = 16
PACK = TOK * GROUP
SCALE = math.log2(math.e) / math.sqrt(HD)
LOW = -1e30
MIB = 1024 * 1024

E_PAIRS = [(i, i ^ 1) for i in range(8)]
O_PAIRS = [(i, (i + 1) % 8 if i % 2 else (i - 1) % 8) for i in range(8)]


def dot_t(a, b):
    return lax.dot_general(a, b, (((1,), (1,)), ((), ())), preferred_element_type=jnp.float32)


def dot(a, b):
    return jnp.dot(a, b, preferred_element_type=jnp.float32)


def with_ones(v):
    return jnp.concatenate([v, jnp.ones_like(v)], axis=1)


def wide(a, count):
    return jnp.concatenate([a] * count, axis=1) if count > 1 else a


def row_max(s):
    top = s[:, :HD]
    for j in range(HD, s.shape[1], HD):
        top = jnp.maximum(top, s[:, j : j + HD])
    return jnp.max(top, axis=1, keepdims=True)


def join_body(k_ref, v_ref, out_ref, sem):
    copies = [
        pltpu.make_async_copy(k_ref, out_ref.at[:, :HD], sem.at[0]),
        pltpu.make_async_copy(v_ref, out_ref.at[:, HD:], sem.at[1]),
    ]
    for copy in copies:
        copy.start()
    for copy in copies:
        copy.wait()


def join(k, v):
    return pl.pallas_call(
        join_body,
        in_specs=[pl.BlockSpec(memory_space=pltpu.HBM)] * 2,
        out_specs=pl.BlockSpec(memory_space=pltpu.VMEM),
        out_shape=jax.ShapeDtypeStruct((k.shape[0], 2 * HD), k.dtype),
        scratch_shapes=[pltpu.SemaphoreType.DMA((2,))],
        compiler_params=pltpu.CompilerParams(vmem_limit_bytes=60 * MIB),
        name="join",
    )(k, v)


def suffix_body(q_ref, nk_ref, nv_ref, sk_all, sv_all, len_ref, qp_ref, m_ref, acc_ref, sk_held, sv_held, sem):
    packs = q_ref.shape[0] // TOK
    base = pl.program_id(0) * packs
    per = TOK // STEPS
    keys = per * SLOTS
    now = pl.program_id(0)
    block = packs * keys

    def fetch(i):
        rows = pl.ds(pl.multiple_of(i * block, block), block)
        return [
            pltpu.make_async_copy(sk_all.at[rows, :], sk_held.at[i], sem.at[0, i]),
            pltpu.make_async_copy(sv_all.at[rows, :], sv_held.at[i], sem.at[1, i]),
        ]

    @pl.when(now == 0)
    def _():
        for i in range(sk_held.shape[0]):
            for copy in fetch(i):
                copy.start()

    for copy in fetch(now):
        copy.wait()
    sk_ref, sv_ref = sk_held.at[now], sv_held.at[now]
    row = lax.broadcasted_iota(jnp.int32, (PACK, keys), 0)
    col = lax.broadcasted_iota(jnp.int32, (PACK, keys), 1)
    owner = (row >> 2) & 3
    same = owner == (col >> 6)
    slot = col & (SLOTS - 1)
    row_n = lax.broadcasted_iota(jnp.int32, (PACK, TOK), 0)
    col_n = lax.broadcasted_iota(jnp.int32, (PACK, TOK), 1)
    same_n = (((row_n >> 2) & 3) == (col_n >> 2)) & ((col_n & 3) <= (row_n & 3))

    def scores(g):
        block = q_ref[g * TOK : (g + 1) * TOK, :]
        q = jnp.concatenate([block[:, h * HD : (h + 1) * HD] for h in range(GROUP)], axis=0)
        qp_ref[g * PACK : (g + 1) * PACK, :] = q
        return dot_t(q, sk_ref[g * keys : (g + 1) * keys, :]), dot_t(q, nk_ref[g * TOK : (g + 1) * TOK, :])

    ahead = scores(0)
    for g in range(packs):
        s, s_n = ahead
        if g + 1 < packs:
            ahead = scores(g + 1)
        rows = pl.ds(g * PACK, PACK)
        length = jnp.full((PACK, keys), len_ref[(base + g) * per], jnp.int32)
        for j in range(1, per):
            length = jnp.where(owner == j, len_ref[(base + g) * per + j], length)
        s = jnp.where(same & (slot < length), s * SCALE, LOW)
        s_n = jnp.where(same_n, s_n * SCALE, LOW)
        m = jnp.maximum(row_max(s), jnp.max(s_n, axis=1, keepdims=True))
        p = jnp.exp2(s - m).astype(jnp.bfloat16)
        p_n = jnp.exp2(s_n - m).astype(jnp.bfloat16)
        new_v = nv_ref[g * TOK : (g + 1) * TOK, :]
        m_ref[rows, :] = jnp.broadcast_to(m, (PACK, HD))
        acc_ref[rows, :] = dot(p, with_ones(sv_ref[g * keys : (g + 1) * keys, :])) + dot(p_n, with_ones(new_v))


def suffix(q, sk, sv, nk, nv, lengths):
    rows = q.shape[0] * GROUP
    grid = 4
    part = lambda a: pl.BlockSpec((a.shape[0] // grid, a.shape[1]), lambda i: (i, 0))
    outs = [
        jax.ShapeDtypeStruct((rows, HD), jnp.bfloat16),
        jax.ShapeDtypeStruct((rows, HD), jnp.float32),
        jax.ShapeDtypeStruct((rows, 2 * HD), jnp.float32),
    ]
    return pl.pallas_call(
        suffix_body,
        grid=(grid,),
        in_specs=[part(a) for a in (q, nk, nv)]
        + [pl.BlockSpec(memory_space=pltpu.HBM)] * 2
        + [pl.BlockSpec(memory_space=pltpu.SMEM)],
        out_specs=[part(o) for o in outs],
        out_shape=outs,
        scratch_shapes=[pltpu.VMEM((grid, sk.shape[0] // grid, HD), jnp.bfloat16)] * 2 + [pltpu.SemaphoreType.DMA((2, grid))],
        cost_estimate=pl.CostEstimate(flops=300_000_000, bytes_accessed=6_000_000, transcendentals=600_000),
        compiler_params=pltpu.CompilerParams(vmem_limit_bytes=12 * MIB),
        name="suffix",
    )(q, nk, nv, sk, sv, lengths)


def attend(q, m, acc, kvs, emit, tile=256):
    tiles = q.shape[0] // tile
    scores = lambda i: [dot_t(q[i * tile : (i + 1) * tile, :], kv[:, :HD]) for kv in kvs]
    ahead = scores(0)
    for i in range(tiles):
        parts = ahead
        if i + 1 < tiles:
            ahead = scores(i + 1)
        rows = slice(i * tile, (i + 1) * tile)
        top = row_max(parts[0])
        for s in parts[1:]:
            top = jnp.maximum(top, row_max(s))
        old = m[rows, :]
        new = jnp.maximum(old, top * SCALE)
        out = acc[rows, :] * wide(jnp.exp2(old - new), 2)
        for s, kv in zip(parts, kvs):
            p = jnp.exp2(s * SCALE - wide(new, s.shape[1] // HD)).astype(jnp.bfloat16)
            out = out + dot(p, with_ones(kv[:, HD:]))
        emit(i, rows, new, out)


def prefix_body(n, *refs):
    m_out, acc_out = refs[3 + n :]

    def emit(_, rows, new, out):
        m_out[rows, :] = new
        acc_out[rows, :] = out

    attend(refs[0], refs[1], refs[2], refs[3 : 3 + n], emit)


def prefix(q, m, acc, kvs, tile=1024):
    rows = q.shape[0]
    part = lambda a: pl.BlockSpec((tile, a.shape[1]), lambda i: (i, 0))
    whole = lambda a: pl.BlockSpec(a.shape, lambda i: (0, 0))
    keys = sum(kv.shape[0] for kv in kvs)
    return pl.pallas_call(
        lambda *refs: prefix_body(len(kvs), *refs),
        grid=(rows // tile,),
        in_specs=[part(q), part(m), part(acc)] + [whole(kv) for kv in kvs],
        out_specs=[part(m), part(acc)],
        out_shape=[jax.ShapeDtypeStruct(m.shape, m.dtype), jax.ShapeDtypeStruct(acc.shape, acc.dtype)],
        cost_estimate=pl.CostEstimate(flops=rows * keys * HD * 8, bytes_accessed=7_000_000, transcendentals=rows * keys),
        compiler_params=pltpu.CompilerParams(vmem_limit_bytes=16 * MIB),
        name="prefix",
    )(q, m, acc, *kvs)


def final_body(n, *refs):
    weight_ref = refs[3 + n]
    mine_ref, other_ref, heads_ref = refs[4 + n :]

    def emit(i, rows, _, out):
        heads = (out[:, :HD] / out[:, HD:]).astype(jnp.bfloat16)
        packs = heads.shape[0] // PACK
        for g in range(packs):
            for h in range(GROUP):
                first = g * PACK + h * TOK
                to = (i * packs + g) * TOK
                heads_ref[to : to + TOK, h * HD : (h + 1) * HD] = heads[first : first + TOK, :]

    attend(refs[0], refs[1], refs[2], refs[3 : 3 + n], emit)
    heads = heads_ref[...]
    requests, steps, half = mine_ref.shape
    core = lax.axis_index("core")
    width = 512
    for ref, side in ((other_ref, 1 - core), (mine_ref, core)):
        for j in range(0, half, width):
            columns = pl.ds(pl.multiple_of(side * half + j, width), width)
            terms = dot(heads, weight_ref[:, columns])
            ref[:, :, j : j + width] = terms.reshape(requests, steps, width).astype(ref.dtype)


def final(q, m, acc, kvs, weight):
    rows = q.shape[0]
    tokens, half = rows // GROUP, weight.shape[1] // 2
    keys = sum(kv.shape[0] for kv in kvs)
    whole = lambda a: pl.BlockSpec(a.shape, lambda i: (0,) * len(a.shape))
    shape = (tokens // STEPS, STEPS, half)
    outs = [jax.ShapeDtypeStruct(shape, jnp.float32), jax.ShapeDtypeStruct(shape, jnp.bfloat16)]
    return pl.pallas_call(
        lambda *refs: final_body(len(kvs), *refs),
        grid=(1,),
        in_specs=[whole(a) for a in (q, m, acc, *kvs)] + [pl.BlockSpec(memory_space=pltpu.VMEM)],
        out_specs=[whole(o) for o in outs],
        out_shape=outs,
        scratch_shapes=[pltpu.VMEM((tokens, GROUP * HD), jnp.bfloat16)],
        cost_estimate=pl.CostEstimate(
            flops=rows * keys * HD * 8 + 8 * tokens * weight.size, bytes_accessed=12_000_000, transcendentals=rows * keys
        ),
        compiler_params=pltpu.CompilerParams(vmem_limit_bytes=24 * MIB),
        name="final",
    )(q, m, acc, *kvs, weight)


def place_body(n, lows, *refs):
    out_ref, sem = refs[-2:]
    half = refs[0].shape[2]
    core = lax.axis_index("core")
    copies = []
    for i in range(n):
        side = core if i % 2 == 0 else 1 - core
        rows = pl.ds(lows[i // 2], refs[i].shape[0])
        columns = pl.ds(pl.multiple_of(side * half, half), half)
        copies.append(pltpu.make_async_copy(refs[i], out_ref.at[rows, :, columns], sem.at[i]))
    for copy in copies:
        copy.start()
    for copy in copies:
        copy.wait()


def place(pieces, lows, shape, out=None):
    n = len(pieces)
    return pl.pallas_call(
        lambda *refs: place_body(n, lows, *refs),
        in_specs=[pl.BlockSpec(memory_space=pltpu.VMEM)] * n + ([] if out is None else [pl.BlockSpec(memory_space=pl.ANY)]),
        out_specs=pl.BlockSpec(memory_space=pl.ANY),
        out_shape=jax.ShapeDtypeStruct(shape, pieces[0].dtype),
        scratch_shapes=[pltpu.SemaphoreType.DMA((n,))],
        input_output_aliases={} if out is None else {n: 0},
        compiler_params=pltpu.CompilerParams(vmem_limit_bytes=2 * MIB),
        name="place",
    )(*pieces, *([] if out is None else [out]))


def local(queries, prefix_keys, prefix_values, suffix_keys, suffix_values, new_keys, new_values, suffix_lengths, out_weight):
    requests = queries.shape[0]
    even = lambda a: lax.ppermute(a, "z", E_PAIRS)
    odd = lambda a: lax.ppermute(a, "z", O_PAIRS)
    x1 = lambda a: lax.ppermute(a, "x", [(i, i ^ 1) for i in range(4)])
    x3 = lambda a: lax.ppermute(a, "x", [(i, i ^ 3) for i in range(4)])
    y = lambda a: lax.ppermute(a, "ylo", [(0, 1), (1, 0)])
    swap_core = lambda a: lax.ppermute(a, "core", [(0, 1), (1, 0)])
    swap_y = lambda a: lax.ppermute(a, "yhi", [(0, 1), (1, 0)])

    flat = lambda a: a.reshape(-1, a.shape[-1])
    args = [flat(a) for a in (queries, suffix_keys, suffix_values, new_keys, new_values)]

    kv = join(prefix_keys, prefix_values)
    pair = jnp.concatenate([kv, even(kv)], axis=0)
    r2 = odd(pair)
    r3 = even(r2)
    r4 = odd(r3)
    line = jnp.concatenate([pair, r2, r3, r4], axis=0)
    b_x1, b_x3, b_y = x1(line), x3(line), y(line)
    b_yx1, b_yx3 = x1(b_y), x3(b_y)
    b_far = x1(b_x3)
    b_yfar = x3(b_yx1)

    q, m, acc = suffix(*args, suffix_lengths)
    m, acc = prefix(q, m, acc, [line])
    m, acc = prefix(q, m, acc, [b_x1, b_x3, b_y])
    m, acc = prefix(q, m, acc, [b_yx1, b_yx3])
    mine, other = final(q, m, acc, [b_far, b_yfar], out_weight)
    terms = (mine + swap_core(other).astype(jnp.float32)).astype(jnp.bfloat16)
    sizes = (16, 16, 16, 8, 8)
    lows = [sum(sizes[:i]) for i in range(len(sizes))]
    pieces = [terms[low : low + size] for low, size in zip(lows, sizes)]
    moved = [swap_y(piece) for piece in pieces]
    halves = []
    for piece, got in zip(pieces, moved):
        total = piece + got
        halves += [total, swap_core(total)]
    shape = (requests, STEPS, out_weight.shape[1])
    early = 2 * (len(sizes) - 1)
    out = place(halves[:early], lows[:-1], shape)
    return place(halves[early:], lows[-1:], shape, out)


def solution(mesh):
    fine = Mesh(mesh.devices.reshape(2, 4, 8, 2, 2), ("ylo", "x", "z", "yhi", "core"))
    req, tp = ("ylo", "x", "z"), ("yhi", "core")
    in_specs = (
        P(req, None, tp),
        P(req, tp),
        P(req, tp),
        P(req, None, tp),
        P(req, None, tp),
        P(req, None, tp),
        P(req, None, tp),
        P(req),
        P(tp, None),
    )
    return jax.shard_map(local, mesh=fine, in_specs=in_specs, out_specs=P(req, None, None), check_vma=False)
```

time: 115 us -> 95.5 us (0.83)
  matrix products: 15.5 us -> 0 us
  Pallas kernels: 36.4 us -> 21.3 us
  waiting for transfers between devices: 14.3 us -> 25.6 us
  starting transfers between devices: 37.4 us -> 39.9 us
  local copies, waits for them, and re-layouts: 7.26 us -> 5.97 us
    dot_general x8 -> x0, matrix products: 15.5 us -> none  [dot(): return jnp.dot(a, b, preferred_element_type=jnp.float32)]
    pallas_call x3, Pallas kernels: 23.9 us -> 9.03 us  [prefix(): pl.pallas_call(lambda *refs: prefix_body(len(kvs), *refs), grid=(rows //...]
    ppermute x4 -> x5, waiting for transfers between devices: 4.32 us -> 13.8 us  [local(): swap_y = lambda a: lax.ppermute(a, 'yhi', [(0, 1), (1, 0)])]
    dynamic_slice x1 -> x0, local copies, waits for them, and re-layouts: 4.89 us -> none  [local(): lax.dynamic_slice(out_weight, (0, (1 - core) * half), (out_weight.shape[0...]
    ppermute x9 -> x6, starting transfers between devices: 16.3 us -> 11.6 us  [local(): swap_core = lambda a: lax.ppermute(a, 'core', [(0, 1), (1, 0)])]
    unnamed x22 -> x18, local copies, waits for them, and re-layouts: 0.06 us -> 4.37 us
    ppermute x4 -> x5, starting transfers between devices: 6.29 us -> 9.03 us  [local(): swap_y = lambda a: lax.ppermute(a, 'yhi', [(0, 1), (1, 0)])]
    concatenate x5 -> x0, other arithmetic: 2.68 us -> none  [the longest x1 2.53 us: local(): return jnp.concatenate(results, axis=0)]
  transfers between devices with their start and end apart: 24 -> 22, of which waited for: 7 -> 10; matrix products, arithmetic and copies ran while one was open for 15% -> 3% of each run, Pallas kernels for 32% -> 15%
where the time goes in v2:
time: 95.5 us; the launch traced here: 95.1 us
  starting transfers between devices  39.9 us (42%)
  waiting for transfers between devices  25.6 us (27%)
  Pallas kernels  21.3 us (22%)
  local copies, waits for them, and re-layouts  5.97 us (6%)
  other arithmetic  1.95 us (2%)
    ppermute x5, waiting for transfers between devices, local(): swap_y = lambda a: lax.ppermute(a, 'yhi', [(0, 1), (1, 0)])  13.8 us
    ppermute x6, starting transfers between devices, local(): swap_core = lambda a: lax.ppermute(a, 'core', [(0, 1), (1, 0)])  11.6 us
    pallas_call x3, Pallas kernels, prefix(): pl.pallas_call(lambda *refs: prefix_body(len(kvs), *refs), grid=(rows //...  9.03 us
    ppermute x5, starting transfers between devices, local(): swap_y = lambda a: lax.ppermute(a, 'yhi', [(0, 1), (1, 0)])  9.03 us
    ppermute x2, starting transfers between devices, local(): odd = lambda a: lax.ppermute(a, 'z', O_PAIRS)  8.07 us
    ppermute x3, starting transfers between devices, local(): x3 = lambda a: lax.ppermute(a, 'x', [(i, i ^ 3) for i in range(4)])  5.84 us
    pallas_call x1, Pallas kernels, final(): pl.pallas_call(lambda *refs: final_body(len(kvs), *refs), grid=(1,), in_s...  5.04 us
    unnamed x18, local copies, waits for them, and re-layouts  4.37 us
  transfers between devices with their start and end apart: 22, of which 10 were waited for; matrix products, arithmetic and copies ran while one was open for 3% of the time, Pallas kernels for 15%

profile of v2, /device:TPU:1, one launch (start us, length us, event | category | flops | bytes accessed | tf_op | source)
XLA Modules:
  0.0 95.1 jit_solution(12020328535133374022)
XLA Ops:
  0.0 1.5 %join.1 = bf16[64,256]{1,0:T(8,128)(2,1)} custom-call(bf16[64,128]{1,0:T(8,128)(2,1)} %k_ref.1, bf16[64,128]{1,0:T(8,128)(2,1)} %v_ref.1), custom_call_target="tpu_custom_call" | custom-call | tf_op jit(solution)/shard_map/join/pallas_call | solution.py:59
  1.5 2.6 %collective-permute-start = (bf16[64,256]{1,0:T(8,128)(2,1)}, bf16[64,256]{1,0:T(8,128)(2,1)S(1)}, u32[]{:S(2)}, u32[]{:S(2)}) collective-permute-start(bf16[64,256]{1,0:T(8,128)(2,1)} %join.1), channel_id=1, source_target_pairs={{0,4},{4,0},{8,12},{12,8},{16,20},{20,16},{24,28},{28,24},{1,5},{5... | collective-permute-start | bytes 98312 | tf_op jit(solution)/shard_map/ppermute | solution.py:279
  6.3 5.4 %collective-permute-start.1 = (bf16[128,256]{1,0:T(8,128)(2,1)S(1)}, bf16[128,256]{1,0:T(8,128)(2,1)S(1)}, u32[]{:S(2)}, u32[]{:S(2)}) collective-permute-start(bf16[128,256]{1,0:T(8,128)(2,1)S(1)} %pad_maximum_fusion), channel_id=1, source_target_pairs={{0,28},{4,8},{8,4},{12,16},{16,12},{20,24},{24,20},{28,0},{1,29},{... | collective-permute-start | bytes 196616 | tf_op jit(solution)/shard_map/ppermute | solution.py:280
  11.7 1.6 %collective-permute-done.1 = bf16[128,256]{1,0:T(8,128)(2,1)S(1)} collective-permute-done((bf16[128,256]{1,0:T(8,128)(2,1)S(1)}, bf16[128,256]{1,0:T(8,128)(2,1)S(1)}, u32[]{:S(2)}, u32[]{:S(2)}) %collective-permute-start.1) | collective-permute-done | bytes 65568 | tf_op jit(solution)/shard_map/ppermute | solution.py:280
  13.4 3.1 %collective-permute-done.2 = bf16[128,256]{1,0:T(8,128)(2,1)S(1)} collective-permute-done((bf16[128,256]{1,0:T(8,128)(2,1)S(1)}, bf16[128,256]{1,0:T(8,128)(2,1)S(1)}, u32[]{:S(2)}, u32[]{:S(2)}) %collective-permute-start.2) | collective-permute-done | bytes 65568 | tf_op jit(solution)/shard_map/ppermute | solution.py:279
  16.5 2.7 %collective-permute-start.3 = (bf16[128,256]{1,0:T(8,128)(2,1)S(1)}, bf16[128,256]{1,0:T(8,128)(2,1)S(1)}, u32[]{:S(2)}, u32[]{:S(2)}) collective-permute-start(bf16[128,256]{1,0:T(8,128)(2,1)S(1)} %collective-permute-done.2), channel_id=1, source_target_pairs={{0,28},{4,8},{8,4},{12,16},{16,12},{20,24},{24,20},{28,0},{1,29},{... | collective-permute-start | bytes 196616 | tf_op jit(solution)/shard_map/ppermute | solution.py:280
  19.1 1.6 %collective-permute-done.3 = bf16[128,256]{1,0:T(8,128)(2,1)S(1)} collective-permute-done((bf16[128,256]{1,0:T(8,128)(2,1)S(1)}, bf16[128,256]{1,0:T(8,128)(2,1)S(1)}, u32[]{:S(2)}, u32[]{:S(2)}) %collective-permute-start.3) | collective-permute-done | bytes 65568 | tf_op jit(solution)/shard_map/ppermute | solution.py:280
  22.1 2.5 %collective-permute-start.5 = (bf16[512,256]{1,0:T(8,128)(2,1)S(1)}, bf16[512,256]{1,0:T(8,128)(2,1)S(1)}, u32[]{:S(2)}, u32[]{:S(2)}) collective-permute-start(bf16[512,256]{1,0:T(8,128)(2,1)S(1)} %constant_dynamic-update-slice_fusion.refs_3_), channel_id=1, source_target_pairs={{0,96},{32,64},{64,32},{96,0},{1,97},{33,65},{65,33},{97,1},{2,98}... | collective-permute-start | bytes 786440 | tf_op jit(solution)/shard_map/ppermute | solution.py:282
  24.6 1.4 %collective-permute-done.6.refs_5_ = bf16[512,256]{1,0:T(8,128)(2,1)S(1)} collective-permute-done((bf16[512,256]{1,0:T(8,128)(2,1)S(1)}, bf16[512,256]{1,0:T(8,128)(2,1)S(1)}, u32[]{:S(2)}, u32[]{:S(2)}) %collective-permute-start.6) | collective-permute-done | bytes 262176 | tf_op jit(solution)/shard_map/ppermute | solution.py:283
  32.2 3.8 %suffix.1 = (bf16[2048,128]{1,0:T(8,128)(2,1)S(1)}, f32[2048,128]{1,0:T(8,128)S(1)}, f32[2048,256]{1,0:T(8,128)S(1)}) custom-call(bf16[256,1024]{1,0:T(8,128)(2,1)S(1)} %reshape.15.q_ref, bf16[256,128]{1,0:T(8,128)(2,1)S(1)} %bitcast.6, bf16[256,128]{1,0:T(8,128)(2,1)S(1)} %bitcast.7, bf16[4096,128]{1,0:T(8,128)(2,1)S(1)} %bitcast.4, ...), custom_call_target="tpu_custom_call" | custom-call | flops 300000000 | bytes 6000000 | tf_op jit(solution)/shard_map/suffix/pallas_call | solution.py:137
  36.0 1.9 %prefix.3 = (f32[2048,128]{1,0:T(8,128)S(1)}, f32[2048,256]{1,0:T(8,128)S(1)}) custom-call(bf16[2048,128]{1,0:T(8,128)(2,1)S(1)} %get-tuple-element.16.refs_0_, f32[2048,128]{1,0:T(8,128)S(1)} %get-tuple-element.17.refs_1_, f32[2048,256]{1,0:T(8,128)S(1)} %get-tuple-element.18.refs_2_, bf16[512,256]{1,0:T(8,128)(2,1)S(1)} %constant_dynamic-update-slice_fusion.refs_3_), custom_call_target="tpu_custom_call" | custom-call | flops 1073741824 | bytes 7000000 | tf_op jit(solution)/shard_map/prefix/pallas_call | solution.py:188
  38.0 2.6 %collective-permute-start.8 = (bf16[512,256]{1,0:T(8,128)(2,1)S(1)}, bf16[512,256]{1,0:T(8,128)(2,1)S(1)}, u32[]{:S(2)}, u32[]{:S(2)}) collective-permute-start(bf16[512,256]{1,0:T(8,128)(2,1)S(1)} %collective-permute-done.6.refs_5_), channel_id=1, source_target_pairs={{0,96},{32,64},{64,32},{96,0},{1,97},{33,65},{65,33},{97,1},{2,98}... | collective-permute-start | bytes 786440 | tf_op jit(solution)/shard_map/ppermute | solution.py:282
  41.3 4.2 %prefix.4 = (f32[2048,128]{1,0:T(8,128)S(1)}, f32[2048,256]{1,0:T(8,128)S(1)}) custom-call(bf16[2048,128]{1,0:T(8,128)(2,1)S(1)} %get-tuple-element.16.refs_0_, f32[2048,128]{1,0:T(8,128)S(1)} %get-tuple-element.19.refs_1_, f32[2048,256]{1,0:T(8,128)S(1)} %get-tuple-element.20.refs_2_, bf16[512,256]{1,0:T(8,128)(2,1)S(1)} %collective-permute-done.4.refs_3_, ...), custom_call_target="tpu_custom_call" | custom-call | flops 3221225472 | bytes 7000000 | tf_op jit(solution)/shard_map/prefix/pallas_call | solution.py:188
  45.5 2.9 %prefix.5 = (f32[2048,128]{1,0:T(8,128)S(1)}, f32[2048,256]{1,0:T(8,128)S(1)}) custom-call(bf16[2048,128]{1,0:T(8,128)(2,1)S(1)} %get-tuple-element.16.refs_0_, f32[2048,128]{1,0:T(8,128)S(1)} %get-tuple-element.21.refs_1_, f32[2048,256]{1,0:T(8,128)S(1)} %get-tuple-element.22.refs_2_, bf16[512,256]{1,0:T(8,128)(2,1)S(1)} %collective-permute-done.7.refs_3_, ...), custom_call_target="tpu_custom_call" | custom-call | flops 2147483648 | bytes 7000000 | tf_op jit(solution)/shard_map/prefix/pallas_call | solution.py:188
  48.5 5.0 %final.1 = (f32[64,4,2048]{2,1,0:T(4,128)S(1)}, bf16[64,4,2048]{2,1,0:T(4,128)(2,1)S(1)}) custom-call(bf16[2048,128]{1,0:T(8,128)(2,1)S(1)} %get-tuple-element.16.refs_0_, f32[2048,128]{1,0:T(8,128)S(1)} %get-tuple-element.23.refs_1_, f32[2048,256]{1,0:T(8,128)S(1)} %get-tuple-element.24.refs_2_, bf16[512,256]{1,0:T(8,128)(2,1)S(1)} %collective-permute-done.9.refs_3_, ...), custom_call_target="tpu_custom_call" | custom-call | flops 10737418240 | bytes 12000000 | tf_op jit(solution)/shard_map/final/pallas_call | solution.py:232
  53.6 7.6 %collective-permute-start.11 = (bf16[64,4,2048]{2,1,0:T(4,128)(2,1)S(1)}, bf16[64,4,2048]{2,1,0:T(4,128)(2,1)S(1)}, u32[]{:S(2)}, u32[]{:S(2)}) collective-permute-start(bf16[64,4,2048]{2,1,0:T(4,128)(2,1)S(1)} %get-tuple-element.26), channel_id=1, source_target_pairs={{0,1},{1,0},{2,3},{3,2},{4,5},{5,4},{6,7},{7,6},{8,9},{9,8},{10,11... | collective-permute-start | bytes 3145736 | tf_op jit(solution)/shard_map/ppermute | solution.py:284
  61.2 2.3 %collective-permute-done.11 = bf16[64,4,2048]{2,1,0:T(4,128)(2,1)S(1)} collective-permute-done((bf16[64,4,2048]{2,1,0:T(4,128)(2,1)S(1)}, bf16[64,4,2048]{2,1,0:T(4,128)(2,1)S(1)}, u32[]{:S(2)}, u32[]{:S(2)}) %collective-permute-start.11) | collective-permute-done | bytes 1048608 | tf_op jit(solution)/shard_map/ppermute | solution.py:284
  64.5 3.0 %collective-permute-start.14 = (bf16[16,4,2048]{2,1,0:T(4,128)(2,1)S(1)}, bf16[16,4,2048]{2,1,0:T(4,128)(2,1)S(1)}, u32[]{:S(2)}, u32[]{:S(2)}) collective-permute-start(bf16[16,4,2048]{2,1,0:T(4,128)(2,1)S(1)} %get-tuple-element.36), channel_id=1, source_target_pairs={{0,2},{2,0},{1,3},{3,1},{4,6},{6,4},{5,7},{7,5},{8,10},{10,8},{9,1... | collective-permute-start | bytes 786440 | tf_op jit(solution)/shard_map/ppermute | solution.py:285
  67.6 2.9 %collective-permute-start.18 = (bf16[16,4,2048]{2,1,0:T(4,128)(2,1)S(1)}, bf16[16,4,2048]{2,1,0:T(4,128)(2,1)S(1)}, u32[]{:S(2)}, u32[]{:S(2)}) collective-permute-start(bf16[16,4,2048]{2,1,0:T(4,128)(2,1)S(1)} %get-tuple-element.34), channel_id=1, source_target_pairs={{0,2},{2,0},{1,3},{3,1},{4,6},{6,4},{5,7},{7,5},{8,10},{10,8},{9,1... | collective-permute-start | bytes 786440 | tf_op jit(solution)/shard_map/ppermute | solution.py:285
  70.8 2.9 %collective-permute-start.20 = (bf16[8,4,2048]{2,1,0:T(4,128)(2,1)S(1)}, bf16[8,4,2048]{2,1,0:T(4,128)(2,1)S(1)}, u32[]{:S(2)}, u32[]{:S(2)}) collective-permute-start(bf16[8,4,2048]{2,1,0:T(4,128)(2,1)S(1)} %get-tuple-element.29), channel_id=1, source_target_pairs={{0,2},{2,0},{1,3},{3,1},{4,6},{6,4},{5,7},{7,5},{8,10},{10,8},{9,1... | collective-permute-start | bytes 393224 | tf_op jit(solution)/shard_map/ppermute | solution.py:285
  73.6 5.6 %collective-permute-done.16 = bf16[16,4,2048]{2,1,0:T(4,128)(2,1)S(1)} collective-permute-done((bf16[16,4,2048]{2,1,0:T(4,128)(2,1)S(1)}, bf16[16,4,2048]{2,1,0:T(4,128)(2,1)S(1)}, u32[]{:S(2)}, u32[]{:S(2)}) %collective-permute-start.16) | collective-permute-done | bytes 262176 | tf_op jit(solution)/shard_map/ppermute | solution.py:285
  79.2 5.6 %collective-permute-done.18 = bf16[16,4,2048]{2,1,0:T(4,128)(2,1)S(1)} collective-permute-done((bf16[16,4,2048]{2,1,0:T(4,128)(2,1)S(1)}, bf16[16,4,2048]{2,1,0:T(4,128)(2,1)S(1)}, u32[]{:S(2)}, u32[]{:S(2)}) %collective-permute-start.18) | collective-permute-done | bytes 262176 | tf_op jit(solution)/shard_map/ppermute | solution.py:285
  85.2 2.1 %collective-permute-start.15 = (bf16[16,4,2048]{2,1,0:T(4,128)(2,1)S(1)}, bf16[16,4,2048]{2,1,0:T(4,128)(2,1)S(1)}, u32[]{:S(2)}, u32[]{:S(2)}) collective-permute-start(bf16[16,4,2048]{2,1,0:T(4,128)(2,1)S(1)} %get-tuple-element.32.refs_0_), channel_id=1, source_target_pairs={{0,1},{1,0},{2,3},{3,2},{4,5},{5,4},{6,7},{7,6},{8,9},{9,8},{10,11... | collective-permute-start | bytes 786440 | tf_op jit(solution)/shard_map/ppermute | solution.py:284
  87.8 2.6 %collective-permute-done.20 = bf16[8,4,2048]{2,1,0:T(4,128)(2,1)S(1)} collective-permute-done((bf16[8,4,2048]{2,1,0:T(4,128)(2,1)S(1)}, bf16[8,4,2048]{2,1,0:T(4,128)(2,1)S(1)}, u32[]{:S(2)}, u32[]{:S(2)}) %collective-permute-start.20) | collective-permute-done | bytes 131104 | tf_op jit(solution)/shard_map/ppermute | solution.py:285
  (55 shorter events, 17.3 us)
Async XLA Ops:
  0.0 28.7 %copy-start = (bf16[64,64,128]{2,1,0:T(8,128)(2,1)S(1)}, bf16[64,64,128]{2,1,0:T(8,128)(2,1)}, u32[]{:S(2)}) copy-start(bf16[64,64,128]{2,1,0:T(8,128)(2,1)} %param.12) | copy-start | bytes 3145732
  1.5 4.1 %collective-permute-start = (bf16[64,256]{1,0:T(8,128)(2,1)}, bf16[64,256]{1,0:T(8,128)(2,1)S(1)}, u32[]{:S(2)}, u32[]{:S(2)}) collective-permute-start(bf16[64,256]{1,0:T(8,128)(2,1)} %join.1), channel_id=1, source_target_pairs={{0,4},{4,0},{8,12},{12,8},{16,20},{20,16},{24,28},{28,24},{1,5},{5... | collective-permute-start | bytes 98312 | tf_op jit(solution)/shard_map/ppermute | solution.py:279
  6.3 7.1 %collective-permute-start.1 = (bf16[128,256]{1,0:T(8,128)(2,1)S(1)}, bf16[128,256]{1,0:T(8,128)(2,1)S(1)}, u32[]{:S(2)}, u32[]{:S(2)}) collective-permute-start(bf16[128,256]{1,0:T(8,128)(2,1)S(1)} %pad_maximum_fusion), channel_id=1, source_target_pairs={{0,28},{4,8},{8,4},{12,16},{16,12},{20,24},{24,20},{28,0},{1,29},{... | collective-permute-start | bytes 196616 | tf_op jit(solution)/shard_map/ppermute | solution.py:280
  13.3 3.1 %collective-permute-start.2 = (bf16[128,256]{1,0:T(8,128)(2,1)S(1)}, bf16[128,256]{1,0:T(8,128)(2,1)S(1)}, u32[]{:S(2)}, u32[]{:S(2)}) collective-permute-start(bf16[128,256]{1,0:T(8,128)(2,1)S(1)} %collective-permute-done.1), channel_id=1, source_target_pairs={{0,4},{4,0},{8,12},{12,8},{16,20},{20,16},{24,28},{28,24},{1,5},{5... | collective-permute-start | bytes 196616 | tf_op jit(solution)/shard_map/ppermute | solution.py:279
  16.5 4.3 %collective-permute-start.3 = (bf16[128,256]{1,0:T(8,128)(2,1)S(1)}, bf16[128,256]{1,0:T(8,128)(2,1)S(1)}, u32[]{:S(2)}, u32[]{:S(2)}) collective-permute-start(bf16[128,256]{1,0:T(8,128)(2,1)S(1)} %collective-permute-done.2), channel_id=1, source_target_pairs={{0,28},{4,8},{8,4},{12,16},{16,12},{20,24},{24,20},{28,0},{1,29},{... | collective-permute-start | bytes 196616 | tf_op jit(solution)/shard_map/ppermute | solution.py:280
  20.8 5.2 %collective-permute-start.6 = (bf16[512,256]{1,0:T(8,128)(2,1)S(1)}, bf16[512,256]{1,0:T(8,128)(2,1)S(1)}, u32[]{:S(2)}, u32[]{:S(2)}) collective-permute-start(bf16[512,256]{1,0:T(8,128)(2,1)S(1)} %constant_dynamic-update-slice_fusion.refs_3_), channel_id=1, source_target_pairs={{0,128},{128,0},{1,129},{129,1},{2,130},{130,2},{3,131},{131,3},{4... | collective-permute-start | bytes 786440 | tf_op jit(solution)/shard_map/ppermute | solution.py:283
  22.1 18.4 %collective-permute-start.5 = (bf16[512,256]{1,0:T(8,128)(2,1)S(1)}, bf16[512,256]{1,0:T(8,128)(2,1)S(1)}, u32[]{:S(2)}, u32[]{:S(2)}) collective-permute-start(bf16[512,256]{1,0:T(8,128)(2,1)S(1)} %constant_dynamic-update-slice_fusion.refs_3_), channel_id=1, source_target_pairs={{0,96},{32,64},{64,32},{96,0},{1,97},{33,65},{65,33},{97,1},{2,98}... | collective-permute-start | bytes 786440 | tf_op jit(solution)/shard_map/ppermute | solution.py:282
  26.0 14.5 %collective-permute-start.7 = (bf16[512,256]{1,0:T(8,128)(2,1)S(1)}, bf16[512,256]{1,0:T(8,128)(2,1)S(1)}, u32[]{:S(2)}, u32[]{:S(2)}) collective-permute-start(bf16[512,256]{1,0:T(8,128)(2,1)S(1)} %collective-permute-done.6.refs_5_), channel_id=1, source_target_pairs={{0,32},{32,0},{64,96},{96,64},{1,33},{33,1},{65,97},{97,65},{2,34}... | collective-permute-start | bytes 786440 | tf_op jit(solution)/shard_map/ppermute | solution.py:281
  27.2 14.1 %collective-permute-start.4 = (bf16[512,256]{1,0:T(8,128)(2,1)S(1)}, bf16[512,256]{1,0:T(8,128)(2,1)S(1)}, u32[]{:S(2)}, u32[]{:S(2)}) collective-permute-start(bf16[512,256]{1,0:T(8,128)(2,1)S(1)} %constant_dynamic-update-slice_fusion.refs_3_), channel_id=1, source_target_pairs={{0,32},{32,0},{64,96},{96,64},{1,33},{33,1},{65,97},{97,65},{2,34}... | collective-permute-start | bytes 786440 | tf_op jit(solution)/shard_map/ppermute | solution.py:281
  36.0 12.5 %slice-start = ((s8[8388608]{0:T(1024)(128)(4,1)}), s8[4194304]{0:T(1024)(128)(4,1)S(1)}, s32[]{:S(2)}) async-start(s8[8388608]{0:T(1024)(128)(4,1)} %bitcast.8), calls=%async_computation | async-start | bytes 8388608
  38.0 7.6 %collective-permute-start.8 = (bf16[512,256]{1,0:T(8,128)(2,1)S(1)}, bf16[512,256]{1,0:T(8,128)(2,1)S(1)}, u32[]{:S(2)}, u32[]{:S(2)}) collective-permute-start(bf16[512,256]{1,0:T(8,128)(2,1)S(1)} %collective-permute-done.6.refs_5_), channel_id=1, source_target_pairs={{0,96},{32,64},{64,32},{96,0},{1,97},{33,65},{65,33},{97,1},{2,98}... | collective-permute-start | bytes 786440 | tf_op jit(solution)/shard_map/ppermute | solution.py:282
  40.5 8.0 %collective-permute-start.9 = (bf16[512,256]{1,0:T(8,128)(2,1)S(1)}, bf16[512,256]{1,0:T(8,128)(2,1)S(1)}, u32[]{:S(2)}, u32[]{:S(2)}) collective-permute-start(bf16[512,256]{1,0:T(8,128)(2,1)S(1)} %collective-permute-done.5.refs_4_), channel_id=1, source_target_pairs={{0,32},{32,0},{64,96},{96,64},{1,33},{33,1},{65,97},{97,65},{2,34}... | collective-permute-start | bytes 786440 | tf_op jit(solution)/shard_map/ppermute | solution.py:281
  40.5 8.0 %collective-permute-start.10 = (bf16[512,256]{1,0:T(8,128)(2,1)S(1)}, bf16[512,256]{1,0:T(8,128)(2,1)S(1)}, u32[]{:S(2)}, u32[]{:S(2)}) collective-permute-start(bf16[512,256]{1,0:T(8,128)(2,1)S(1)} %collective-permute-done.7.refs_3_), channel_id=1, source_target_pairs={{0,96},{32,64},{64,32},{96,0},{1,97},{33,65},{65,33},{97,1},{2,98}... | collective-permute-start | bytes 786440 | tf_op jit(solution)/shard_map/ppermute | solution.py:282
  53.6 9.9 %collective-permute-start.11 = (bf16[64,4,2048]{2,1,0:T(4,128)(2,1)S(1)}, bf16[64,4,2048]{2,1,0:T(4,128)(2,1)S(1)}, u32[]{:S(2)}, u32[]{:S(2)}) collective-permute-start(bf16[64,4,2048]{2,1,0:T(4,128)(2,1)S(1)} %get-tuple-element.26), channel_id=1, source_target_pairs={{0,1},{1,0},{2,3},{3,2},{4,5},{5,4},{6,7},{7,6},{8,9},{9,8},{10,11... | collective-permute-start | bytes 3145736 | tf_op jit(solution)/shard_map/ppermute | solution.py:284
  64.5 9.1 %collective-permute-start.14 = (bf16[16,4,2048]{2,1,0:T(4,128)(2,1)S(1)}, bf16[16,4,2048]{2,1,0:T(4,128)(2,1)S(1)}, u32[]{:S(2)}, u32[]{:S(2)}) collective-permute-start(bf16[16,4,2048]{2,1,0:T(4,128)(2,1)S(1)} %get-tuple-element.36), channel_id=1, source_target_pairs={{0,2},{2,0},{1,3},{3,1},{4,6},{6,4},{5,7},{7,5},{8,10},{10,8},{9,1... | collective-permute-start | bytes 786440 | tf_op jit(solution)/shard_map/ppermute | solution.py:285
  67.5 11.7 %collective-permute-start.16 = (bf16[16,4,2048]{2,1,0:T(4,128)(2,1)S(1)}, bf16[16,4,2048]{2,1,0:T(4,128)(2,1)S(1)}, u32[]{:S(2)}, u32[]{:S(2)}) collective-permute-start(bf16[16,4,2048]{2,1,0:T(4,128)(2,1)S(1)} %get-tuple-element.35), channel_id=1, source_target_pairs={{0,2},{2,0},{1,3},{3,1},{4,6},{6,4},{5,7},{7,5},{8,10},{10,8},{9,1... | collective-permute-start | bytes 786440 | tf_op jit(solution)/shard_map/ppermute | solution.py:285
  67.6 17.2 %collective-permute-start.18 = (bf16[16,4,2048]{2,1,0:T(4,128)(2,1)S(1)}, bf16[16,4,2048]{2,1,0:T(4,128)(2,1)S(1)}, u32[]{:S(2)}, u32[]{:S(2)}) collective-permute-start(bf16[16,4,2048]{2,1,0:T(4,128)(2,1)S(1)} %get-tuple-element.34), channel_id=1, source_target_pairs={{0,2},{2,0},{1,3},{3,1},{4,6},{6,4},{5,7},{7,5},{8,10},{10,8},{9,1... | collective-permute-start | bytes 786440 | tf_op jit(solution)/shard_map/ppermute | solution.py:285
  70.6 17.3 %collective-permute-start.12 = (bf16[8,4,2048]{2,1,0:T(4,128)(2,1)S(1)}, bf16[8,4,2048]{2,1,0:T(4,128)(2,1)S(1)}, u32[]{:S(2)}, u32[]{:S(2)}) collective-permute-start(bf16[8,4,2048]{2,1,0:T(4,128)(2,1)S(1)} %get-tuple-element.30), channel_id=1, source_target_pairs={{0,2},{2,0},{1,3},{3,1},{4,6},{6,4},{5,7},{7,5},{8,10},{10,8},{9,1... | collective-permute-start | bytes 393224 | tf_op jit(solution)/shard_map/ppermute | solution.py:285
  70.8 19.7 %collective-permute-start.20 = (bf16[8,4,2048]{2,1,0:T(4,128)(2,1)S(1)}, bf16[8,4,2048]{2,1,0:T(4,128)(2,1)S(1)}, u32[]{:S(2)}, u32[]{:S(2)}) collective-permute-start(bf16[8,4,2048]{2,1,0:T(4,128)(2,1)S(1)} %get-tuple-element.29), channel_id=1, source_target_pairs={{0,2},{2,0},{1,3},{3,1},{4,6},{6,4},{5,7},{7,5},{8,10},{10,8},{9,1... | collective-permute-start | bytes 393224 | tf_op jit(solution)/shard_map/ppermute | solution.py:285
  85.2 7.6 %collective-permute-start.15 = (bf16[16,4,2048]{2,1,0:T(4,128)(2,1)S(1)}, bf16[16,4,2048]{2,1,0:T(4,128)(2,1)S(1)}, u32[]{:S(2)}, u32[]{:S(2)}) collective-permute-start(bf16[16,4,2048]{2,1,0:T(4,128)(2,1)S(1)} %get-tuple-element.32.refs_0_), channel_id=1, source_target_pairs={{0,1},{1,0},{2,3},{3,2},{4,5},{5,4},{6,7},{7,6},{8,9},{9,8},{10,11... | collective-permute-start | bytes 786440 | tf_op jit(solution)/shard_map/ppermute | solution.py:284
  87.3 5.5 %collective-permute-start.17 = (bf16[16,4,2048]{2,1,0:T(4,128)(2,1)S(1)}, bf16[16,4,2048]{2,1,0:T(4,128)(2,1)S(1)}, u32[]{:S(2)}, u32[]{:S(2)}) collective-permute-start(bf16[16,4,2048]{2,1,0:T(4,128)(2,1)S(1)} %get-tuple-element.33.refs_2_), channel_id=1, source_target_pairs={{0,1},{1,0},{2,3},{3,2},{4,5},{5,4},{6,7},{7,6},{8,9},{9,8},{10,11... | collective-permute-start | bytes 786440 | tf_op jit(solution)/shard_map/ppermute | solution.py:284
  87.4 5.4 %collective-permute-start.19 = (bf16[16,4,2048]{2,1,0:T(4,128)(2,1)S(1)}, bf16[16,4,2048]{2,1,0:T(4,128)(2,1)S(1)}, u32[]{:S(2)}, u32[]{:S(2)}) collective-permute-start(bf16[16,4,2048]{2,1,0:T(4,128)(2,1)S(1)} %get-tuple-element.31.refs_4_), channel_id=1, source_target_pairs={{0,1},{1,0},{2,3},{3,2},{4,5},{5,4},{6,7},{7,6},{8,9},{9,8},{10,11... | collective-permute-start | bytes 786440 | tf_op jit(solution)/shard_map/ppermute | solution.py:284
  90.6 2.3 %collective-permute-start.21 = (bf16[8,4,2048]{2,1,0:T(4,128)(2,1)S(1)}, bf16[8,4,2048]{2,1,0:T(4,128)(2,1)S(1)}, u32[]{:S(2)}, u32[]{:S(2)}) collective-permute-start(bf16[8,4,2048]{2,1,0:T(4,128)(2,1)S(1)} %get-tuple-element.27.refs_6_), channel_id=1, source_target_pairs={{0,1},{1,0},{2,3},{3,2},{4,5},{5,4},{6,7},{7,6},{8,9},{9,8},{10,11... | collective-permute-start | bytes 393224 | tf_op jit(solution)/shard_map/ppermute | solution.py:284
  91.9 2.3 %collective-permute-start.13 = (bf16[8,4,2048]{2,1,0:T(4,128)(2,1)S(1)}, bf16[8,4,2048]{2,1,0:T(4,128)(2,1)S(1)}, u32[]{:S(2)}, u32[]{:S(2)}) collective-permute-start(bf16[8,4,2048]{2,1,0:T(4,128)(2,1)S(1)} %get-tuple-element.28.refs_0_), channel_id=1, source_target_pairs={{0,1},{1,0},{2,3},{3,2},{4,5},{5,4},{6,7},{7,6},{8,9},{9,8},{10,11... | collective-permute-start | bytes 393224 | tf_op jit(solution)/shard_map/ppermute | solution.py:284
  (5 other events, 10.7 us)

commit v3 on v2

--- a/solution.py
+++ b/solution.py
@@ -44,31 +44,26 @@
     return jnp.max(top, axis=1, keepdims=True)
 
 
-def join_body(k_ref, v_ref, out_ref, sem):
-    copies = [
-        pltpu.make_async_copy(k_ref, out_ref.at[:, :HD], sem.at[0]),
-        pltpu.make_async_copy(v_ref, out_ref.at[:, HD:], sem.at[1]),
-    ]
-    for copy in copies:
-        copy.start()
-    for copy in copies:
-        copy.wait()
-
-
-def join(k, v):
+def join_body(k_ref, v_ref, got_k_ref, got_v_ref, out_ref):
+    rows = k_ref.shape[0]
+    out_ref[:rows, :HD] = k_ref[...]
+    out_ref[:rows, HD:] = v_ref[...]
+    out_ref[rows:, :HD] = got_k_ref[...]
+    out_ref[rows:, HD:] = got_v_ref[...]
+
+
+def join(k, v, got_k, got_v):
     return pl.pallas_call(
         join_body,
-        in_specs=[pl.BlockSpec(memory_space=pltpu.HBM)] * 2,
-        out_specs=pl.BlockSpec(memory_space=pltpu.VMEM),
-        out_shape=jax.ShapeDtypeStruct((k.shape[0], 2 * HD), k.dtype),
-        scratch_shapes=[pltpu.SemaphoreType.DMA((2,))],
-        compiler_params=pltpu.CompilerParams(vmem_limit_bytes=60 * MIB),
+        out_shape=jax.ShapeDtypeStruct((2 * k.shape[0], 2 * HD), k.dtype),
+        cost_estimate=pl.CostEstimate(flops=10_000_000_000, bytes_accessed=200_000, transcendentals=0),
+        compiler_params=pltpu.CompilerParams(vmem_limit_bytes=MIB),
         name="join",
-    )(k, v)
-
-
-def suffix_body(q_ref, nk_ref, nv_ref, sk_all, sv_all, len_ref, qp_ref, m_ref, acc_ref, sk_held, sv_held, sem):
-    packs = q_ref.shape[0] // TOK
+    )(k, v, got_k, got_v)
+
+
+def suffix_body(q_ref, nk_ref, nv_ref, sk_all, sv_all, len_ref, _, qp_ref, m_ref, acc_ref, sk_held, sv_held, sem):
+    packs = q_ref.shape[0] * STEPS // TOK
     base = pl.program_id(0) * packs
     per = TOK // STEPS
     keys = per * SLOTS
@@ -101,7 +96,8 @@
     same_n = (((row_n >> 2) & 3) == (col_n >> 2)) & ((col_n & 3) <= (row_n & 3))
 
     def scores(g):
-        block = q_ref[g * TOK : (g + 1) * TOK, :]
+        block = q_ref[g * per : (g + 1) * per, :, :].astype(jnp.float32)
+        block = block.reshape(TOK, GROUP * HD).astype(jnp.bfloat16)
         q = jnp.concatenate([block[:, h * HD : (h + 1) * HD] for h in range(GROUP)], axis=0)
         qp_ref[g * PACK : (g + 1) * PACK, :] = q
         return dot_t(q, sk_ref[g * keys : (g + 1) * keys, :]), dot_t(q, nk_ref[g * TOK : (g + 1) * TOK, :])
@@ -125,10 +121,10 @@
         acc_ref[rows, :] = dot(p, with_ones(sv_ref[g * keys : (g + 1) * keys, :])) + dot(p_n, with_ones(new_v))
 
 
-def suffix(q, sk, sv, nk, nv, lengths):
-    rows = q.shape[0] * GROUP
+def suffix(q, sk, sv, nk, nv, lengths, after):
+    rows = q.shape[0] * STEPS * GROUP
     grid = 4
-    part = lambda a: pl.BlockSpec((a.shape[0] // grid, a.shape[1]), lambda i: (i, 0))
+    part = lambda a: pl.BlockSpec((a.shape[0] // grid,) + a.shape[1:], lambda i: (i,) + (0,) * (len(a.shape) - 1))
     outs = [
         jax.ShapeDtypeStruct((rows, HD), jnp.bfloat16),
         jax.ShapeDtypeStruct((rows, HD), jnp.float32),
@@ -139,14 +135,14 @@
         grid=(grid,),
         in_specs=[part(a) for a in (q, nk, nv)]
         + [pl.BlockSpec(memory_space=pltpu.HBM)] * 2
-        + [pl.BlockSpec(memory_space=pltpu.SMEM)],
+        + [pl.BlockSpec(memory_space=pltpu.SMEM), pl.BlockSpec(memory_space=pl.ANY)],
         out_specs=[part(o) for o in outs],
         out_shape=outs,
         scratch_shapes=[pltpu.VMEM((grid, sk.shape[0] // grid, HD), jnp.bfloat16)] * 2 + [pltpu.SemaphoreType.DMA((2, grid))],
-        cost_estimate=pl.CostEstimate(flops=300_000_000, bytes_accessed=6_000_000, transcendentals=600_000),
+        cost_estimate=pl.CostEstimate(flops=4_000_000_000, bytes_accessed=6_000_000, transcendentals=600_000),
         compiler_params=pltpu.CompilerParams(vmem_limit_bytes=12 * MIB),
         name="suffix",
-    )(q, nk, nv, sk, sv, lengths)
+    )(q, nk, nv, sk, sv, lengths, after)
 
 
 def attend(q, m, acc, kvs, emit, tile=256):
@@ -198,8 +194,7 @@
 
 
 def final_body(n, *refs):
-    weight_ref = refs[3 + n]
-    mine_ref, other_ref, heads_ref = refs[4 + n :]
+    weight_ref, mine_ref, other_ref, heads_ref = refs[3 + n :]
 
     def emit(i, rows, _, out):
         heads = (out[:, :HD] / out[:, HD:]).astype(jnp.bfloat16)
@@ -260,18 +255,17 @@
         copy.wait()
 
 
-def place(pieces, lows, shape, out=None):
+def place(pieces, lows, shape):
     n = len(pieces)
     return pl.pallas_call(
         lambda *refs: place_body(n, lows, *refs),
-        in_specs=[pl.BlockSpec(memory_space=pltpu.VMEM)] * n + ([] if out is None else [pl.BlockSpec(memory_space=pl.ANY)]),
+        in_specs=[pl.BlockSpec(memory_space=pltpu.VMEM)] * n,
         out_specs=pl.BlockSpec(memory_space=pl.ANY),
         out_shape=jax.ShapeDtypeStruct(shape, pieces[0].dtype),
         scratch_shapes=[pltpu.SemaphoreType.DMA((n,))],
-        input_output_aliases={} if out is None else {n: 0},
         compiler_params=pltpu.CompilerParams(vmem_limit_bytes=2 * MIB),
         name="place",
-    )(*pieces, *([] if out is None else [out]))
+    )(*pieces)
 
 
 def local(queries, prefix_keys, prefix_values, suffix_keys, suffix_values, new_keys, new_values, suffix_lengths, out_weight):
@@ -285,12 +279,13 @@
     swap_y = lambda a: lax.ppermute(a, "yhi", [(0, 1), (1, 0)])
 
     flat = lambda a: a.reshape(-1, a.shape[-1])
-    args = [flat(a) for a in (queries, suffix_keys, suffix_values, new_keys, new_values)]
-
-    kv = join(prefix_keys, prefix_values)
-    pair = jnp.concatenate([kv, even(kv)], axis=0)
+    args = [queries] + [flat(a) for a in (suffix_keys, suffix_values, new_keys, new_values)]
+    after = lambda a, b: lax.optimization_barrier((a, b))[0]
+
+    pair = join(prefix_keys, prefix_values, even(prefix_keys), even(prefix_values))
     r2 = odd(pair)
-    r3 = even(r2)
+    q, m, acc = suffix(*args, suffix_lengths, r2)
+    r3 = after(even(r2), m)
     r4 = odd(r3)
     line = jnp.concatenate([pair, r2, r3, r4], axis=0)
     b_x1, b_x3, b_y = x1(line), x3(line), y(line)
@@ -298,24 +293,20 @@
     b_far = x1(b_x3)
     b_yfar = x3(b_yx1)
 
-    q, m, acc = suffix(*args, suffix_lengths)
     m, acc = prefix(q, m, acc, [line])
     m, acc = prefix(q, m, acc, [b_x1, b_x3, b_y])
-    m, acc = prefix(q, m, acc, [b_yx1, b_yx3])
-    mine, other = final(q, m, acc, [b_far, b_yfar], out_weight)
+    m, acc = prefix(q, m, acc, [b_yx1, b_yx3, b_far])
+
+    mine, other = final(q, m, acc, [b_yfar], out_weight)
     terms = (mine + swap_core(other).astype(jnp.float32)).astype(jnp.bfloat16)
-    sizes = (16, 16, 16, 8, 8)
-    lows = [sum(sizes[:i]) for i in range(len(sizes))]
-    pieces = [terms[low : low + size] for low, size in zip(lows, sizes)]
-    moved = [swap_y(piece) for piece in pieces]
+    shape = (requests, STEPS, out_weight.shape[1])
+    cuts = (0, 16, 32, 48, 56, requests)
+    pieces = [terms[low:high] for low, high in zip(cuts, cuts[1:])]
     halves = []
-    for piece, got in zip(pieces, moved):
-        total = piece + got
+    for piece in pieces:
+        total = piece + swap_y(piece)
         halves += [total, swap_core(total)]
-    shape = (requests, STEPS, out_weight.shape[1])
-    early = 2 * (len(sizes) - 1)
-    out = place(halves[:early], lows[:-1], shape)
-    return place(halves[early:], lows[-1:], shape, out)
+    return place(halves, cuts[:-1], shape)
 
 
 def solution(mesh):

time: 95.5 us -> 89.6 us (0.938)
  local copies, waits for them, and re-layouts: 5.97 us -> 1.9 us
  waiting for transfers between devices: 25.6 us -> 28 us
  Pallas kernels: 21.3 us -> 19.4 us
  starting transfers between devices: 39.9 us -> 38.5 us
    unnamed x18 -> x20, local copies, waits for them, and re-layouts: 4.37 us -> 1.46 us
    ppermute x3, waiting for transfers between devices: 0.01 us -> 2.89 us  [local(): x1 = lambda a: lax.ppermute(a, 'x', [(i, i ^ 1) for i in range(4)])]
    ppermute x1, waiting for transfers between devices: 1.45 us -> 0.01 us  [local(): y = lambda a: lax.ppermute(a, 'ylo', [(0, 1), (1, 0)])]
    pallas_call x1, Pallas kernels: 1.45 us -> 0.01 us  [join(): pl.pallas_call(join_body, out_shape=jax.ShapeDtypeStruct((2 * k.shape[0],...]
    ppermute x3, waiting for transfers between devices: 0.01 us -> 1.43 us  [local(): x3 = lambda a: lax.ppermute(a, 'x', [(i, i ^ 3) for i in range(4)])]
    pallas_call x3, Pallas kernels: 9.03 us -> 10.3 us  [prefix(): pl.pallas_call(lambda *refs: prefix_body(len(kvs), *refs), grid=(rows //...]
    reshape x1 -> x0, local copies, waits for them, and re-layouts: 1.16 us -> none  [local(): flat = lambda a: a.reshape(-1, a.shape[-1])]
    ppermute x3, starting transfers between devices: 5.84 us -> 4.69 us  [local(): x3 = lambda a: lax.ppermute(a, 'x', [(i, i ^ 3) for i in range(4)])]
  transfers between devices with their start and end apart: 22 -> 23, of which waited for: 10 -> 15; matrix products, arithmetic and copies ran while one was open for 3% -> 1% of each run, Pallas kernels for 15% -> 16%
where the time goes in v3:
time: 89.6 us; the launch traced here: 89.4 us
  starting transfers between devices  38.5 us (43%)
  waiting for transfers between devices  28 us (31%)
  Pallas kernels  19.4 us (22%)
  local copies, waits for them, and re-layouts  1.9 us (2%)
  other arithmetic  1.24 us (1%)
    ppermute x5, waiting for transfers between devices, local(): swap_y = lambda a: lax.ppermute(a, 'yhi', [(0, 1), (1, 0)])  14.1 us
    ppermute x6, starting transfers between devices, local(): swap_core = lambda a: lax.ppermute(a, 'core', [(0, 1), (1, 0)])  11.6 us
    pallas_call x3, Pallas kernels, prefix(): pl.pallas_call(lambda *refs: prefix_body(len(kvs), *refs), grid=(rows //...  10.3 us
    ppermute x5, starting transfers between devices, local(): swap_y = lambda a: lax.ppermute(a, 'yhi', [(0, 1), (1, 0)])  8.74 us
    ppermute x2, starting transfers between devices, local(): odd = lambda a: lax.ppermute(a, 'z', O_PAIRS)  7.51 us
    ppermute x3, starting transfers between devices, local(): x3 = lambda a: lax.ppermute(a, 'x', [(i, i ^ 3) for i in range(4)])  4.69 us
    pallas_call x1, Pallas kernels, final(): pl.pallas_call(lambda *refs: final_body(len(kvs), *refs), grid=(1,), in_s...  3.93 us
    pallas_call x1, Pallas kernels, suffix(): pl.pallas_call(suffix_body, grid=(grid,), in_specs=[part(a) for a in (q,...  3.83 us
  transfers between devices with their start and end apart: 23, of which 15 were waited for; matrix products, arithmetic and copies ran while one was open for 1% of the time, Pallas kernels for 16%

profile of v3, /device:TPU:1, one launch (start us, length us, event | category | flops | bytes accessed | tf_op | source)
XLA Modules:
  0.0 89.4 jit_solution(2008292644300116998)
XLA Ops:
  0.0 2.6 %collective-permute-start = (bf16[64,128]{1,0:T(8,128)(2,1)}, bf16[64,128]{1,0:T(8,128)(2,1)S(1)}, u32[]{:S(2)}, u32[]{:S(2)}) collective-permute-start(bf16[64,128]{1,0:T(8,128)(2,1)} %k_ref.1), channel_id=1, source_target_pairs={{0,4},{4,0},{8,12},{12,8},{16,20},{20,16},{24,28},{28,24},{1,5},{5... | collective-permute-start | bytes 49160 | tf_op jit(solution)/shard_map/ppermute | solution.py:273
  3.9 1.5 %collective-permute-done.1.got_v_ref = bf16[64,128]{1,0:T(8,128)(2,1)S(1)} collective-permute-done((bf16[64,128]{1,0:T(8,128)(2,1)}, bf16[64,128]{1,0:T(8,128)(2,1)S(1)}, u32[]{:S(2)}, u32[]{:S(2)}) %collective-permute-start.1) | collective-permute-done | bytes 16416 | tf_op jit(solution)/shard_map/ppermute | solution.py:273
  6.8 4.8 %collective-permute-start.2 = (bf16[128,256]{1,0:T(8,128)(2,1)S(1)}, bf16[128,256]{1,0:T(8,128)(2,1)S(1)}, u32[]{:S(2)}, u32[]{:S(2)}) collective-permute-start(bf16[128,256]{1,0:T(8,128)(2,1)S(1)} %join.1), channel_id=1, source_target_pairs={{0,28},{4,8},{8,4},{12,16},{16,12},{20,24},{24,20},{28,0},{1,29},{... | collective-permute-start | bytes 196616 | tf_op jit(solution)/shard_map/ppermute | solution.py:274
  11.6 1.7 %collective-permute-done.2._ = bf16[128,256]{1,0:T(8,128)(2,1)S(1)} collective-permute-done((bf16[128,256]{1,0:T(8,128)(2,1)S(1)}, bf16[128,256]{1,0:T(8,128)(2,1)S(1)}, u32[]{:S(2)}, u32[]{:S(2)}) %collective-permute-start.2) | collective-permute-done | bytes 65568 | tf_op jit(solution)/shard_map/ppermute | solution.py:274
  13.3 3.8 %suffix.1 = (bf16[2048,128]{1,0:T(8,128)(2,1)S(1)}, f32[2048,128]{1,0:T(8,128)S(1)}, f32[2048,256]{1,0:T(8,128)S(1)}) custom-call(bf16[64,4,1024]{2,1,0:T(4,128)(2,1)S(1)} %copy-done.2, bf16[256,128]{1,0:T(8,128)(2,1)S(1)} %bitcast.8, bf16[256,128]{1,0:T(8,128)(2,1)S(1)} %bitcast.9, bf16[4096,128]{1,0:T(8,128)(2,1)S(1)} %bitcast.6, ...), custom_call_target="tpu_custom_call" | custom-call | flops 4000000000 | bytes 6000000 | tf_op jit(solution)/shard_map/suffix/pallas_call | solution.py:133
  17.1 2.8 %collective-permute-start.4 = (bf16[128,256]{1,0:T(8,128)(2,1)S(1)}, bf16[128,256]{1,0:T(8,128)(2,1)S(1)}, u32[]{:S(2)}, u32[]{:S(2)}) collective-permute-start(bf16[128,256]{1,0:T(8,128)(2,1)S(1)} %collective-permute-done.3), channel_id=1, source_target_pairs={{0,28},{4,8},{8,4},{12,16},{16,12},{20,24},{24,20},{28,0},{1,29},{... | collective-permute-start | bytes 196616 | tf_op jit(solution)/shard_map/ppermute | solution.py:274
  19.9 1.7 %collective-permute-done.4 = bf16[128,256]{1,0:T(8,128)(2,1)S(1)} collective-permute-done((bf16[128,256]{1,0:T(8,128)(2,1)S(1)}, bf16[128,256]{1,0:T(8,128)(2,1)S(1)}, u32[]{:S(2)}, u32[]{:S(2)}) %collective-permute-start.4) | collective-permute-done | bytes 65568 | tf_op jit(solution)/shard_map/ppermute | solution.py:274
  23.0 2.5 %collective-permute-start.6 = (bf16[512,256]{1,0:T(8,128)(2,1)S(1)}, bf16[512,256]{1,0:T(8,128)(2,1)S(1)}, u32[]{:S(2)}, u32[]{:S(2)}) collective-permute-start(bf16[512,256]{1,0:T(8,128)(2,1)S(1)} %pad_maximum_fusion.refs_3_), channel_id=1, source_target_pairs={{0,96},{32,64},{64,32},{96,0},{1,97},{33,65},{65,33},{97,1},{2,98}... | collective-permute-start | bytes 786440 | tf_op jit(solution)/shard_map/ppermute | solution.py:276
  25.4 1.9 %prefix.3 = (f32[2048,128]{1,0:T(8,128)S(1)}, f32[2048,256]{1,0:T(8,128)S(1)}) custom-call(bf16[2048,128]{1,0:T(8,128)(2,1)S(1)} %get-tuple-element.17.refs_0_, f32[2048,128]{1,0:T(8,128)S(1)} %get-tuple-element.18.refs_1_, f32[2048,256]{1,0:T(8,128)S(1)} %get-tuple-element.19.refs_2_, bf16[512,256]{1,0:T(8,128)(2,1)S(1)} %pad_maximum_fusion.refs_3_), custom_call_target="tpu_custom_call" | custom-call | flops 1073741824 | bytes 7000000 | tf_op jit(solution)/shard_map/prefix/pallas_call | solution.py:184
  27.4 1.5 %collective-permute-start.8 = (bf16[512,256]{1,0:T(8,128)(2,1)S(1)}, bf16[512,256]{1,0:T(8,128)(2,1)S(1)}, u32[]{:S(2)}, u32[]{:S(2)}) collective-permute-start(bf16[512,256]{1,0:T(8,128)(2,1)S(1)} %collective-permute-done.7.refs_5_), channel_id=1, source_target_pairs={{0,32},{32,0},{64,96},{96,64},{1,33},{33,1},{65,97},{97,65},{2,34}... | collective-permute-start | bytes 786440 | tf_op jit(solution)/shard_map/ppermute | solution.py:275
  31.0 4.2 %prefix.4 = (f32[2048,128]{1,0:T(8,128)S(1)}, f32[2048,256]{1,0:T(8,128)S(1)}) custom-call(bf16[2048,128]{1,0:T(8,128)(2,1)S(1)} %get-tuple-element.17.refs_0_, f32[2048,128]{1,0:T(8,128)S(1)} %get-tuple-element.21.refs_1_, f32[2048,256]{1,0:T(8,128)S(1)} %get-tuple-element.22.refs_2_, bf16[512,256]{1,0:T(8,128)(2,1)S(1)} %collective-permute-done.5.refs_3_, ...), custom_call_target="tpu_custom_call" | custom-call | flops 3221225472 | bytes 7000000 | tf_op jit(solution)/shard_map/prefix/pallas_call | solution.py:184
  37.4 2.2 %collective-permute-done.10.refs_5_ = bf16[512,256]{1,0:T(8,128)(2,1)S(1)} collective-permute-done((bf16[512,256]{1,0:T(8,128)(2,1)S(1)}, bf16[512,256]{1,0:T(8,128)(2,1)S(1)}, u32[]{:S(2)}, u32[]{:S(2)}) %collective-permute-start.10) | collective-permute-done | bytes 262176 | tf_op jit(solution)/shard_map/ppermute | solution.py:275
  39.5 4.2 %prefix.5 = (f32[2048,128]{1,0:T(8,128)S(1)}, f32[2048,256]{1,0:T(8,128)S(1)}) custom-call(bf16[2048,128]{1,0:T(8,128)(2,1)S(1)} %get-tuple-element.17.refs_0_, f32[2048,128]{1,0:T(8,128)S(1)} %get-tuple-element.23.refs_1_, f32[2048,256]{1,0:T(8,128)S(1)} %get-tuple-element.24.refs_2_, bf16[512,256]{1,0:T(8,128)(2,1)S(1)} %collective-permute-done.8.refs_3_, ...), custom_call_target="tpu_custom_call" | custom-call | flops 3221225472 | bytes 7000000 | tf_op jit(solution)/shard_map/prefix/pallas_call | solution.py:184
  44.2 3.9 %final.1 = (f32[64,4,2048]{2,1,0:T(4,128)S(1)}, bf16[64,4,2048]{2,1,0:T(4,128)(2,1)S(1)}) custom-call(bf16[2048,128]{1,0:T(8,128)(2,1)S(1)} %get-tuple-element.17.refs_0_, f32[2048,128]{1,0:T(8,128)S(1)} %get-tuple-element.25.refs_1_, f32[2048,256]{1,0:T(8,128)S(1)} %get-tuple-element.26.refs_2_, bf16[512,256]{1,0:T(8,128)(2,1)S(1)} %collective-permute-done.11.refs_3_, ...), custom_call_target="tpu_custom_call" | custom-call | flops 9663676416 | bytes 12000000 | tf_op jit(solution)/shard_map/final/pallas_call | solution.py:227
  48.1 7.6 %collective-permute-start.12 = (bf16[64,4,2048]{2,1,0:T(4,128)(2,1)S(1)}, bf16[64,4,2048]{2,1,0:T(4,128)(2,1)S(1)}, u32[]{:S(2)}, u32[]{:S(2)}) collective-permute-start(bf16[64,4,2048]{2,1,0:T(4,128)(2,1)S(1)} %get-tuple-element.28), channel_id=1, source_target_pairs={{0,1},{1,0},{2,3},{3,2},{4,5},{5,4},{6,7},{7,6},{8,9},{9,8},{10,11... | collective-permute-start | bytes 3145736 | tf_op jit(solution)/shard_map/ppermute | solution.py:278
  55.7 2.3 %collective-permute-done.12 = bf16[64,4,2048]{2,1,0:T(4,128)(2,1)S(1)} collective-permute-done((bf16[64,4,2048]{2,1,0:T(4,128)(2,1)S(1)}, bf16[64,4,2048]{2,1,0:T(4,128)(2,1)S(1)}, u32[]{:S(2)}, u32[]{:S(2)}) %collective-permute-start.12) | collective-permute-done | bytes 1048608 | tf_op jit(solution)/shard_map/ppermute | solution.py:278
  59.0 2.7 %collective-permute-start.13 = (bf16[16,4,2048]{2,1,0:T(4,128)(2,1)S(1)}, bf16[16,4,2048]{2,1,0:T(4,128)(2,1)S(1)}, u32[]{:S(2)}, u32[]{:S(2)}) collective-permute-start(bf16[16,4,2048]{2,1,0:T(4,128)(2,1)S(1)} %get-tuple-element.38), channel_id=1, source_target_pairs={{0,2},{2,0},{1,3},{3,1},{4,6},{6,4},{5,7},{7,5},{8,10},{10,8},{9,1... | collective-permute-start | bytes 786440 | tf_op jit(solution)/shard_map/ppermute | solution.py:279
  62.1 2.6 %collective-permute-start.17 = (bf16[16,4,2048]{2,1,0:T(4,128)(2,1)S(1)}, bf16[16,4,2048]{2,1,0:T(4,128)(2,1)S(1)}, u32[]{:S(2)}, u32[]{:S(2)}) collective-permute-start(bf16[16,4,2048]{2,1,0:T(4,128)(2,1)S(1)} %get-tuple-element.36), channel_id=1, source_target_pairs={{0,2},{2,0},{1,3},{3,1},{4,6},{6,4},{5,7},{7,5},{8,10},{10,8},{9,1... | collective-permute-start | bytes 786440 | tf_op jit(solution)/shard_map/ppermute | solution.py:279
  65.3 2.6 %collective-permute-start.21 = (bf16[8,4,2048]{2,1,0:T(4,128)(2,1)S(1)}, bf16[8,4,2048]{2,1,0:T(4,128)(2,1)S(1)}, u32[]{:S(2)}, u32[]{:S(2)}) collective-permute-start(bf16[8,4,2048]{2,1,0:T(4,128)(2,1)S(1)} %get-tuple-element.31), channel_id=1, source_target_pairs={{0,2},{2,0},{1,3},{3,1},{4,6},{6,4},{5,7},{7,5},{8,10},{10,8},{9,1... | collective-permute-start | bytes 393224 | tf_op jit(solution)/shard_map/ppermute | solution.py:279
  68.2 5.6 %collective-permute-done.15 = bf16[16,4,2048]{2,1,0:T(4,128)(2,1)S(1)} collective-permute-done((bf16[16,4,2048]{2,1,0:T(4,128)(2,1)S(1)}, bf16[16,4,2048]{2,1,0:T(4,128)(2,1)S(1)}, u32[]{:S(2)}, u32[]{:S(2)}) %collective-permute-start.15) | collective-permute-done | bytes 262176 | tf_op jit(solution)/shard_map/ppermute | solution.py:279
  73.8 5.6 %collective-permute-done.17 = bf16[16,4,2048]{2,1,0:T(4,128)(2,1)S(1)} collective-permute-done((bf16[16,4,2048]{2,1,0:T(4,128)(2,1)S(1)}, bf16[16,4,2048]{2,1,0:T(4,128)(2,1)S(1)}, u32[]{:S(2)}, u32[]{:S(2)}) %collective-permute-start.17) | collective-permute-done | bytes 262176 | tf_op jit(solution)/shard_map/ppermute | solution.py:279
  79.8 2.1 %collective-permute-start.14 = (bf16[16,4,2048]{2,1,0:T(4,128)(2,1)S(1)}, bf16[16,4,2048]{2,1,0:T(4,128)(2,1)S(1)}, u32[]{:S(2)}, u32[]{:S(2)}) collective-permute-start(bf16[16,4,2048]{2,1,0:T(4,128)(2,1)S(1)} %get-tuple-element.34.refs_0_), channel_id=1, source_target_pairs={{0,1},{1,0},{2,3},{3,2},{4,5},{5,4},{6,7},{7,6},{8,9},{9,8},{10,11... | collective-permute-start | bytes 786440 | tf_op jit(solution)/shard_map/ppermute | solution.py:278
  82.4 2.6 %collective-permute-done.21 = bf16[8,4,2048]{2,1,0:T(4,128)(2,1)S(1)} collective-permute-done((bf16[8,4,2048]{2,1,0:T(4,128)(2,1)S(1)}, bf16[8,4,2048]{2,1,0:T(4,128)(2,1)S(1)}, u32[]{:S(2)}, u32[]{:S(2)}) %collective-permute-start.21) | collective-permute-done | bytes 131104 | tf_op jit(solution)/shard_map/ppermute | solution.py:279
  87.8 1.4 %place.1 = bf16[64,4,4096]{2,1,0:T(4,128)(2,1)} custom-call(bf16[16,4,2048]{2,1,0:T(4,128)(2,1)S(1)} %get-tuple-element.34.refs_0_, bf16[16,4,2048]{2,1,0:T(4,128)(2,1)S(1)} %collective-permute-done.14.refs_1_, bf16[16,4,2048]{2,1,0:T(4,128)(2,1)S(1)} %get-tuple-element.35.refs_2_, bf16[16,4,2048]{2,1,0:T(4,128)(2,1)S(1)} %collective-permute-done.16.refs_3_, ...), custom_call_target="tpu_custom_call" | custom-call | tf_op jit(solution)/shard_map/place/pallas_call | solution.py:260
  (56 shorter events, 14.8 us)
Async XLA Ops:
  0.0 13.3 %copy-start.1 = (bf16[64,64,128]{2,1,0:T(8,128)(2,1)S(1)}, bf16[64,64,128]{2,1,0:T(8,128)(2,1)}, u32[]{:S(2)}) copy-start(bf16[64,64,128]{2,1,0:T(8,128)(2,1)} %param.13) | copy-start | bytes 3145732
  0.0 3.9 %collective-permute-start = (bf16[64,128]{1,0:T(8,128)(2,1)}, bf16[64,128]{1,0:T(8,128)(2,1)S(1)}, u32[]{:S(2)}, u32[]{:S(2)}) collective-permute-start(bf16[64,128]{1,0:T(8,128)(2,1)} %k_ref.1), channel_id=1, source_target_pairs={{0,4},{4,0},{8,12},{12,8},{16,20},{20,16},{24,28},{28,24},{1,5},{5... | collective-permute-start | bytes 49160 | tf_op jit(solution)/shard_map/ppermute | solution.py:273
  2.6 2.8 %collective-permute-start.1 = (bf16[64,128]{1,0:T(8,128)(2,1)}, bf16[64,128]{1,0:T(8,128)(2,1)S(1)}, u32[]{:S(2)}, u32[]{:S(2)}) collective-permute-start(bf16[64,128]{1,0:T(8,128)(2,1)} %v_ref.1), channel_id=1, source_target_pairs={{0,4},{4,0},{8,12},{12,8},{16,20},{20,16},{24,28},{28,24},{1,5},{5... | collective-permute-start | bytes 49160 | tf_op jit(solution)/shard_map/ppermute | solution.py:273
  6.8 6.4 %collective-permute-start.2 = (bf16[128,256]{1,0:T(8,128)(2,1)S(1)}, bf16[128,256]{1,0:T(8,128)(2,1)S(1)}, u32[]{:S(2)}, u32[]{:S(2)}) collective-permute-start(bf16[128,256]{1,0:T(8,128)(2,1)S(1)} %join.1), channel_id=1, source_target_pairs={{0,28},{4,8},{8,4},{12,16},{16,12},{20,24},{24,20},{28,0},{1,29},{... | collective-permute-start | bytes 196616 | tf_op jit(solution)/shard_map/ppermute | solution.py:274
  13.2 3.9 %collective-permute-start.3 = (bf16[128,256]{1,0:T(8,128)(2,1)S(1)}, bf16[128,256]{1,0:T(8,128)(2,1)S(1)}, u32[]{:S(2)}, u32[]{:S(2)}) collective-permute-start(bf16[128,256]{1,0:T(8,128)(2,1)S(1)} %collective-permute-done.2._), channel_id=1, source_target_pairs={{0,4},{4,0},{8,12},{12,8},{16,20},{20,16},{24,28},{28,24},{1,5},{5... | collective-permute-start | bytes 196616 | tf_op jit(solution)/shard_map/ppermute | solution.py:273
  17.1 4.4 %collective-permute-start.4 = (bf16[128,256]{1,0:T(8,128)(2,1)S(1)}, bf16[128,256]{1,0:T(8,128)(2,1)S(1)}, u32[]{:S(2)}, u32[]{:S(2)}) collective-permute-start(bf16[128,256]{1,0:T(8,128)(2,1)S(1)} %collective-permute-done.3), channel_id=1, source_target_pairs={{0,28},{4,8},{8,4},{12,16},{16,12},{20,24},{24,20},{28,0},{1,29},{... | collective-permute-start | bytes 196616 | tf_op jit(solution)/shard_map/ppermute | solution.py:274
  21.6 5.8 %collective-permute-start.7 = (bf16[512,256]{1,0:T(8,128)(2,1)S(1)}, bf16[512,256]{1,0:T(8,128)(2,1)S(1)}, u32[]{:S(2)}, u32[]{:S(2)}) collective-permute-start(bf16[512,256]{1,0:T(8,128)(2,1)S(1)} %pad_maximum_fusion.refs_3_), channel_id=1, source_target_pairs={{0,128},{128,0},{1,129},{129,1},{2,130},{130,2},{3,131},{131,3},{4... | collective-permute-start | bytes 786440 | tf_op jit(solution)/shard_map/ppermute | solution.py:277
  23.0 7.0 %collective-permute-start.6 = (bf16[512,256]{1,0:T(8,128)(2,1)S(1)}, bf16[512,256]{1,0:T(8,128)(2,1)S(1)}, u32[]{:S(2)}, u32[]{:S(2)}) collective-permute-start(bf16[512,256]{1,0:T(8,128)(2,1)S(1)} %pad_maximum_fusion.refs_3_), channel_id=1, source_target_pairs={{0,96},{32,64},{64,32},{96,0},{1,97},{33,65},{65,33},{97,1},{2,98}... | collective-permute-start | bytes 786440 | tf_op jit(solution)/shard_map/ppermute | solution.py:276
  25.4 5.5 %collective-permute-start.5 = (bf16[512,256]{1,0:T(8,128)(2,1)S(1)}, bf16[512,256]{1,0:T(8,128)(2,1)S(1)}, u32[]{:S(2)}, u32[]{:S(2)}) collective-permute-start(bf16[512,256]{1,0:T(8,128)(2,1)S(1)} %pad_maximum_fusion.refs_3_), channel_id=1, source_target_pairs={{0,32},{32,0},{64,96},{96,64},{1,33},{33,1},{65,97},{97,65},{2,34}... | collective-permute-start | bytes 786440 | tf_op jit(solution)/shard_map/ppermute | solution.py:275
  27.4 7.8 %collective-permute-start.8 = (bf16[512,256]{1,0:T(8,128)(2,1)S(1)}, bf16[512,256]{1,0:T(8,128)(2,1)S(1)}, u32[]{:S(2)}, u32[]{:S(2)}) collective-permute-start(bf16[512,256]{1,0:T(8,128)(2,1)S(1)} %collective-permute-done.7.refs_5_), channel_id=1, source_target_pairs={{0,32},{32,0},{64,96},{96,64},{1,33},{33,1},{65,97},{97,65},{2,34}... | collective-permute-start | bytes 786440 | tf_op jit(solution)/shard_map/ppermute | solution.py:275
  28.9 8.4 %collective-permute-start.9 = (bf16[512,256]{1,0:T(8,128)(2,1)S(1)}, bf16[512,256]{1,0:T(8,128)(2,1)S(1)}, u32[]{:S(2)}, u32[]{:S(2)}) collective-permute-start(bf16[512,256]{1,0:T(8,128)(2,1)S(1)} %collective-permute-done.7.refs_5_), channel_id=1, source_target_pairs={{0,96},{32,64},{64,32},{96,0},{1,97},{33,65},{65,33},{97,1},{2,98}... | collective-permute-start | bytes 786440 | tf_op jit(solution)/shard_map/ppermute | solution.py:276
  29.9 9.6 %collective-permute-start.10 = (bf16[512,256]{1,0:T(8,128)(2,1)S(1)}, bf16[512,256]{1,0:T(8,128)(2,1)S(1)}, u32[]{:S(2)}, u32[]{:S(2)}) collective-permute-start(bf16[512,256]{1,0:T(8,128)(2,1)S(1)} %collective-permute-done.6.refs_4_), channel_id=1, source_target_pairs={{0,32},{32,0},{64,96},{96,64},{1,33},{33,1},{65,97},{97,65},{2,34}... | collective-permute-start | bytes 786440 | tf_op jit(solution)/shard_map/ppermute | solution.py:275
  35.2 9.0 %collective-permute-start.11 = (bf16[512,256]{1,0:T(8,128)(2,1)S(1)}, bf16[512,256]{1,0:T(8,128)(2,1)S(1)}, u32[]{:S(2)}, u32[]{:S(2)}) collective-permute-start(bf16[512,256]{1,0:T(8,128)(2,1)S(1)} %collective-permute-done.8.refs_3_), channel_id=1, source_target_pairs={{0,96},{32,64},{64,32},{96,0},{1,97},{33,65},{65,33},{97,1},{2,98}... | collective-permute-start | bytes 786440 | tf_op jit(solution)/shard_map/ppermute | solution.py:276
  48.1 9.9 %collective-permute-start.12 = (bf16[64,4,2048]{2,1,0:T(4,128)(2,1)S(1)}, bf16[64,4,2048]{2,1,0:T(4,128)(2,1)S(1)}, u32[]{:S(2)}, u32[]{:S(2)}) collective-permute-start(bf16[64,4,2048]{2,1,0:T(4,128)(2,1)S(1)} %get-tuple-element.28), channel_id=1, source_target_pairs={{0,1},{1,0},{2,3},{3,2},{4,5},{5,4},{6,7},{7,6},{8,9},{9,8},{10,11... | collective-permute-start | bytes 3145736 | tf_op jit(solution)/shard_map/ppermute | solution.py:278
  59.0 9.1 %collective-permute-start.13 = (bf16[16,4,2048]{2,1,0:T(4,128)(2,1)S(1)}, bf16[16,4,2048]{2,1,0:T(4,128)(2,1)S(1)}, u32[]{:S(2)}, u32[]{:S(2)}) collective-permute-start(bf16[16,4,2048]{2,1,0:T(4,128)(2,1)S(1)} %get-tuple-element.38), channel_id=1, source_target_pairs={{0,2},{2,0},{1,3},{3,1},{4,6},{6,4},{5,7},{7,5},{8,10},{10,8},{9,1... | collective-permute-start | bytes 786440 | tf_op jit(solution)/shard_map/ppermute | solution.py:279
  61.8 12.0 %collective-permute-start.15 = (bf16[16,4,2048]{2,1,0:T(4,128)(2,1)S(1)}, bf16[16,4,2048]{2,1,0:T(4,128)(2,1)S(1)}, u32[]{:S(2)}, u32[]{:S(2)}) collective-permute-start(bf16[16,4,2048]{2,1,0:T(4,128)(2,1)S(1)} %get-tuple-element.37), channel_id=1, source_target_pairs={{0,2},{2,0},{1,3},{3,1},{4,6},{6,4},{5,7},{7,5},{8,10},{10,8},{9,1... | collective-permute-start | bytes 786440 | tf_op jit(solution)/shard_map/ppermute | solution.py:279
  62.1 17.3 %collective-permute-start.17 = (bf16[16,4,2048]{2,1,0:T(4,128)(2,1)S(1)}, bf16[16,4,2048]{2,1,0:T(4,128)(2,1)S(1)}, u32[]{:S(2)}, u32[]{:S(2)}) collective-permute-start(bf16[16,4,2048]{2,1,0:T(4,128)(2,1)S(1)} %get-tuple-element.36), channel_id=1, source_target_pairs={{0,2},{2,0},{1,3},{3,1},{4,6},{6,4},{5,7},{7,5},{8,10},{10,8},{9,1... | collective-permute-start | bytes 786440 | tf_op jit(solution)/shard_map/ppermute | solution.py:279
  64.8 17.6 %collective-permute-start.19 = (bf16[8,4,2048]{2,1,0:T(4,128)(2,1)S(1)}, bf16[8,4,2048]{2,1,0:T(4,128)(2,1)S(1)}, u32[]{:S(2)}, u32[]{:S(2)}) collective-permute-start(bf16[8,4,2048]{2,1,0:T(4,128)(2,1)S(1)} %get-tuple-element.32), channel_id=1, source_target_pairs={{0,2},{2,0},{1,3},{3,1},{4,6},{6,4},{5,7},{7,5},{8,10},{10,8},{9,1... | collective-permute-start | bytes 393224 | tf_op jit(solution)/shard_map/ppermute | solution.py:279
  65.3 19.7 %collective-permute-start.21 = (bf16[8,4,2048]{2,1,0:T(4,128)(2,1)S(1)}, bf16[8,4,2048]{2,1,0:T(4,128)(2,1)S(1)}, u32[]{:S(2)}, u32[]{:S(2)}) collective-permute-start(bf16[8,4,2048]{2,1,0:T(4,128)(2,1)S(1)} %get-tuple-element.31), channel_id=1, source_target_pairs={{0,2},{2,0},{1,3},{3,1},{4,6},{6,4},{5,7},{7,5},{8,10},{10,8},{9,1... | collective-permute-start | bytes 393224 | tf_op jit(solution)/shard_map/ppermute | solution.py:279
  79.8 8.0 %collective-permute-start.14 = (bf16[16,4,2048]{2,1,0:T(4,128)(2,1)S(1)}, bf16[16,4,2048]{2,1,0:T(4,128)(2,1)S(1)}, u32[]{:S(2)}, u32[]{:S(2)}) collective-permute-start(bf16[16,4,2048]{2,1,0:T(4,128)(2,1)S(1)} %get-tuple-element.34.refs_0_), channel_id=1, source_target_pairs={{0,1},{1,0},{2,3},{3,2},{4,5},{5,4},{6,7},{7,6},{8,9},{9,8},{10,11... | collective-permute-start | bytes 786440 | tf_op jit(solution)/shard_map/ppermute | solution.py:278
  81.9 5.9 %collective-permute-start.16 = (bf16[16,4,2048]{2,1,0:T(4,128)(2,1)S(1)}, bf16[16,4,2048]{2,1,0:T(4,128)(2,1)S(1)}, u32[]{:S(2)}, u32[]{:S(2)}) collective-permute-start(bf16[16,4,2048]{2,1,0:T(4,128)(2,1)S(1)} %get-tuple-element.35.refs_2_), channel_id=1, source_target_pairs={{0,1},{1,0},{2,3},{3,2},{4,5},{5,4},{6,7},{7,6},{8,9},{9,8},{10,11... | collective-permute-start | bytes 786440 | tf_op jit(solution)/shard_map/ppermute | solution.py:278
  82.0 5.8 %collective-permute-start.18 = (bf16[16,4,2048]{2,1,0:T(4,128)(2,1)S(1)}, bf16[16,4,2048]{2,1,0:T(4,128)(2,1)S(1)}, u32[]{:S(2)}, u32[]{:S(2)}) collective-permute-start(bf16[16,4,2048]{2,1,0:T(4,128)(2,1)S(1)} %get-tuple-element.33.refs_4_), channel_id=1, source_target_pairs={{0,1},{1,0},{2,3},{3,2},{4,5},{5,4},{6,7},{7,6},{8,9},{9,8},{10,11... | collective-permute-start | bytes 786440 | tf_op jit(solution)/shard_map/ppermute | solution.py:278
  85.1 2.3 %collective-permute-start.20 = (bf16[8,4,2048]{2,1,0:T(4,128)(2,1)S(1)}, bf16[8,4,2048]{2,1,0:T(4,128)(2,1)S(1)}, u32[]{:S(2)}, u32[]{:S(2)}) collective-permute-start(bf16[8,4,2048]{2,1,0:T(4,128)(2,1)S(1)} %get-tuple-element.30.refs_6_), channel_id=1, source_target_pairs={{0,1},{1,0},{2,3},{3,2},{4,5},{5,4},{6,7},{7,6},{8,9},{9,8},{10,11... | collective-permute-start | bytes 393224 | tf_op jit(solution)/shard_map/ppermute | solution.py:278
  86.4 1.3 %collective-permute-start.22 = (bf16[8,4,2048]{2,1,0:T(4,128)(2,1)S(1)}, bf16[8,4,2048]{2,1,0:T(4,128)(2,1)S(1)}, u32[]{:S(2)}, u32[]{:S(2)}) collective-permute-start(bf16[8,4,2048]{2,1,0:T(4,128)(2,1)S(1)} %get-tuple-element.29.refs_8_), channel_id=1, source_target_pairs={{0,1},{1,0},{2,3},{3,2},{4,5},{5,4},{6,7},{7,6},{8,9},{9,8},{10,11... | collective-permute-start | bytes 393224 | tf_op jit(solution)/shard_map/ppermute | solution.py:278
  (9 other events, 78.8 us)

commit v4 on v3

--- a/solution.py
+++ b/solution.py
@@ -44,22 +44,26 @@
     return jnp.max(top, axis=1, keepdims=True)
 
 
-def join_body(k_ref, v_ref, got_k_ref, got_v_ref, out_ref):
+def pack_body(k_ref, v_ref, out_ref):
+    out_ref[:, :HD] = k_ref[...]
+    out_ref[:, HD:] = v_ref[...]
+
+
+def join_body(own_ref, k_ref, v_ref, out_ref):
     rows = k_ref.shape[0]
-    out_ref[:rows, :HD] = k_ref[...]
-    out_ref[:rows, HD:] = v_ref[...]
-    out_ref[rows:, :HD] = got_k_ref[...]
-    out_ref[rows:, HD:] = got_v_ref[...]
-
-
-def join(k, v, got_k, got_v):
-    return pl.pallas_call(
-        join_body,
-        out_shape=jax.ShapeDtypeStruct((2 * k.shape[0], 2 * HD), k.dtype),
-        cost_estimate=pl.CostEstimate(flops=10_000_000_000, bytes_accessed=200_000, transcendentals=0),
+    out_ref[:rows, :] = own_ref[...]
+    out_ref[rows:, :HD] = k_ref[...]
+    out_ref[rows:, HD:] = v_ref[...]
+
+
+def glue(body, rows, flops, *arrays):
+    return pl.pallas_call(
+        body,
+        out_shape=jax.ShapeDtypeStruct((rows, 2 * HD), arrays[0].dtype),
+        cost_estimate=pl.CostEstimate(flops=flops, bytes_accessed=200_000, transcendentals=0),
         compiler_params=pltpu.CompilerParams(vmem_limit_bytes=MIB),
-        name="join",
-    )(k, v, got_k, got_v)
+        name="glue",
+    )(*arrays)
 
 
 def suffix_body(q_ref, nk_ref, nv_ref, sk_all, sv_all, len_ref, _, qp_ref, m_ref, acc_ref, sk_held, sv_held, sem):
@@ -194,7 +198,8 @@
 
 
 def final_body(n, *refs):
-    weight_ref, mine_ref, other_ref, heads_ref = refs[3 + n :]
+    weight_ref, mine_ref, head_ref, tail_ref, heads_ref = refs[3 + n :]
+    low = head_ref.shape[0]
 
     def emit(i, rows, _, out):
         heads = (out[:, :HD] / out[:, HD:]).astype(jnp.bfloat16)
@@ -210,20 +215,26 @@
     requests, steps, half = mine_ref.shape
     core = lax.axis_index("core")
     width = 512
-    for ref, side in ((other_ref, 1 - core), (mine_ref, core)):
+    for side in (1 - core, core):
         for j in range(0, half, width):
             columns = pl.ds(pl.multiple_of(side * half + j, width), width)
-            terms = dot(heads, weight_ref[:, columns])
-            ref[:, :, j : j + width] = terms.reshape(requests, steps, width).astype(ref.dtype)
-
-
-def final(q, m, acc, kvs, weight):
+            terms = dot(heads, weight_ref[:, columns]).reshape(requests, steps, width)
+            if side is core:
+                mine_ref[:, :, j : j + width] = terms
+            else:
+                terms = terms.astype(head_ref.dtype)
+                head_ref[:, :, j : j + width] = terms[:low]
+                tail_ref[:, :, j : j + width] = terms[low:]
+
+
+def final(q, m, acc, kvs, weight, low):
     rows = q.shape[0]
     tokens, half = rows // GROUP, weight.shape[1] // 2
     keys = sum(kv.shape[0] for kv in kvs)
     whole = lambda a: pl.BlockSpec(a.shape, lambda i: (0,) * len(a.shape))
-    shape = (tokens // STEPS, STEPS, half)
-    outs = [jax.ShapeDtypeStruct(shape, jnp.float32), jax.ShapeDtypeStruct(shape, jnp.bfloat16)]
+    requests = tokens // STEPS
+    outs = [jax.ShapeDtypeStruct((requests, STEPS, half), jnp.float32)]
+    outs += [jax.ShapeDtypeStruct((n, STEPS, half), jnp.bfloat16) for n in (low, requests - low)]
     return pl.pallas_call(
         lambda *refs: final_body(len(kvs), *refs),
         grid=(1,),
@@ -282,29 +293,34 @@
     args = [queries] + [flat(a) for a in (suffix_keys, suffix_values, new_keys, new_values)]
     after = lambda a, b: lax.optimization_barrier((a, b))[0]
 
-    pair = join(prefix_keys, prefix_values, even(prefix_keys), even(prefix_values))
+    own = glue(pack_body, prefix_keys.shape[0], 2_000_000_000, prefix_keys, prefix_values)
+    pair = glue(join_body, 2 * own.shape[0], 10_000_000_000, own, even(prefix_keys), even(prefix_values))
     r2 = odd(pair)
     q, m, acc = suffix(*args, suffix_lengths, r2)
     r3 = after(even(r2), m)
     r4 = odd(r3)
     line = jnp.concatenate([pair, r2, r3, r4], axis=0)
     b_x1, b_x3, b_y = x1(line), x3(line), y(line)
-    b_yx1, b_yx3 = x1(b_y), x3(b_y)
-    b_far = x1(b_x3)
-    b_yfar = x3(b_yx1)
-
     m, acc = prefix(q, m, acc, [line])
-    m, acc = prefix(q, m, acc, [b_x1, b_x3, b_y])
-    m, acc = prefix(q, m, acc, [b_yx1, b_yx3, b_far])
-
-    mine, other = final(q, m, acc, [b_yfar], out_weight)
-    terms = (mine + swap_core(other).astype(jnp.float32)).astype(jnp.bfloat16)
+    sent_y = after(b_y, m)
+    b_yx1, b_yx3 = x1(sent_y), x3(sent_y)
+    m, acc = prefix(q, m, acc, [b_y, b_x1])
+    b_far, b_yfar = x1(after(b_x3, (b_yx1, m))), x3(after(b_yx1, m))
+    m, acc = prefix(q, m, acc, [b_x3, b_yx1, b_yx3])
+
     shape = (requests, STEPS, out_weight.shape[1])
     cuts = (0, 16, 32, 48, 56, requests)
-    pieces = [terms[low:high] for low, high in zip(cuts, cuts[1:])]
+    low = cuts[1]
+    mine, other_head, other_tail = final(q, m, acc, [b_far, b_yfar], out_weight, low)
+    combine = lambda mine, got: (mine + got.astype(jnp.float32)).astype(jnp.bfloat16)
+    head = combine(mine[:low], swap_core(other_head))
+    tail = combine(mine[low:], swap_core(other_tail))
+    pieces = [head] + [tail[a - low : b - low] for a, b in zip(cuts[1:], cuts[2:])]
+    moved = [swap_y(piece) for piece in pieces]
+    moved[:3] = lax.optimization_barrier(moved[:3])
     halves = []
-    for piece in pieces:
-        total = piece + swap_y(piece)
+    for piece, got in zip(pieces, moved):
+        total = piece + got
         halves += [total, swap_core(total)]
     return place(halves, cuts[:-1], shape)
 

time: 89.6 us -> 85.4 us (0.953)
  starting transfers between devices: 38.5 us -> 35.1 us
    ppermute x6 -> x7, starting transfers between devices: 11.6 us -> 8.51 us  [local(): swap_core = lambda a: lax.ppermute(a, 'core', [(0, 1), (1, 0)])]
    ppermute x3, waiting for transfers between devices: 2.7 us -> 1.25 us  [local(): even = lambda a: lax.ppermute(a, 'z', E_PAIRS)]
    ppermute x3, waiting for transfers between devices: 2.89 us -> 4.21 us  [local(): x1 = lambda a: lax.ppermute(a, 'x', [(i, i ^ 1) for i in range(4)])]
    pallas_call x3, Pallas kernels: 10.3 us -> 9 us  [prefix(): pl.pallas_call(lambda *refs: prefix_body(len(kvs), *refs), grid=(rows //...]
    pallas_call x1, Pallas kernels: 3.93 us -> 5.04 us  [final(): pl.pallas_call(lambda *refs: final_body(len(kvs), *refs), grid=(1,), in_s...]
    ppermute x6 -> x7, waiting for transfers between devices: 3.54 us -> 3.44 us  [local(): swap_core = lambda a: lax.ppermute(a, 'core', [(0, 1), (1, 0)])]
  transfers between devices with their start and end apart: 23 -> 24, of which waited for: 15 -> 12; matrix products, arithmetic and copies ran while one was open for 1% -> 2% of each run, Pallas kernels for 16% -> 15%
where the time goes in v4:
time: 85.4 us; the launch traced here: 85.1 us
  starting transfers between devices  35.1 us (41%)
  waiting for transfers between devices  27.3 us (32%)
  Pallas kernels  19.3 us (23%)
  local copies, waits for them, and re-layouts  1.79 us (2%)
  other arithmetic  1.21 us (1%)
    ppermute x5, waiting for transfers between devices, local(): swap_y = lambda a: lax.ppermute(a, 'yhi', [(0, 1), (1, 0)])  13.5 us
    ppermute x5, starting transfers between devices, local(): swap_y = lambda a: lax.ppermute(a, 'yhi', [(0, 1), (1, 0)])  9.42 us
    pallas_call x3, Pallas kernels, prefix(): pl.pallas_call(lambda *refs: prefix_body(len(kvs), *refs), grid=(rows //...  9 us
    ppermute x7, starting transfers between devices, local(): swap_core = lambda a: lax.ppermute(a, 'core', [(0, 1), (1, 0)])  8.51 us
    ppermute x2, starting transfers between devices, local(): odd = lambda a: lax.ppermute(a, 'z', O_PAIRS)  7.51 us
    pallas_call x1, Pallas kernels, final(): pl.pallas_call(lambda *refs: final_body(len(kvs), *refs), grid=(1,), in_s...  5.04 us
    ppermute x3, waiting for transfers between devices, local(): x1 = lambda a: lax.ppermute(a, 'x', [(i, i ^ 1) for i in range(4)])  4.21 us
    ppermute x3, starting transfers between devices, local(): x3 = lambda a: lax.ppermute(a, 'x', [(i, i ^ 3) for i in range(4)])  4.19 us
  transfers between devices with their start and end apart: 24, of which 12 were waited for; matrix products, arithmetic and copies ran while one was open for 2% of the time, Pallas kernels for 15%

profile of v4, /device:TPU:1, one launch (start us, length us, event | category | flops | bytes accessed | tf_op | source)
XLA Modules:
  0.0 85.1 jit_solution(3373443866368953855)
XLA Ops:
  0.0 2.5 %collective-permute-start = (bf16[64,128]{1,0:T(8,128)(2,1)}, bf16[64,128]{1,0:T(8,128)(2,1)S(1)}, u32[]{:S(2)}, u32[]{:S(2)}) collective-permute-start(bf16[64,128]{1,0:T(8,128)(2,1)} %k_ref.1), channel_id=1, source_target_pairs={{0,4},{4,0},{8,12},{12,8},{16,20},{20,16},{24,28},{28,24},{1,5},{5... | collective-permute-start | bytes 49160 | tf_op jit(solution)/shard_map/ppermute | solution.py:284
  5.3 4.8 %collective-permute-start.2 = (bf16[128,256]{1,0:T(8,128)(2,1)S(1)}, bf16[128,256]{1,0:T(8,128)(2,1)S(1)}, u32[]{:S(2)}, u32[]{:S(2)}) collective-permute-start(bf16[128,256]{1,0:T(8,128)(2,1)S(1)} %glue.3), channel_id=1, source_target_pairs={{0,28},{4,8},{8,4},{12,16},{16,12},{20,24},{24,20},{28,0},{1,29},{... | collective-permute-start | bytes 196616 | tf_op jit(solution)/shard_map/ppermute | solution.py:285
  10.0 1.7 %collective-permute-done.2._ = bf16[128,256]{1,0:T(8,128)(2,1)S(1)} collective-permute-done((bf16[128,256]{1,0:T(8,128)(2,1)S(1)}, bf16[128,256]{1,0:T(8,128)(2,1)S(1)}, u32[]{:S(2)}, u32[]{:S(2)}) %collective-permute-start.2) | collective-permute-done | bytes 65568 | tf_op jit(solution)/shard_map/ppermute | solution.py:285
  11.7 3.8 %suffix.1 = (bf16[2048,128]{1,0:T(8,128)(2,1)S(1)}, f32[2048,128]{1,0:T(8,128)S(1)}, f32[2048,256]{1,0:T(8,128)S(1)}) custom-call(bf16[64,4,1024]{2,1,0:T(4,128)(2,1)S(1)} %copy-done.2, bf16[256,128]{1,0:T(8,128)(2,1)S(1)} %bitcast.8, bf16[256,128]{1,0:T(8,128)(2,1)S(1)} %bitcast.9, bf16[4096,128]{1,0:T(8,128)(2,1)S(1)} %bitcast.6, ...), custom_call_target="tpu_custom_call" | custom-call | flops 4000000000 | bytes 6000000 | tf_op jit(solution)/shard_map/suffix/pallas_call | solution.py:137
  15.6 2.8 %collective-permute-start.4 = (bf16[128,256]{1,0:T(8,128)(2,1)S(1)}, bf16[128,256]{1,0:T(8,128)(2,1)S(1)}, u32[]{:S(2)}, u32[]{:S(2)}) collective-permute-start(bf16[128,256]{1,0:T(8,128)(2,1)S(1)} %collective-permute-done.3), channel_id=1, source_target_pairs={{0,28},{4,8},{8,4},{12,16},{16,12},{20,24},{24,20},{28,0},{1,29},{... | collective-permute-start | bytes 196616 | tf_op jit(solution)/shard_map/ppermute | solution.py:285
  18.3 1.7 %collective-permute-done.4 = bf16[128,256]{1,0:T(8,128)(2,1)S(1)} collective-permute-done((bf16[128,256]{1,0:T(8,128)(2,1)S(1)}, bf16[128,256]{1,0:T(8,128)(2,1)S(1)}, u32[]{:S(2)}, u32[]{:S(2)}) %collective-permute-start.4) | collective-permute-done | bytes 65568 | tf_op jit(solution)/shard_map/ppermute | solution.py:285
  22.6 1.8 %collective-permute-start.7 = (bf16[512,256]{1,0:T(8,128)(2,1)S(1)}, bf16[512,256]{1,0:T(8,128)(2,1)S(1)}, u32[]{:S(2)}, u32[]{:S(2)}) collective-permute-start(bf16[512,256]{1,0:T(8,128)(2,1)S(1)} %pad_maximum_fusion.refs_3_), channel_id=1, source_target_pairs={{0,96},{32,64},{64,32},{96,0},{1,97},{33,65},{65,33},{97,1},{2,98}... | collective-permute-start | bytes 786440 | tf_op jit(solution)/shard_map/ppermute | solution.py:287
  24.4 1.9 %prefix.3 = (f32[2048,128]{1,0:T(8,128)S(1)}, f32[2048,256]{1,0:T(8,128)S(1)}) custom-call(bf16[2048,128]{1,0:T(8,128)(2,1)S(1)} %get-tuple-element.24.refs_0_, f32[2048,128]{1,0:T(8,128)S(1)} %get-tuple-element.25.refs_1_, f32[2048,256]{1,0:T(8,128)S(1)} %get-tuple-element.26.refs_2_, bf16[512,256]{1,0:T(8,128)(2,1)S(1)} %pad_maximum_fusion.refs_3_), custom_call_target="tpu_custom_call" | custom-call | flops 1073741824 | bytes 7000000 | tf_op jit(solution)/shard_map/prefix/pallas_call | solution.py:188
  26.8 1.6 %collective-permute-start.9 = (bf16[512,256]{1,0:T(8,128)(2,1)S(1)}, bf16[512,256]{1,0:T(8,128)(2,1)S(1)}, u32[]{:S(2)}, u32[]{:S(2)}) collective-permute-start(bf16[512,256]{1,0:T(8,128)(2,1)S(1)} %collective-permute-done.5.refs_3_), channel_id=1, source_target_pairs={{0,96},{32,64},{64,32},{96,0},{1,97},{33,65},{65,33},{97,1},{2,98}... | collective-permute-start | bytes 786440 | tf_op jit(solution)/shard_map/ppermute | solution.py:287
  28.4 2.9 %prefix.4 = (f32[2048,128]{1,0:T(8,128)S(1)}, f32[2048,256]{1,0:T(8,128)S(1)}) custom-call(bf16[2048,128]{1,0:T(8,128)(2,1)S(1)} %get-tuple-element.24.refs_0_, f32[2048,128]{1,0:T(8,128)S(1)} %get-tuple-element.28.refs_1_, f32[2048,256]{1,0:T(8,128)S(1)} %get-tuple-element.29.refs_2_, bf16[512,256]{1,0:T(8,128)(2,1)S(1)} %collective-permute-done.5.refs_3_, ...), custom_call_target="tpu_custom_call" | custom-call | flops 2147483648 | bytes 7000000 | tf_op jit(solution)/shard_map/prefix/pallas_call | solution.py:188
  31.3 3.4 %collective-permute-done.8.refs_4_ = bf16[512,256]{1,0:T(8,128)(2,1)S(1)} collective-permute-done((bf16[512,256]{1,0:T(8,128)(2,1)S(1)}, bf16[512,256]{1,0:T(8,128)(2,1)S(1)}, u32[]{:S(2)}, u32[]{:S(2)}) %collective-permute-start.8) | collective-permute-done | bytes 262176 | tf_op jit(solution)/shard_map/ppermute | solution.py:286
  35.4 4.2 %prefix.5 = (f32[2048,128]{1,0:T(8,128)S(1)}, f32[2048,256]{1,0:T(8,128)S(1)}) custom-call(bf16[2048,128]{1,0:T(8,128)(2,1)S(1)} %get-tuple-element.24.refs_0_, f32[2048,128]{1,0:T(8,128)S(1)} %get-tuple-element.30.refs_1_, f32[2048,256]{1,0:T(8,128)S(1)} %get-tuple-element.31.refs_2_, bf16[512,256]{1,0:T(8,128)(2,1)S(1)} %collective-permute-done.7.refs_3_, ...), custom_call_target="tpu_custom_call" | custom-call | flops 3221225472 | bytes 7000000 | tf_op jit(solution)/shard_map/prefix/pallas_call | solution.py:188
  40.5 1.6 %collective-permute-done.11.refs_4_ = bf16[512,256]{1,0:T(8,128)(2,1)S(1)} collective-permute-done((bf16[512,256]{1,0:T(8,128)(2,1)S(1)}, bf16[512,256]{1,0:T(8,128)(2,1)S(1)}, u32[]{:S(2)}, u32[]{:S(2)}) %collective-permute-start.11) | collective-permute-done | bytes 262176 | tf_op jit(solution)/shard_map/ppermute | solution.py:287
  42.1 5.0 %final.1 = (f32[64,4,2048]{2,1,0:T(4,128)S(1)}, bf16[16,4,2048]{2,1,0:T(4,128)(2,1)S(1)}, bf16[48,4,2048]{2,1,0:T(4,128)(2,1)S(1)}) custom-call(bf16[2048,128]{1,0:T(8,128)(2,1)S(1)} %get-tuple-element.24.refs_0_, f32[2048,128]{1,0:T(8,128)S(1)} %get-tuple-element.33.refs_1_, f32[2048,256]{1,0:T(8,128)S(1)} %get-tuple-element.34.refs_2_, ...), custom_call_target="tpu_custom_call" | custom-call | flops 10737418240 | bytes 12000000 | tf_op jit(solution)/shard_map/final/pallas_call | solution.py:238
  47.1 5.0 %collective-permute-start.14 = (bf16[48,4,2048]{2,1,0:T(4,128)(2,1)S(1)}, bf16[48,4,2048]{2,1,0:T(4,128)(2,1)S(1)}, u32[]{:S(2)}, u32[]{:S(2)}) collective-permute-start(bf16[48,4,2048]{2,1,0:T(4,128)(2,1)S(1)} %get-tuple-element.39), channel_id=1, source_target_pairs={{0,1},{1,0},{2,3},{3,2},{4,5},{5,4},{6,7},{7,6},{8,9},{9,8},{10,11... | collective-permute-start | bytes 2359304 | tf_op jit(solution)/shard_map/ppermute | solution.py:289
  52.2 2.2 %collective-permute-done.12 = bf16[16,4,2048]{2,1,0:T(4,128)(2,1)S(1)} collective-permute-done((bf16[16,4,2048]{2,1,0:T(4,128)(2,1)S(1)}, bf16[16,4,2048]{2,1,0:T(4,128)(2,1)S(1)}, u32[]{:S(2)}, u32[]{:S(2)}) %collective-permute-start.12) | collective-permute-done | bytes 262176 | tf_op jit(solution)/shard_map/ppermute | solution.py:289
  54.6 3.3 %collective-permute-start.13 = (bf16[16,4,2048]{2,1,0:T(4,128)(2,1)S(1)}, bf16[16,4,2048]{2,1,0:T(4,128)(2,1)S(1)}, u32[]{:S(2)}, u32[]{:S(2)}) collective-permute-start(bf16[16,4,2048]{2,1,0:T(4,128)(2,1)S(1)} %add_convert_fusion.1), channel_id=1, source_target_pairs={{0,2},{2,0},{1,3},{3,1},{4,6},{6,4},{5,7},{7,5},{8,10},{10,8},{9,1... | collective-permute-start | bytes 786440 | tf_op jit(solution)/shard_map/ppermute | solution.py:290
  58.7 2.9 %collective-permute-start.16 = (bf16[16,4,2048]{2,1,0:T(4,128)(2,1)S(1)}, bf16[16,4,2048]{2,1,0:T(4,128)(2,1)S(1)}, u32[]{:S(2)}, u32[]{:S(2)}) collective-permute-start(bf16[16,4,2048]{2,1,0:T(4,128)(2,1)S(1)} %get-tuple-element.49), channel_id=1, source_target_pairs={{0,2},{2,0},{1,3},{3,1},{4,6},{6,4},{5,7},{7,5},{8,10},{10,8},{9,1... | collective-permute-start | bytes 786440 | tf_op jit(solution)/shard_map/ppermute | solution.py:290
  61.9 2.9 %collective-permute-start.20 = (bf16[8,4,2048]{2,1,0:T(4,128)(2,1)S(1)}, bf16[8,4,2048]{2,1,0:T(4,128)(2,1)S(1)}, u32[]{:S(2)}, u32[]{:S(2)}) collective-permute-start(bf16[8,4,2048]{2,1,0:T(4,128)(2,1)S(1)} %get-tuple-element.46), channel_id=1, source_target_pairs={{0,2},{2,0},{1,3},{3,1},{4,6},{6,4},{5,7},{7,5},{8,10},{10,8},{9,1... | collective-permute-start | bytes 393224 | tf_op jit(solution)/shard_map/ppermute | solution.py:290
  64.8 5.0 %collective-permute-done.15 = bf16[16,4,2048]{2,1,0:T(4,128)(2,1)S(1)} collective-permute-done((bf16[16,4,2048]{2,1,0:T(4,128)(2,1)S(1)}, bf16[16,4,2048]{2,1,0:T(4,128)(2,1)S(1)}, u32[]{:S(2)}, u32[]{:S(2)}) %collective-permute-start.15) | collective-permute-done | bytes 262176 | tf_op jit(solution)/shard_map/ppermute | solution.py:290
  69.8 5.6 %collective-permute-done.16 = bf16[16,4,2048]{2,1,0:T(4,128)(2,1)S(1)} collective-permute-done((bf16[16,4,2048]{2,1,0:T(4,128)(2,1)S(1)}, bf16[16,4,2048]{2,1,0:T(4,128)(2,1)S(1)}, u32[]{:S(2)}, u32[]{:S(2)}) %collective-permute-start.16) | collective-permute-done | bytes 262176 | tf_op jit(solution)/shard_map/ppermute | solution.py:290
  75.6 1.7 %collective-permute-start.17 = (bf16[16,4,2048]{2,1,0:T(4,128)(2,1)S(1)}, bf16[16,4,2048]{2,1,0:T(4,128)(2,1)S(1)}, u32[]{:S(2)}, u32[]{:S(2)}) collective-permute-start(bf16[16,4,2048]{2,1,0:T(4,128)(2,1)S(1)} %add.23.refs_0_), channel_id=1, source_target_pairs={{0,1},{1,0},{2,3},{3,2},{4,5},{5,4},{6,7},{7,6},{8,9},{9,8},{10,11... | collective-permute-start | bytes 786440 | tf_op jit(solution)/shard_map/ppermute | solution.py:289
  78.3 2.8 %collective-permute-done.20 = bf16[8,4,2048]{2,1,0:T(4,128)(2,1)S(1)} collective-permute-done((bf16[8,4,2048]{2,1,0:T(4,128)(2,1)S(1)}, bf16[8,4,2048]{2,1,0:T(4,128)(2,1)S(1)}, u32[]{:S(2)}, u32[]{:S(2)}) %collective-permute-start.20) | collective-permute-done | bytes 131104 | tf_op jit(solution)/shard_map/ppermute | solution.py:290
  83.6 1.4 %place.1 = bf16[64,4,4096]{2,1,0:T(4,128)(2,1)} custom-call(bf16[16,4,2048]{2,1,0:T(4,128)(2,1)S(1)} %add.23.refs_0_, bf16[16,4,2048]{2,1,0:T(4,128)(2,1)S(1)} %collective-permute-done.17.refs_1_, bf16[16,4,2048]{2,1,0:T(4,128)(2,1)S(1)} %get-tuple-element.48.refs_2_, bf16[16,4,2048]{2,1,0:T(4,128)(2,1)S(1)} %collective-permute-done.18.refs_3_, ...), custom_call_target="tpu_custom_call" | custom-call | tf_op jit(solution)/shard_map/place/pallas_call | solution.py:271
  (61 shorter events, 12.3 us)
Async XLA Ops:
  0.0 4.0 %collective-permute-start = (bf16[64,128]{1,0:T(8,128)(2,1)}, bf16[64,128]{1,0:T(8,128)(2,1)S(1)}, u32[]{:S(2)}, u32[]{:S(2)}) collective-permute-start(bf16[64,128]{1,0:T(8,128)(2,1)} %k_ref.1), channel_id=1, source_target_pairs={{0,4},{4,0},{8,12},{12,8},{16,20},{20,16},{24,28},{28,24},{1,5},{5... | collective-permute-start | bytes 49160 | tf_op jit(solution)/shard_map/ppermute | solution.py:284
  2.5 2.8 %collective-permute-start.1 = (bf16[64,128]{1,0:T(8,128)(2,1)}, bf16[64,128]{1,0:T(8,128)(2,1)S(1)}, u32[]{:S(2)}, u32[]{:S(2)}) collective-permute-start(bf16[64,128]{1,0:T(8,128)(2,1)} %v_ref.1), channel_id=1, source_target_pairs={{0,4},{4,0},{8,12},{12,8},{16,20},{20,16},{24,28},{28,24},{1,5},{5... | collective-permute-start | bytes 49160 | tf_op jit(solution)/shard_map/ppermute | solution.py:284
  5.3 6.4 %collective-permute-start.2 = (bf16[128,256]{1,0:T(8,128)(2,1)S(1)}, bf16[128,256]{1,0:T(8,128)(2,1)S(1)}, u32[]{:S(2)}, u32[]{:S(2)}) collective-permute-start(bf16[128,256]{1,0:T(8,128)(2,1)S(1)} %glue.3), channel_id=1, source_target_pairs={{0,28},{4,8},{8,4},{12,16},{16,12},{20,24},{24,20},{28,0},{1,29},{... | collective-permute-start | bytes 196616 | tf_op jit(solution)/shard_map/ppermute | solution.py:285
  11.7 3.9 %collective-permute-start.3 = (bf16[128,256]{1,0:T(8,128)(2,1)S(1)}, bf16[128,256]{1,0:T(8,128)(2,1)S(1)}, u32[]{:S(2)}, u32[]{:S(2)}) collective-permute-start(bf16[128,256]{1,0:T(8,128)(2,1)S(1)} %collective-permute-done.2._), channel_id=1, source_target_pairs={{0,4},{4,0},{8,12},{12,8},{16,20},{20,16},{24,28},{28,24},{1,5},{5... | collective-permute-start | bytes 196616 | tf_op jit(solution)/shard_map/ppermute | solution.py:284
  15.6 4.4 %collective-permute-start.4 = (bf16[128,256]{1,0:T(8,128)(2,1)S(1)}, bf16[128,256]{1,0:T(8,128)(2,1)S(1)}, u32[]{:S(2)}, u32[]{:S(2)}) collective-permute-start(bf16[128,256]{1,0:T(8,128)(2,1)S(1)} %collective-permute-done.3), channel_id=1, source_target_pairs={{0,28},{4,8},{8,4},{12,16},{16,12},{20,24},{24,20},{28,0},{1,29},{... | collective-permute-start | bytes 196616 | tf_op jit(solution)/shard_map/ppermute | solution.py:285
  20.0 6.3 %collective-permute-start.5 = (bf16[512,256]{1,0:T(8,128)(2,1)S(1)}, bf16[512,256]{1,0:T(8,128)(2,1)S(1)}, u32[]{:S(2)}, u32[]{:S(2)}) collective-permute-start(bf16[512,256]{1,0:T(8,128)(2,1)S(1)} %pad_maximum_fusion.refs_3_), channel_id=1, source_target_pairs={{0,128},{128,0},{1,129},{129,1},{2,130},{130,2},{3,131},{131,3},{4... | collective-permute-start | bytes 786440 | tf_op jit(solution)/shard_map/ppermute | solution.py:288
  21.4 7.0 %collective-permute-start.6 = (bf16[512,256]{1,0:T(8,128)(2,1)S(1)}, bf16[512,256]{1,0:T(8,128)(2,1)S(1)}, u32[]{:S(2)}, u32[]{:S(2)}) collective-permute-start(bf16[512,256]{1,0:T(8,128)(2,1)S(1)} %pad_maximum_fusion.refs_3_), channel_id=1, source_target_pairs={{0,32},{32,0},{64,96},{96,64},{1,33},{33,1},{65,97},{97,65},{2,34}... | collective-permute-start | bytes 786440 | tf_op jit(solution)/shard_map/ppermute | solution.py:286
  22.6 8.7 %collective-permute-start.7 = (bf16[512,256]{1,0:T(8,128)(2,1)S(1)}, bf16[512,256]{1,0:T(8,128)(2,1)S(1)}, u32[]{:S(2)}, u32[]{:S(2)}) collective-permute-start(bf16[512,256]{1,0:T(8,128)(2,1)S(1)} %pad_maximum_fusion.refs_3_), channel_id=1, source_target_pairs={{0,96},{32,64},{64,32},{96,0},{1,97},{33,65},{65,33},{97,1},{2,98}... | collective-permute-start | bytes 786440 | tf_op jit(solution)/shard_map/ppermute | solution.py:287
  26.4 8.3 %collective-permute-start.8 = (bf16[512,256]{1,0:T(8,128)(2,1)S(1)}, bf16[512,256]{1,0:T(8,128)(2,1)S(1)}, u32[]{:S(2)}, u32[]{:S(2)}) collective-permute-start(bf16[512,256]{1,0:T(8,128)(2,1)S(1)} %collective-permute-done.5.refs_3_), channel_id=1, source_target_pairs={{0,32},{32,0},{64,96},{96,64},{1,33},{33,1},{65,97},{97,65},{2,34}... | collective-permute-start | bytes 786440 | tf_op jit(solution)/shard_map/ppermute | solution.py:286
  26.8 8.7 %collective-permute-start.9 = (bf16[512,256]{1,0:T(8,128)(2,1)S(1)}, bf16[512,256]{1,0:T(8,128)(2,1)S(1)}, u32[]{:S(2)}, u32[]{:S(2)}) collective-permute-start(bf16[512,256]{1,0:T(8,128)(2,1)S(1)} %collective-permute-done.5.refs_3_), channel_id=1, source_target_pairs={{0,96},{32,64},{64,32},{96,0},{1,97},{33,65},{65,33},{97,1},{2,98}... | collective-permute-start | bytes 786440 | tf_op jit(solution)/shard_map/ppermute | solution.py:287
  34.7 5.8 %collective-permute-start.10 = (bf16[512,256]{1,0:T(8,128)(2,1)S(1)}, bf16[512,256]{1,0:T(8,128)(2,1)S(1)}, u32[]{:S(2)}, u32[]{:S(2)}) collective-permute-start(bf16[512,256]{1,0:T(8,128)(2,1)S(1)} %collective-permute-done.7.refs_3_), channel_id=1, source_target_pairs={{0,32},{32,0},{64,96},{96,64},{1,33},{33,1},{65,97},{97,65},{2,34}... | collective-permute-start | bytes 786440 | tf_op jit(solution)/shard_map/ppermute | solution.py:286
  34.7 7.4 %collective-permute-start.11 = (bf16[512,256]{1,0:T(8,128)(2,1)S(1)}, bf16[512,256]{1,0:T(8,128)(2,1)S(1)}, u32[]{:S(2)}, u32[]{:S(2)}) collective-permute-start(bf16[512,256]{1,0:T(8,128)(2,1)S(1)} %collective-permute-done.8.refs_4_), channel_id=1, source_target_pairs={{0,96},{32,64},{64,32},{96,0},{1,97},{33,65},{65,33},{97,1},{2,98}... | collective-permute-start | bytes 786440 | tf_op jit(solution)/shard_map/ppermute | solution.py:287
  47.1 10.7 %collective-permute-start.14 = (bf16[48,4,2048]{2,1,0:T(4,128)(2,1)S(1)}, bf16[48,4,2048]{2,1,0:T(4,128)(2,1)S(1)}, u32[]{:S(2)}, u32[]{:S(2)}) collective-permute-start(bf16[48,4,2048]{2,1,0:T(4,128)(2,1)S(1)} %get-tuple-element.39), channel_id=1, source_target_pairs={{0,1},{1,0},{2,3},{3,2},{4,5},{5,4},{6,7},{7,6},{8,9},{9,8},{10,11... | collective-permute-start | bytes 2359304 | tf_op jit(solution)/shard_map/ppermute | solution.py:289
  52.1 2.3 %collective-permute-start.12 = (bf16[16,4,2048]{2,1,0:T(4,128)(2,1)S(1)}, bf16[16,4,2048]{2,1,0:T(4,128)(2,1)S(1)}, u32[]{:S(2)}, u32[]{:S(2)}) collective-permute-start(bf16[16,4,2048]{2,1,0:T(4,128)(2,1)S(1)} %get-tuple-element.38), channel_id=1, source_target_pairs={{0,1},{1,0},{2,3},{3,2},{4,5},{5,4},{6,7},{7,6},{8,9},{9,8},{10,11... | collective-permute-start | bytes 786440 | tf_op jit(solution)/shard_map/ppermute | solution.py:289
  54.6 10.2 %collective-permute-start.13 = (bf16[16,4,2048]{2,1,0:T(4,128)(2,1)S(1)}, bf16[16,4,2048]{2,1,0:T(4,128)(2,1)S(1)}, u32[]{:S(2)}, u32[]{:S(2)}) collective-permute-start(bf16[16,4,2048]{2,1,0:T(4,128)(2,1)S(1)} %add_convert_fusion.1), channel_id=1, source_target_pairs={{0,2},{2,0},{1,3},{3,1},{4,6},{6,4},{5,7},{7,5},{8,10},{10,8},{9,1... | collective-permute-start | bytes 786440 | tf_op jit(solution)/shard_map/ppermute | solution.py:290
  58.6 11.3 %collective-permute-start.15 = (bf16[16,4,2048]{2,1,0:T(4,128)(2,1)S(1)}, bf16[16,4,2048]{2,1,0:T(4,128)(2,1)S(1)}, u32[]{:S(2)}, u32[]{:S(2)}) collective-permute-start(bf16[16,4,2048]{2,1,0:T(4,128)(2,1)S(1)} %get-tuple-element.50), channel_id=1, source_target_pairs={{0,2},{2,0},{1,3},{3,1},{4,6},{6,4},{5,7},{7,5},{8,10},{10,8},{9,1... | collective-permute-start | bytes 786440 | tf_op jit(solution)/shard_map/ppermute | solution.py:290
  58.7 16.8 %collective-permute-start.16 = (bf16[16,4,2048]{2,1,0:T(4,128)(2,1)S(1)}, bf16[16,4,2048]{2,1,0:T(4,128)(2,1)S(1)}, u32[]{:S(2)}, u32[]{:S(2)}) collective-permute-start(bf16[16,4,2048]{2,1,0:T(4,128)(2,1)S(1)} %get-tuple-element.49), channel_id=1, source_target_pairs={{0,2},{2,0},{1,3},{3,1},{4,6},{6,4},{5,7},{7,5},{8,10},{10,8},{9,1... | collective-permute-start | bytes 786440 | tf_op jit(solution)/shard_map/ppermute | solution.py:290
  61.7 16.5 %collective-permute-start.22 = (bf16[8,4,2048]{2,1,0:T(4,128)(2,1)S(1)}, bf16[8,4,2048]{2,1,0:T(4,128)(2,1)S(1)}, u32[]{:S(2)}, u32[]{:S(2)}) collective-permute-start(bf16[8,4,2048]{2,1,0:T(4,128)(2,1)S(1)} %get-tuple-element.45), channel_id=1, source_target_pairs={{0,2},{2,0},{1,3},{3,1},{4,6},{6,4},{5,7},{7,5},{8,10},{10,8},{9,1... | collective-permute-start | bytes 393224 | tf_op jit(solution)/shard_map/ppermute | solution.py:290
  61.9 19.1 %collective-permute-start.20 = (bf16[8,4,2048]{2,1,0:T(4,128)(2,1)S(1)}, bf16[8,4,2048]{2,1,0:T(4,128)(2,1)S(1)}, u32[]{:S(2)}, u32[]{:S(2)}) collective-permute-start(bf16[8,4,2048]{2,1,0:T(4,128)(2,1)S(1)} %get-tuple-element.46), channel_id=1, source_target_pairs={{0,2},{2,0},{1,3},{3,1},{4,6},{6,4},{5,7},{7,5},{8,10},{10,8},{9,1... | collective-permute-start | bytes 393224 | tf_op jit(solution)/shard_map/ppermute | solution.py:290
  75.6 8.0 %collective-permute-start.17 = (bf16[16,4,2048]{2,1,0:T(4,128)(2,1)S(1)}, bf16[16,4,2048]{2,1,0:T(4,128)(2,1)S(1)}, u32[]{:S(2)}, u32[]{:S(2)}) collective-permute-start(bf16[16,4,2048]{2,1,0:T(4,128)(2,1)S(1)} %add.23.refs_0_), channel_id=1, source_target_pairs={{0,1},{1,0},{2,3},{3,2},{4,5},{5,4},{6,7},{7,6},{8,9},{9,8},{10,11... | collective-permute-start | bytes 786440 | tf_op jit(solution)/shard_map/ppermute | solution.py:289
  77.6 6.0 %collective-permute-start.18 = (bf16[16,4,2048]{2,1,0:T(4,128)(2,1)S(1)}, bf16[16,4,2048]{2,1,0:T(4,128)(2,1)S(1)}, u32[]{:S(2)}, u32[]{:S(2)}) collective-permute-start(bf16[16,4,2048]{2,1,0:T(4,128)(2,1)S(1)} %get-tuple-element.48.refs_2_), channel_id=1, source_target_pairs={{0,1},{1,0},{2,3},{3,2},{4,5},{5,4},{6,7},{7,6},{8,9},{9,8},{10,11... | collective-permute-start | bytes 786440 | tf_op jit(solution)/shard_map/ppermute | solution.py:289
  77.7 5.8 %collective-permute-start.19 = (bf16[16,4,2048]{2,1,0:T(4,128)(2,1)S(1)}, bf16[16,4,2048]{2,1,0:T(4,128)(2,1)S(1)}, u32[]{:S(2)}, u32[]{:S(2)}) collective-permute-start(bf16[16,4,2048]{2,1,0:T(4,128)(2,1)S(1)} %get-tuple-element.47.refs_4_), channel_id=1, source_target_pairs={{0,1},{1,0},{2,3},{3,2},{4,5},{5,4},{6,7},{7,6},{8,9},{9,8},{10,11... | collective-permute-start | bytes 786440 | tf_op jit(solution)/shard_map/ppermute | solution.py:289
  81.2 2.0 %collective-permute-start.21 = (bf16[8,4,2048]{2,1,0:T(4,128)(2,1)S(1)}, bf16[8,4,2048]{2,1,0:T(4,128)(2,1)S(1)}, u32[]{:S(2)}, u32[]{:S(2)}) collective-permute-start(bf16[8,4,2048]{2,1,0:T(4,128)(2,1)S(1)} %get-tuple-element.44.refs_6_), channel_id=1, source_target_pairs={{0,1},{1,0},{2,3},{3,2},{4,5},{5,4},{6,7},{7,6},{8,9},{9,8},{10,11... | collective-permute-start | bytes 393224 | tf_op jit(solution)/shard_map/ppermute | solution.py:289
  82.2 1.3 %collective-permute-start.23 = (bf16[8,4,2048]{2,1,0:T(4,128)(2,1)S(1)}, bf16[8,4,2048]{2,1,0:T(4,128)(2,1)S(1)}, u32[]{:S(2)}, u32[]{:S(2)}) collective-permute-start(bf16[8,4,2048]{2,1,0:T(4,128)(2,1)S(1)} %get-tuple-element.43.refs_8_), channel_id=1, source_target_pairs={{0,1},{1,0},{2,3},{3,2},{4,5},{5,4},{6,7},{7,6},{8,9},{9,8},{10,11... | collective-permute-start | bytes 393224 | tf_op jit(solution)/shard_map/ppermute | solution.py:289
  (10 other events, 68.3 us)

commit v5 on v4

--- a/solution.py
+++ b/solution.py
@@ -19,6 +19,7 @@
 
 E_PAIRS = [(i, i ^ 1) for i in range(8)]
 O_PAIRS = [(i, (i + 1) % 8 if i % 2 else (i - 1) % 8) for i in range(8)]
+SKIP_PAIRS = [((i + 2) % 8 if i % 2 else (i - 2) % 8, i) for i in range(8)]
 
 
 def dot_t(a, b):
@@ -198,8 +199,7 @@
 
 
 def final_body(n, *refs):
-    weight_ref, mine_ref, head_ref, tail_ref, heads_ref = refs[3 + n :]
-    low = head_ref.shape[0]
+    weight_ref, mine_ref, other_ref, heads_ref = refs[3 + n :]
 
     def emit(i, rows, _, out):
         heads = (out[:, :HD] / out[:, HD:]).astype(jnp.bfloat16)
@@ -215,30 +215,26 @@
     requests, steps, half = mine_ref.shape
     core = lax.axis_index("core")
     width = 512
-    for side in (1 - core, core):
+    for ref, side in ((other_ref, 1 - core), (mine_ref, core)):
         for j in range(0, half, width):
             columns = pl.ds(pl.multiple_of(side * half + j, width), width)
-            terms = dot(heads, weight_ref[:, columns]).reshape(requests, steps, width)
-            if side is core:
-                mine_ref[:, :, j : j + width] = terms
-            else:
-                terms = terms.astype(head_ref.dtype)
-                head_ref[:, :, j : j + width] = terms[:low]
-                tail_ref[:, :, j : j + width] = terms[low:]
-
-
-def final(q, m, acc, kvs, weight, low):
-    rows = q.shape[0]
+            terms = dot(heads, weight_ref[:, columns])
+            ref[:, :, j : j + width] = terms.reshape(requests, steps, width).astype(ref.dtype)
+
+
+def final(q, m, acc, kvs, weight, part, parts):
+    rows = q.shape[0] // parts
     tokens, half = rows // GROUP, weight.shape[1] // 2
     keys = sum(kv.shape[0] for kv in kvs)
     whole = lambda a: pl.BlockSpec(a.shape, lambda i: (0,) * len(a.shape))
-    requests = tokens // STEPS
-    outs = [jax.ShapeDtypeStruct((requests, STEPS, half), jnp.float32)]
-    outs += [jax.ShapeDtypeStruct((n, STEPS, half), jnp.bfloat16) for n in (low, requests - low)]
+    shape = (tokens // STEPS, STEPS, half)
+    outs = [jax.ShapeDtypeStruct(shape, jnp.float32), jax.ShapeDtypeStruct(shape, jnp.bfloat16)]
     return pl.pallas_call(
         lambda *refs: final_body(len(kvs), *refs),
         grid=(1,),
-        in_specs=[whole(a) for a in (q, m, acc, *kvs)] + [pl.BlockSpec(memory_space=pltpu.VMEM)],
+        in_specs=[pl.BlockSpec((rows, a.shape[1]), lambda i: (part, 0)) for a in (q, m, acc)]
+        + [whole(kv) for kv in kvs]
+        + [pl.BlockSpec(memory_space=pltpu.VMEM)],
         out_specs=[whole(o) for o in outs],
         out_shape=outs,
         scratch_shapes=[pltpu.VMEM((tokens, GROUP * HD), jnp.bfloat16)],
@@ -282,6 +278,7 @@
 def local(queries, prefix_keys, prefix_values, suffix_keys, suffix_values, new_keys, new_values, suffix_lengths, out_weight):
     requests = queries.shape[0]
     even = lambda a: lax.ppermute(a, "z", E_PAIRS)
+    skip = lambda a: lax.ppermute(a, "z", SKIP_PAIRS)
     odd = lambda a: lax.ppermute(a, "z", O_PAIRS)
     x1 = lambda a: lax.ppermute(a, "x", [(i, i ^ 1) for i in range(4)])
     x3 = lambda a: lax.ppermute(a, "x", [(i, i ^ 3) for i in range(4)])
@@ -297,8 +294,7 @@
     pair = glue(join_body, 2 * own.shape[0], 10_000_000_000, own, even(prefix_keys), even(prefix_values))
     r2 = odd(pair)
     q, m, acc = suffix(*args, suffix_lengths, r2)
-    r3 = after(even(r2), m)
-    r4 = odd(r3)
+    r3, r4 = even(r2), after(skip(r2), m)
     line = jnp.concatenate([pair, r2, r3, r4], axis=0)
     b_x1, b_x3, b_y = x1(line), x3(line), y(line)
     m, acc = prefix(q, m, acc, [line])
@@ -309,20 +305,22 @@
     m, acc = prefix(q, m, acc, [b_x3, b_yx1, b_yx3])
 
     shape = (requests, STEPS, out_weight.shape[1])
-    cuts = (0, 16, 32, 48, 56, requests)
-    low = cuts[1]
-    mine, other_head, other_tail = final(q, m, acc, [b_far, b_yfar], out_weight, low)
+    last = [b_far, b_yfar]
+    mine, other = final(q, m, acc, last, out_weight, 0, 2)
+    mine_b, other_b = final(q, m, acc, last, out_weight, 1, 2)
+    got = after(swap_core(other), mine_b)
     combine = lambda mine, got: (mine + got.astype(jnp.float32)).astype(jnp.bfloat16)
-    head = combine(mine[:low], swap_core(other_head))
-    tail = combine(mine[low:], swap_core(other_tail))
-    pieces = [head] + [tail[a - low : b - low] for a, b in zip(cuts[1:], cuts[2:])]
+    cut = lambda a, sizes: [a[sum(sizes[:i]) : sum(sizes[: i + 1])] for i in range(len(sizes))]
+    pieces = cut(combine(mine, got), (16, 16))
+    pieces += cut(combine(mine_b, swap_core(other_b)), (16, 8, 8))
     moved = [swap_y(piece) for piece in pieces]
     moved[:3] = lax.optimization_barrier(moved[:3])
-    halves = []
+    halves, lows = [], [0]
     for piece, got in zip(pieces, moved):
         total = piece + got
         halves += [total, swap_core(total)]
-    return place(halves, cuts[:-1], shape)
+        lows.append(lows[-1] + piece.shape[0])
+    return place(halves, lows[:-1], shape)
 
 
 def solution(mesh):

time: 85.4 us -> 82.9 us (0.971)
  waiting for transfers between devices: 27.3 us -> 21.5 us
  starting transfers between devices: 35.1 us -> 37.8 us
    ppermute x3, starting transfers between devices: 2.5 us -> 6.35 us  [local(): even = lambda a: lax.ppermute(a, 'z', E_PAIRS)]
    ppermute x2 -> x1, starting transfers between devices: 7.51 us -> 4.75 us  [local(): odd = lambda a: lax.ppermute(a, 'z', O_PAIRS)]
    ppermute x7, waiting for transfers between devices: 3.44 us -> 1.26 us  [local(): swap_core = lambda a: lax.ppermute(a, 'core', [(0, 1), (1, 0)])]
    ppermute x2 -> x1, waiting for transfers between devices: 3.31 us -> 1.66 us  [local(): odd = lambda a: lax.ppermute(a, 'z', O_PAIRS)]
    ppermute x3, waiting for transfers between devices: 4.21 us -> 2.99 us  [local(): x1 = lambda a: lax.ppermute(a, 'x', [(i, i ^ 1) for i in range(4)])]
    ppermute x7, starting transfers between devices: 8.51 us -> 9.58 us  [local(): swap_core = lambda a: lax.ppermute(a, 'core', [(0, 1), (1, 0)])]
    pallas_call x1 -> x2, Pallas kernels: 5.04 us -> 5.54 us  [final(): pl.pallas_call(lambda *refs: final_body(len(kvs), *refs), grid=(1,), in_s...]
  transfers between devices with their start and end apart: 24 -> 24, of which waited for: 12 -> 9; matrix products, arithmetic and copies ran while one was open for 2% -> 2% of each run, Pallas kernels for 15% -> 19%
where the time goes in v5:
time: 82.9 us; the launch traced here: 82.6 us
  starting transfers between devices  37.8 us (46%)
  waiting for transfers between devices  21.5 us (26%)
  Pallas kernels  19.8 us (24%)
  local copies, waits for them, and re-layouts  1.9 us (2%)
  other arithmetic  1.2 us (1%)
    ppermute x5, waiting for transfers between devices, local(): swap_y = lambda a: lax.ppermute(a, 'yhi', [(0, 1), (1, 0)])  13 us
    ppermute x7, starting transfers between devices, local(): swap_core = lambda a: lax.ppermute(a, 'core', [(0, 1), (1, 0)])  9.58 us
    pallas_call x3, Pallas kernels, prefix(): pl.pallas_call(lambda *refs: prefix_body(len(kvs), *refs), grid=(rows //...  9 us
    ppermute x5, starting transfers between devices, local(): swap_y = lambda a: lax.ppermute(a, 'yhi', [(0, 1), (1, 0)])  8.88 us
    ppermute x3, starting transfers between devices, local(): even = lambda a: lax.ppermute(a, 'z', E_PAIRS)  6.35 us
    pallas_call x2, Pallas kernels, final(): pl.pallas_call(lambda *refs: final_body(len(kvs), *refs), grid=(1,), in_s...  5.54 us
    ppermute x3, starting transfers between devices, local(): x3 = lambda a: lax.ppermute(a, 'x', [(i, i ^ 3) for i in range(4)])  4.79 us
    ppermute x1, starting transfers between devices, local(): odd = lambda a: lax.ppermute(a, 'z', O_PAIRS)  4.75 us
  transfers between devices with their start and end apart: 24, of which 9 were waited for; matrix products, arithmetic and copies ran while one was open for 2% of the time, Pallas kernels for 19%

profile of v5, /device:TPU:1, one launch (start us, length us, event | category | flops | bytes accessed | tf_op | source)
XLA Modules:
  0.0 82.6 jit_solution(17488438468907105755)
XLA Ops:
  0.0 2.5 %collective-permute-start = (bf16[64,128]{1,0:T(8,128)(2,1)}, bf16[64,128]{1,0:T(8,128)(2,1)S(1)}, u32[]{:S(2)}, u32[]{:S(2)}) collective-permute-start(bf16[64,128]{1,0:T(8,128)(2,1)} %k_ref.1), channel_id=1, source_target_pairs={{0,4},{4,0},{8,12},{12,8},{16,20},{20,16},{24,28},{28,24},{1,5},{5... | collective-permute-start | bytes 49160 | tf_op jit(solution)/shard_map/ppermute | solution.py:280
  5.3 4.8 %collective-permute-start.2 = (bf16[128,256]{1,0:T(8,128)(2,1)S(1)}, bf16[128,256]{1,0:T(8,128)(2,1)S(1)}, u32[]{:S(2)}, u32[]{:S(2)}) collective-permute-start(bf16[128,256]{1,0:T(8,128)(2,1)S(1)} %glue.3), channel_id=1, source_target_pairs={{0,28},{4,8},{8,4},{12,16},{16,12},{20,24},{24,20},{28,0},{1,29},{... | collective-permute-start | bytes 196616 | tf_op jit(solution)/shard_map/ppermute | solution.py:282
  10.0 1.7 %collective-permute-done.2._ = bf16[128,256]{1,0:T(8,128)(2,1)S(1)} collective-permute-done((bf16[128,256]{1,0:T(8,128)(2,1)S(1)}, bf16[128,256]{1,0:T(8,128)(2,1)S(1)}, u32[]{:S(2)}, u32[]{:S(2)}) %collective-permute-start.2) | collective-permute-done | bytes 65568 | tf_op jit(solution)/shard_map/ppermute | solution.py:282
  11.7 3.9 %collective-permute-start.3 = (bf16[128,256]{1,0:T(8,128)(2,1)S(1)}, bf16[128,256]{1,0:T(8,128)(2,1)S(1)}, u32[]{:S(2)}, u32[]{:S(2)}) collective-permute-start(bf16[128,256]{1,0:T(8,128)(2,1)S(1)} %collective-permute-done.2._), channel_id=1, source_target_pairs={{0,4},{4,0},{8,12},{12,8},{16,20},{20,16},{24,28},{28,24},{1,5},{5... | collective-permute-start | bytes 196616 | tf_op jit(solution)/shard_map/ppermute | solution.py:280
  15.6 3.8 %suffix.1 = (bf16[2048,128]{1,0:T(8,128)(2,1)S(1)}, f32[2048,128]{1,0:T(8,128)S(1)}, f32[2048,256]{1,0:T(8,128)S(1)}) custom-call(bf16[64,4,1024]{2,1,0:T(4,128)(2,1)S(1)} %copy-done.2, bf16[256,128]{1,0:T(8,128)(2,1)S(1)} %bitcast.8, bf16[256,128]{1,0:T(8,128)(2,1)S(1)} %bitcast.9, bf16[4096,128]{1,0:T(8,128)(2,1)S(1)} %bitcast.6, ...), custom_call_target="tpu_custom_call" | custom-call | flops 4000000000 | bytes 6000000 | tf_op jit(solution)/shard_map/suffix/pallas_call | solution.py:138
  19.5 1.4 %collective-permute-start.5 = (bf16[512,256]{1,0:T(8,128)(2,1)S(1)}, bf16[512,256]{1,0:T(8,128)(2,1)S(1)}, u32[]{:S(2)}, u32[]{:S(2)}) collective-permute-start(bf16[512,256]{1,0:T(8,128)(2,1)S(1)} %pad_maximum_fusion.refs_3_), channel_id=1, source_target_pairs={{0,128},{128,0},{1,129},{129,1},{2,130},{130,2},{3,131},{131,3},{4... | collective-permute-start | bytes 786440 | tf_op jit(solution)/shard_map/ppermute | solution.py:285
  22.1 1.8 %collective-permute-start.7 = (bf16[512,256]{1,0:T(8,128)(2,1)S(1)}, bf16[512,256]{1,0:T(8,128)(2,1)S(1)}, u32[]{:S(2)}, u32[]{:S(2)}) collective-permute-start(bf16[512,256]{1,0:T(8,128)(2,1)S(1)} %pad_maximum_fusion.refs_3_), channel_id=1, source_target_pairs={{0,96},{32,64},{64,32},{96,0},{1,97},{33,65},{65,33},{97,1},{2,98}... | collective-permute-start | bytes 786440 | tf_op jit(solution)/shard_map/ppermute | solution.py:284
  23.9 1.9 %prefix.3 = (f32[2048,128]{1,0:T(8,128)S(1)}, f32[2048,256]{1,0:T(8,128)S(1)}) custom-call(bf16[2048,128]{1,0:T(8,128)(2,1)S(1)} %get-tuple-element.26.refs_0_, f32[2048,128]{1,0:T(8,128)S(1)} %get-tuple-element.27.refs_1_, f32[2048,256]{1,0:T(8,128)S(1)} %get-tuple-element.28.refs_2_, bf16[512,256]{1,0:T(8,128)(2,1)S(1)} %pad_maximum_fusion.refs_3_), custom_call_target="tpu_custom_call" | custom-call | flops 1073741824 | bytes 7000000 | tf_op jit(solution)/shard_map/prefix/pallas_call | solution.py:189
  26.2 1.6 %collective-permute-start.9 = (bf16[512,256]{1,0:T(8,128)(2,1)S(1)}, bf16[512,256]{1,0:T(8,128)(2,1)S(1)}, u32[]{:S(2)}, u32[]{:S(2)}) collective-permute-start(bf16[512,256]{1,0:T(8,128)(2,1)S(1)} %collective-permute-done.5.refs_3_), channel_id=1, source_target_pairs={{0,96},{32,64},{64,32},{96,0},{1,97},{33,65},{65,33},{97,1},{2,98}... | collective-permute-start | bytes 786440 | tf_op jit(solution)/shard_map/ppermute | solution.py:284
  27.8 2.9 %prefix.4 = (f32[2048,128]{1,0:T(8,128)S(1)}, f32[2048,256]{1,0:T(8,128)S(1)}) custom-call(bf16[2048,128]{1,0:T(8,128)(2,1)S(1)} %get-tuple-element.26.refs_0_, f32[2048,128]{1,0:T(8,128)S(1)} %get-tuple-element.30.refs_1_, f32[2048,256]{1,0:T(8,128)S(1)} %get-tuple-element.31.refs_2_, bf16[512,256]{1,0:T(8,128)(2,1)S(1)} %collective-permute-done.5.refs_3_, ...), custom_call_target="tpu_custom_call" | custom-call | flops 2147483648 | bytes 7000000 | tf_op jit(solution)/shard_map/prefix/pallas_call | solution.py:189
  30.7 3.0 %collective-permute-done.8.refs_4_ = bf16[512,256]{1,0:T(8,128)(2,1)S(1)} collective-permute-done((bf16[512,256]{1,0:T(8,128)(2,1)S(1)}, bf16[512,256]{1,0:T(8,128)(2,1)S(1)}, u32[]{:S(2)}, u32[]{:S(2)}) %collective-permute-start.8) | collective-permute-done | bytes 262176 | tf_op jit(solution)/shard_map/ppermute | solution.py:283
  35.6 4.2 %prefix.5 = (f32[2048,128]{1,0:T(8,128)S(1)}, f32[2048,256]{1,0:T(8,128)S(1)}) custom-call(bf16[2048,128]{1,0:T(8,128)(2,1)S(1)} %get-tuple-element.26.refs_0_, f32[2048,128]{1,0:T(8,128)S(1)} %get-tuple-element.32.refs_1_, f32[2048,256]{1,0:T(8,128)S(1)} %get-tuple-element.33.refs_2_, bf16[512,256]{1,0:T(8,128)(2,1)S(1)} %collective-permute-done.7.refs_3_, ...), custom_call_target="tpu_custom_call" | custom-call | flops 3221225472 | bytes 7000000 | tf_op jit(solution)/shard_map/prefix/pallas_call | solution.py:189
  41.1 2.8 %final.2 = (f32[32,4,2048]{2,1,0:T(4,128)S(1)}, bf16[32,4,2048]{2,1,0:T(4,128)(2,1)S(1)}) custom-call(bf16[2048,128]{1,0:T(8,128)(2,1)S(1)} %get-tuple-element.26.refs_0_, f32[2048,128]{1,0:T(8,128)S(1)} %get-tuple-element.35.refs_1_, f32[2048,256]{1,0:T(8,128)S(1)} %get-tuple-element.36.refs_2_, bf16[512,256]{1,0:T(8,128)(2,1)S(1)} %collective-permute-done.10.refs_3_, ...), custom_call_target="tpu_custom_call" | custom-call | flops 5368709120 | bytes 12000000 | tf_op jit(solution)/shard_map/final/pallas_call | solution.py:232
  43.8 5.0 %collective-permute-start.12 = (bf16[32,4,2048]{2,1,0:T(4,128)(2,1)S(1)}, bf16[32,4,2048]{2,1,0:T(4,128)(2,1)S(1)}, u32[]{:S(2)}, u32[]{:S(2)}) collective-permute-start(bf16[32,4,2048]{2,1,0:T(4,128)(2,1)S(1)} %get-tuple-element.40), channel_id=1, source_target_pairs={{0,1},{1,0},{2,3},{3,2},{4,5},{5,4},{6,7},{7,6},{8,9},{9,8},{10,11... | collective-permute-start | bytes 1572872 | tf_op jit(solution)/shard_map/ppermute | solution.py:286
  48.8 2.8 %final.3 = (f32[32,4,2048]{2,1,0:T(4,128)S(1)}, bf16[32,4,2048]{2,1,0:T(4,128)(2,1)S(1)}) custom-call(bf16[2048,128]{1,0:T(8,128)(2,1)S(1)} %get-tuple-element.26.refs_0_, f32[2048,128]{1,0:T(8,128)S(1)} %get-tuple-element.35.refs_1_, f32[2048,256]{1,0:T(8,128)S(1)} %get-tuple-element.36.refs_2_, bf16[512,256]{1,0:T(8,128)(2,1)S(1)} %collective-permute-done.10.refs_3_, ...), custom_call_target="tpu_custom_call" | custom-call | flops 5368709120 | bytes 12000000 | tf_op jit(solution)/shard_map/final/pallas_call | solution.py:232
  52.3 2.8 %collective-permute-start.13 = (bf16[16,4,2048]{2,1,0:T(4,128)(2,1)S(1)}, bf16[16,4,2048]{2,1,0:T(4,128)(2,1)S(1)}, u32[]{:S(2)}, u32[]{:S(2)}) collective-permute-start(bf16[16,4,2048]{2,1,0:T(4,128)(2,1)S(1)} %get-tuple-element.54), channel_id=1, source_target_pairs={{0,2},{2,0},{1,3},{3,1},{4,6},{6,4},{5,7},{7,5},{8,10},{10,8},{9,1... | collective-permute-start | bytes 786440 | tf_op jit(solution)/shard_map/ppermute | solution.py:287
  55.8 2.8 %collective-permute-start.16 = (bf16[16,4,2048]{2,1,0:T(4,128)(2,1)S(1)}, bf16[16,4,2048]{2,1,0:T(4,128)(2,1)S(1)}, u32[]{:S(2)}, u32[]{:S(2)}) collective-permute-start(bf16[16,4,2048]{2,1,0:T(4,128)(2,1)S(1)} %slice.22), channel_id=1, source_target_pairs={{0,2},{2,0},{1,3},{3,1},{4,6},{6,4},{5,7},{7,5},{8,10},{10,8},{9,1... | collective-permute-start | bytes 786440 | tf_op jit(solution)/shard_map/ppermute | solution.py:287
  59.0 2.7 %collective-permute-start.20 = (bf16[8,4,2048]{2,1,0:T(4,128)(2,1)S(1)}, bf16[8,4,2048]{2,1,0:T(4,128)(2,1)S(1)}, u32[]{:S(2)}, u32[]{:S(2)}) collective-permute-start(bf16[8,4,2048]{2,1,0:T(4,128)(2,1)S(1)} %get-tuple-element.50), channel_id=1, source_target_pairs={{0,2},{2,0},{1,3},{3,1},{4,6},{6,4},{5,7},{7,5},{8,10},{10,8},{9,1... | collective-permute-start | bytes 393224 | tf_op jit(solution)/shard_map/ppermute | solution.py:287
  61.7 5.2 %collective-permute-done.14 = bf16[16,4,2048]{2,1,0:T(4,128)(2,1)S(1)} collective-permute-done((bf16[16,4,2048]{2,1,0:T(4,128)(2,1)S(1)}, bf16[16,4,2048]{2,1,0:T(4,128)(2,1)S(1)}, u32[]{:S(2)}, u32[]{:S(2)}) %collective-permute-start.14) | collective-permute-done | bytes 262176 | tf_op jit(solution)/shard_map/ppermute | solution.py:287
  66.9 5.6 %collective-permute-done.16 = bf16[16,4,2048]{2,1,0:T(4,128)(2,1)S(1)} collective-permute-done((bf16[16,4,2048]{2,1,0:T(4,128)(2,1)S(1)}, bf16[16,4,2048]{2,1,0:T(4,128)(2,1)S(1)}, u32[]{:S(2)}, u32[]{:S(2)}) %collective-permute-start.16) | collective-permute-done | bytes 262176 | tf_op jit(solution)/shard_map/ppermute | solution.py:287
  72.8 2.4 %collective-permute-start.17 = (bf16[16,4,2048]{2,1,0:T(4,128)(2,1)S(1)}, bf16[16,4,2048]{2,1,0:T(4,128)(2,1)S(1)}, u32[]{:S(2)}, u32[]{:S(2)}) collective-permute-start(bf16[16,4,2048]{2,1,0:T(4,128)(2,1)S(1)} %get-tuple-element.52.refs_0_), channel_id=1, source_target_pairs={{0,1},{1,0},{2,3},{3,2},{4,5},{5,4},{6,7},{7,6},{8,9},{9,8},{10,11... | collective-permute-start | bytes 786440 | tf_op jit(solution)/shard_map/ppermute | solution.py:286
  75.9 2.2 %collective-permute-done.20 = bf16[8,4,2048]{2,1,0:T(4,128)(2,1)S(1)} collective-permute-done((bf16[8,4,2048]{2,1,0:T(4,128)(2,1)S(1)}, bf16[8,4,2048]{2,1,0:T(4,128)(2,1)S(1)}, u32[]{:S(2)}, u32[]{:S(2)}) %collective-permute-start.20) | collective-permute-done | bytes 131104 | tf_op jit(solution)/shard_map/ppermute | solution.py:287
  78.3 1.4 %collective-permute-start.21 = (bf16[8,4,2048]{2,1,0:T(4,128)(2,1)S(1)}, bf16[8,4,2048]{2,1,0:T(4,128)(2,1)S(1)}, u32[]{:S(2)}, u32[]{:S(2)}) collective-permute-start(bf16[8,4,2048]{2,1,0:T(4,128)(2,1)S(1)} %get-tuple-element.48.refs_6_), channel_id=1, source_target_pairs={{0,1},{1,0},{2,3},{3,2},{4,5},{5,4},{6,7},{7,6},{8,9},{9,8},{10,11... | collective-permute-start | bytes 393224 | tf_op jit(solution)/shard_map/ppermute | solution.py:286
  81.0 1.4 %place.1 = bf16[64,4,4096]{2,1,0:T(4,128)(2,1)} custom-call(bf16[16,4,2048]{2,1,0:T(4,128)(2,1)S(1)} %get-tuple-element.52.refs_0_, bf16[16,4,2048]{2,1,0:T(4,128)(2,1)S(1)} %collective-permute-done.17.refs_1_, bf16[16,4,2048]{2,1,0:T(4,128)(2,1)S(1)} %get-tuple-element.51.refs_2_, bf16[16,4,2048]{2,1,0:T(4,128)(2,1)S(1)} %collective-permute-done.18.refs_3_, ...), custom_call_target="tpu_custom_call" | custom-call | tf_op jit(solution)/shard_map/place/pallas_call | solution.py:267
  (63 shorter events, 11.9 us)
Async XLA Ops:
  0.0 4.0 %collective-permute-start = (bf16[64,128]{1,0:T(8,128)(2,1)}, bf16[64,128]{1,0:T(8,128)(2,1)S(1)}, u32[]{:S(2)}, u32[]{:S(2)}) collective-permute-start(bf16[64,128]{1,0:T(8,128)(2,1)} %k_ref.1), channel_id=1, source_target_pairs={{0,4},{4,0},{8,12},{12,8},{16,20},{20,16},{24,28},{28,24},{1,5},{5... | collective-permute-start | bytes 49160 | tf_op jit(solution)/shard_map/ppermute | solution.py:280
  2.5 2.8 %collective-permute-start.1 = (bf16[64,128]{1,0:T(8,128)(2,1)}, bf16[64,128]{1,0:T(8,128)(2,1)S(1)}, u32[]{:S(2)}, u32[]{:S(2)}) collective-permute-start(bf16[64,128]{1,0:T(8,128)(2,1)} %v_ref.1), channel_id=1, source_target_pairs={{0,4},{4,0},{8,12},{12,8},{16,20},{20,16},{24,28},{28,24},{1,5},{5... | collective-permute-start | bytes 49160 | tf_op jit(solution)/shard_map/ppermute | solution.py:280
  5.3 6.4 %collective-permute-start.2 = (bf16[128,256]{1,0:T(8,128)(2,1)S(1)}, bf16[128,256]{1,0:T(8,128)(2,1)S(1)}, u32[]{:S(2)}, u32[]{:S(2)}) collective-permute-start(bf16[128,256]{1,0:T(8,128)(2,1)S(1)} %glue.3), channel_id=1, source_target_pairs={{0,28},{4,8},{8,4},{12,16},{16,12},{20,24},{24,20},{28,0},{1,29},{... | collective-permute-start | bytes 196616 | tf_op jit(solution)/shard_map/ppermute | solution.py:282
  11.7 7.7 %collective-permute-start.4 = (bf16[128,256]{1,0:T(8,128)(2,1)S(1)}, bf16[128,256]{1,0:T(8,128)(2,1)S(1)}, u32[]{:S(2)}, u32[]{:S(2)}) collective-permute-start(bf16[128,256]{1,0:T(8,128)(2,1)S(1)} %collective-permute-done.2._), channel_id=1, source_target_pairs={{24,0},{12,4},{0,8},{20,12},{8,16},{28,20},{16,24},{4,28},{25,1},{... | collective-permute-start | bytes 196616 | tf_op jit(solution)/shard_map/ppermute | solution.py:281
  11.7 7.7 %collective-permute-start.3 = (bf16[128,256]{1,0:T(8,128)(2,1)S(1)}, bf16[128,256]{1,0:T(8,128)(2,1)S(1)}, u32[]{:S(2)}, u32[]{:S(2)}) collective-permute-start(bf16[128,256]{1,0:T(8,128)(2,1)S(1)} %collective-permute-done.2._), channel_id=1, source_target_pairs={{0,4},{4,0},{8,12},{12,8},{16,20},{20,16},{24,28},{28,24},{1,5},{5... | collective-permute-start | bytes 196616 | tf_op jit(solution)/shard_map/ppermute | solution.py:280
  19.5 6.3 %collective-permute-start.5 = (bf16[512,256]{1,0:T(8,128)(2,1)S(1)}, bf16[512,256]{1,0:T(8,128)(2,1)S(1)}, u32[]{:S(2)}, u32[]{:S(2)}) collective-permute-start(bf16[512,256]{1,0:T(8,128)(2,1)S(1)} %pad_maximum_fusion.refs_3_), channel_id=1, source_target_pairs={{0,128},{128,0},{1,129},{129,1},{2,130},{130,2},{3,131},{131,3},{4... | collective-permute-start | bytes 786440 | tf_op jit(solution)/shard_map/ppermute | solution.py:285
  20.8 7.0 %collective-permute-start.6 = (bf16[512,256]{1,0:T(8,128)(2,1)S(1)}, bf16[512,256]{1,0:T(8,128)(2,1)S(1)}, u32[]{:S(2)}, u32[]{:S(2)}) collective-permute-start(bf16[512,256]{1,0:T(8,128)(2,1)S(1)} %pad_maximum_fusion.refs_3_), channel_id=1, source_target_pairs={{0,32},{32,0},{64,96},{96,64},{1,33},{33,1},{65,97},{97,65},{2,34}... | collective-permute-start | bytes 786440 | tf_op jit(solution)/shard_map/ppermute | solution.py:283
  22.1 8.7 %collective-permute-start.7 = (bf16[512,256]{1,0:T(8,128)(2,1)S(1)}, bf16[512,256]{1,0:T(8,128)(2,1)S(1)}, u32[]{:S(2)}, u32[]{:S(2)}) collective-permute-start(bf16[512,256]{1,0:T(8,128)(2,1)S(1)} %pad_maximum_fusion.refs_3_), channel_id=1, source_target_pairs={{0,96},{32,64},{64,32},{96,0},{1,97},{33,65},{65,33},{97,1},{2,98}... | collective-permute-start | bytes 786440 | tf_op jit(solution)/shard_map/ppermute | solution.py:284
  25.8 7.9 %collective-permute-start.8 = (bf16[512,256]{1,0:T(8,128)(2,1)S(1)}, bf16[512,256]{1,0:T(8,128)(2,1)S(1)}, u32[]{:S(2)}, u32[]{:S(2)}) collective-permute-start(bf16[512,256]{1,0:T(8,128)(2,1)S(1)} %collective-permute-done.5.refs_3_), channel_id=1, source_target_pairs={{0,32},{32,0},{64,96},{96,64},{1,33},{33,1},{65,97},{97,65},{2,34}... | collective-permute-start | bytes 786440 | tf_op jit(solution)/shard_map/ppermute | solution.py:283
  26.2 9.4 %collective-permute-start.9 = (bf16[512,256]{1,0:T(8,128)(2,1)S(1)}, bf16[512,256]{1,0:T(8,128)(2,1)S(1)}, u32[]{:S(2)}, u32[]{:S(2)}) collective-permute-start(bf16[512,256]{1,0:T(8,128)(2,1)S(1)} %collective-permute-done.5.refs_3_), channel_id=1, source_target_pairs={{0,96},{32,64},{64,32},{96,0},{1,97},{33,65},{65,33},{97,1},{2,98}... | collective-permute-start | bytes 786440 | tf_op jit(solution)/shard_map/ppermute | solution.py:284
  33.7 6.0 %collective-permute-start.10 = (bf16[512,256]{1,0:T(8,128)(2,1)S(1)}, bf16[512,256]{1,0:T(8,128)(2,1)S(1)}, u32[]{:S(2)}, u32[]{:S(2)}) collective-permute-start(bf16[512,256]{1,0:T(8,128)(2,1)S(1)} %collective-permute-done.7.refs_3_), channel_id=1, source_target_pairs={{0,32},{32,0},{64,96},{96,64},{1,33},{33,1},{65,97},{97,65},{2,34}... | collective-permute-start | bytes 786440 | tf_op jit(solution)/shard_map/ppermute | solution.py:283
  34.2 6.9 %collective-permute-start.11 = (bf16[512,256]{1,0:T(8,128)(2,1)S(1)}, bf16[512,256]{1,0:T(8,128)(2,1)S(1)}, u32[]{:S(2)}, u32[]{:S(2)}) collective-permute-start(bf16[512,256]{1,0:T(8,128)(2,1)S(1)} %collective-permute-done.8.refs_4_), channel_id=1, source_target_pairs={{0,96},{32,64},{64,32},{96,0},{1,97},{33,65},{65,33},{97,1},{2,98}... | collective-permute-start | bytes 786440 | tf_op jit(solution)/shard_map/ppermute | solution.py:284
  43.8 7.9 %collective-permute-start.12 = (bf16[32,4,2048]{2,1,0:T(4,128)(2,1)S(1)}, bf16[32,4,2048]{2,1,0:T(4,128)(2,1)S(1)}, u32[]{:S(2)}, u32[]{:S(2)}) collective-permute-start(bf16[32,4,2048]{2,1,0:T(4,128)(2,1)S(1)} %get-tuple-element.40), channel_id=1, source_target_pairs={{0,1},{1,0},{2,3},{3,2},{4,5},{5,4},{6,7},{7,6},{8,9},{9,8},{10,11... | collective-permute-start | bytes 1572872 | tf_op jit(solution)/shard_map/ppermute | solution.py:286
  51.6 3.7 %collective-permute-start.15 = (bf16[32,4,2048]{2,1,0:T(4,128)(2,1)S(1)}, bf16[32,4,2048]{2,1,0:T(4,128)(2,1)S(1)}, u32[]{:S(2)}, u32[]{:S(2)}) collective-permute-start(bf16[32,4,2048]{2,1,0:T(4,128)(2,1)S(1)} %get-tuple-element.43), channel_id=1, source_target_pairs={{0,1},{1,0},{2,3},{3,2},{4,5},{5,4},{6,7},{7,6},{8,9},{9,8},{10,11... | collective-permute-start | bytes 1572872 | tf_op jit(solution)/shard_map/ppermute | solution.py:286
  52.3 9.4 %collective-permute-start.13 = (bf16[16,4,2048]{2,1,0:T(4,128)(2,1)S(1)}, bf16[16,4,2048]{2,1,0:T(4,128)(2,1)S(1)}, u32[]{:S(2)}, u32[]{:S(2)}) collective-permute-start(bf16[16,4,2048]{2,1,0:T(4,128)(2,1)S(1)} %get-tuple-element.54), channel_id=1, source_target_pairs={{0,2},{2,0},{1,3},{3,1},{4,6},{6,4},{5,7},{7,5},{8,10},{10,8},{9,1... | collective-permute-start | bytes 786440 | tf_op jit(solution)/shard_map/ppermute | solution.py:287
  55.0 11.8 %collective-permute-start.14 = (bf16[16,4,2048]{2,1,0:T(4,128)(2,1)S(1)}, bf16[16,4,2048]{2,1,0:T(4,128)(2,1)S(1)}, u32[]{:S(2)}, u32[]{:S(2)}) collective-permute-start(bf16[16,4,2048]{2,1,0:T(4,128)(2,1)S(1)} %get-tuple-element.53), channel_id=1, source_target_pairs={{0,2},{2,0},{1,3},{3,1},{4,6},{6,4},{5,7},{7,5},{8,10},{10,8},{9,1... | collective-permute-start | bytes 786440 | tf_op jit(solution)/shard_map/ppermute | solution.py:287
  55.8 16.7 %collective-permute-start.16 = (bf16[16,4,2048]{2,1,0:T(4,128)(2,1)S(1)}, bf16[16,4,2048]{2,1,0:T(4,128)(2,1)S(1)}, u32[]{:S(2)}, u32[]{:S(2)}) collective-permute-start(bf16[16,4,2048]{2,1,0:T(4,128)(2,1)S(1)} %slice.22), channel_id=1, source_target_pairs={{0,2},{2,0},{1,3},{3,1},{4,6},{6,4},{5,7},{7,5},{8,10},{10,8},{9,1... | collective-permute-start | bytes 786440 | tf_op jit(solution)/shard_map/ppermute | solution.py:287
  58.6 17.2 %collective-permute-start.22 = (bf16[8,4,2048]{2,1,0:T(4,128)(2,1)S(1)}, bf16[8,4,2048]{2,1,0:T(4,128)(2,1)S(1)}, u32[]{:S(2)}, u32[]{:S(2)}) collective-permute-start(bf16[8,4,2048]{2,1,0:T(4,128)(2,1)S(1)} %get-tuple-element.49), channel_id=1, source_target_pairs={{0,2},{2,0},{1,3},{3,1},{4,6},{6,4},{5,7},{7,5},{8,10},{10,8},{9,1... | collective-permute-start | bytes 393224 | tf_op jit(solution)/shard_map/ppermute | solution.py:287
  59.0 19.1 %collective-permute-start.20 = (bf16[8,4,2048]{2,1,0:T(4,128)(2,1)S(1)}, bf16[8,4,2048]{2,1,0:T(4,128)(2,1)S(1)}, u32[]{:S(2)}, u32[]{:S(2)}) collective-permute-start(bf16[8,4,2048]{2,1,0:T(4,128)(2,1)S(1)} %get-tuple-element.50), channel_id=1, source_target_pairs={{0,2},{2,0},{1,3},{3,1},{4,6},{6,4},{5,7},{7,5},{8,10},{10,8},{9,1... | collective-permute-start | bytes 393224 | tf_op jit(solution)/shard_map/ppermute | solution.py:287
  72.8 8.3 %collective-permute-start.17 = (bf16[16,4,2048]{2,1,0:T(4,128)(2,1)S(1)}, bf16[16,4,2048]{2,1,0:T(4,128)(2,1)S(1)}, u32[]{:S(2)}, u32[]{:S(2)}) collective-permute-start(bf16[16,4,2048]{2,1,0:T(4,128)(2,1)S(1)} %get-tuple-element.52.refs_0_), channel_id=1, source_target_pairs={{0,1},{1,0},{2,3},{3,2},{4,5},{5,4},{6,7},{7,6},{8,9},{9,8},{10,11... | collective-permute-start | bytes 786440 | tf_op jit(solution)/shard_map/ppermute | solution.py:286
  75.1 5.9 %collective-permute-start.18 = (bf16[16,4,2048]{2,1,0:T(4,128)(2,1)S(1)}, bf16[16,4,2048]{2,1,0:T(4,128)(2,1)S(1)}, u32[]{:S(2)}, u32[]{:S(2)}) collective-permute-start(bf16[16,4,2048]{2,1,0:T(4,128)(2,1)S(1)} %get-tuple-element.51.refs_2_), channel_id=1, source_target_pairs={{0,1},{1,0},{2,3},{3,2},{4,5},{5,4},{6,7},{7,6},{8,9},{9,8},{10,11... | collective-permute-start | bytes 786440 | tf_op jit(solution)/shard_map/ppermute | solution.py:286
  75.4 5.7 %collective-permute-start.19 = (bf16[16,4,2048]{2,1,0:T(4,128)(2,1)S(1)}, bf16[16,4,2048]{2,1,0:T(4,128)(2,1)S(1)}, u32[]{:S(2)}, u32[]{:S(2)}) collective-permute-start(bf16[16,4,2048]{2,1,0:T(4,128)(2,1)S(1)} %slice_add_fusion.2.refs_4_), channel_id=1, source_target_pairs={{0,1},{1,0},{2,3},{3,2},{4,5},{5,4},{6,7},{7,6},{8,9},{9,8},{10,11... | collective-permute-start | bytes 786440 | tf_op jit(solution)/shard_map/ppermute | solution.py:286
  78.3 2.4 %collective-permute-start.21 = (bf16[8,4,2048]{2,1,0:T(4,128)(2,1)S(1)}, bf16[8,4,2048]{2,1,0:T(4,128)(2,1)S(1)}, u32[]{:S(2)}, u32[]{:S(2)}) collective-permute-start(bf16[8,4,2048]{2,1,0:T(4,128)(2,1)S(1)} %get-tuple-element.48.refs_6_), channel_id=1, source_target_pairs={{0,1},{1,0},{2,3},{3,2},{4,5},{5,4},{6,7},{7,6},{8,9},{9,8},{10,11... | collective-permute-start | bytes 393224 | tf_op jit(solution)/shard_map/ppermute | solution.py:286
  79.7 1.3 %collective-permute-start.23 = (bf16[8,4,2048]{2,1,0:T(4,128)(2,1)S(1)}, bf16[8,4,2048]{2,1,0:T(4,128)(2,1)S(1)}, u32[]{:S(2)}, u32[]{:S(2)}) collective-permute-start(bf16[8,4,2048]{2,1,0:T(4,128)(2,1)S(1)} %get-tuple-element.47.refs_8_), channel_id=1, source_target_pairs={{0,1},{1,0},{2,3},{3,2},{4,5},{5,4},{6,7},{7,6},{8,9},{9,8},{10,11... | collective-permute-start | bytes 393224 | tf_op jit(solution)/shard_map/ppermute | solution.py:286
  (10 other events, 89.7 us)

commit v6 on v5

--- a/solution.py
+++ b/solution.py
@@ -67,16 +67,17 @@
     )(*arrays)
 
 
-def suffix_body(q_ref, nk_ref, nv_ref, sk_all, sv_all, len_ref, _, qp_ref, m_ref, acc_ref, sk_held, sv_held, sem):
+def suffix_body(first, q_ref, nk_ref, nv_ref, sk_all, sv_all, len_ref, *refs):
+    qp_ref, m_ref, acc_ref, sk_held, sv_held, sem = refs[-6:]
     packs = q_ref.shape[0] * STEPS // TOK
-    base = pl.program_id(0) * packs
+    base = (first + pl.program_id(0)) * packs
     per = TOK // STEPS
     keys = per * SLOTS
     now = pl.program_id(0)
     block = packs * keys
 
     def fetch(i):
-        rows = pl.ds(pl.multiple_of(i * block, block), block)
+        rows = pl.ds(pl.multiple_of((first + i) * block, block), block)
         return [
             pltpu.make_async_copy(sk_all.at[rows, :], sk_held.at[i], sem.at[0, i]),
             pltpu.make_async_copy(sv_all.at[rows, :], sv_held.at[i], sem.at[1, i]),
@@ -126,31 +127,34 @@
         acc_ref[rows, :] = dot(p, with_ones(sv_ref[g * keys : (g + 1) * keys, :])) + dot(p_n, with_ones(new_v))
 
 
-def suffix(q, sk, sv, nk, nv, lengths, after):
+def suffix(q, sk, sv, nk, nv, lengths, later, half, state=()):
     rows = q.shape[0] * STEPS * GROUP
-    grid = 4
-    part = lambda a: pl.BlockSpec((a.shape[0] // grid,) + a.shape[1:], lambda i: (i,) + (0,) * (len(a.shape) - 1))
+    grid = 2
+    first = half * grid
+    part = lambda a: pl.BlockSpec((a.shape[0] // (2 * grid),) + a.shape[1:], lambda i: (first + i,) + (0,) * (len(a.shape) - 1))
     outs = [
         jax.ShapeDtypeStruct((rows, HD), jnp.bfloat16),
         jax.ShapeDtypeStruct((rows, HD), jnp.float32),
         jax.ShapeDtypeStruct((rows, 2 * HD), jnp.float32),
     ]
     return pl.pallas_call(
-        suffix_body,
+        lambda *refs: suffix_body(first, *refs),
         grid=(grid,),
         in_specs=[part(a) for a in (q, nk, nv)]
         + [pl.BlockSpec(memory_space=pltpu.HBM)] * 2
-        + [pl.BlockSpec(memory_space=pltpu.SMEM), pl.BlockSpec(memory_space=pl.ANY)],
+        + [pl.BlockSpec(memory_space=pltpu.SMEM)]
+        + [pl.BlockSpec(memory_space=pl.ANY)] * (1 + len(state)),
         out_specs=[part(o) for o in outs],
         out_shape=outs,
-        scratch_shapes=[pltpu.VMEM((grid, sk.shape[0] // grid, HD), jnp.bfloat16)] * 2 + [pltpu.SemaphoreType.DMA((2, grid))],
-        cost_estimate=pl.CostEstimate(flops=4_000_000_000, bytes_accessed=6_000_000, transcendentals=600_000),
+        input_output_aliases={7 + i: i for i in range(len(state))},
+        scratch_shapes=[pltpu.VMEM((grid, sk.shape[0] // (2 * grid), HD), jnp.bfloat16)] * 2 + [pltpu.SemaphoreType.DMA((2, grid))],
+        cost_estimate=pl.CostEstimate(flops=2_000_000_000, bytes_accessed=3_000_000, transcendentals=300_000),
         compiler_params=pltpu.CompilerParams(vmem_limit_bytes=12 * MIB),
         name="suffix",
-    )(q, nk, nv, sk, sv, lengths, after)
-
-
-def attend(q, m, acc, kvs, emit, tile=256):
+    )(q, nk, nv, sk, sv, lengths, later, *state)
+
+
+def attend(q, m, acc, kvs, emit, tile=512):
     tiles = q.shape[0] // tile
     scores = lambda i: [dot_t(q[i * tile : (i + 1) * tile, :], kv[:, :HD]) for kv in kvs]
     ahead = scores(0)
@@ -193,7 +197,7 @@
         out_specs=[part(m), part(acc)],
         out_shape=[jax.ShapeDtypeStruct(m.shape, m.dtype), jax.ShapeDtypeStruct(acc.shape, acc.dtype)],
         cost_estimate=pl.CostEstimate(flops=rows * keys * HD * 8, bytes_accessed=7_000_000, transcendentals=rows * keys),
-        compiler_params=pltpu.CompilerParams(vmem_limit_bytes=16 * MIB),
+        compiler_params=pltpu.CompilerParams(vmem_limit_bytes=24 * MIB),
         name="prefix",
     )(q, m, acc, *kvs)
 
@@ -292,8 +296,9 @@
 
     own = glue(pack_body, prefix_keys.shape[0], 2_000_000_000, prefix_keys, prefix_values)
     pair = glue(join_body, 2 * own.shape[0], 10_000_000_000, own, even(prefix_keys), even(prefix_values))
-    r2 = odd(pair)
-    q, m, acc = suffix(*args, suffix_lengths, r2)
+    state = suffix(*args, suffix_lengths, pair, 0)
+    r2 = after(odd(pair), state[1])
+    q, m, acc = suffix(*args, suffix_lengths, r2, 1, state)
     r3, r4 = even(r2), after(skip(r2), m)
     line = jnp.concatenate([pair, r2, r3, r4], axis=0)
     b_x1, b_x3, b_y = x1(line), x3(line), y(line)
@@ -311,7 +316,9 @@
     got = after(swap_core(other), mine_b)
     combine = lambda mine, got: (mine + got.astype(jnp.float32)).astype(jnp.bfloat16)
     cut = lambda a, sizes: [a[sum(sizes[:i]) : sum(sizes[: i + 1])] for i in range(len(sizes))]
-    pieces = cut(combine(mine, got), (16, 16))
+    low = requests // 4
+    pieces = [combine(mine[:low], got[:low])]
+    pieces += [combine(mine[low:], after(got, pieces[0])[low:])]
     pieces += cut(combine(mine_b, swap_core(other_b)), (16, 8, 8))
     moved = [swap_y(piece) for piece in pieces]
     moved[:3] = lax.optimization_barrier(moved[:3])

time: 82.9 us -> 81.6 us (0.984)
  starting transfers between devices: 37.8 us -> 36.7 us
    ppermute x1, waiting for transfers between devices: 1.66 us -> 0.01 us  [local(): odd = lambda a: lax.ppermute(a, 'z', O_PAIRS)]
    ppermute x3, waiting for transfers between devices: 2.99 us -> 4.44 us  [local(): x1 = lambda a: lax.ppermute(a, 'x', [(i, i ^ 1) for i in range(4)])]
    pallas_call x1 -> x2, Pallas kernels: 3.83 us -> 4.36 us  [suffix(): pl.pallas_call(lambda *refs: suffix_body(first, *refs), grid=(grid,), in_...]
  transfers between devices with their start and end apart: 24 -> 24, of which waited for: 9 -> 10; matrix products, arithmetic and copies ran while one was open for 2% -> 2% of each run, Pallas kernels for 19% -> 19%
where the time goes in v6:
time: 81.6 us; the launch traced here: 81.3 us
  starting transfers between devices  36.7 us (45%)
  waiting for transfers between devices  21.8 us (27%)
  Pallas kernels  19.5 us (24%)
  local copies, waits for them, and re-layouts  1.68 us (2%)
  other arithmetic  1.22 us (1%)
    ppermute x5, waiting for transfers between devices, local(): swap_y = lambda a: lax.ppermute(a, 'yhi', [(0, 1), (1, 0)])  13 us
    ppermute x5, starting transfers between devices, local(): swap_y = lambda a: lax.ppermute(a, 'yhi', [(0, 1), (1, 0)])  9.48 us
    ppermute x7, starting transfers between devices, local(): swap_core = lambda a: lax.ppermute(a, 'core', [(0, 1), (1, 0)])  9.24 us
    pallas_call x3, Pallas kernels, prefix(): pl.pallas_call(lambda *refs: prefix_body(len(kvs), *refs), grid=(rows //...  8.38 us
    ppermute x3, starting transfers between devices, local(): even = lambda a: lax.ppermute(a, 'z', E_PAIRS)  5.68 us
    pallas_call x2, Pallas kernels, final(): pl.pallas_call(lambda *refs: final_body(len(kvs), *refs), grid=(1,), in_s...  5.31 us
    ppermute x1, starting transfers between devices, local(): odd = lambda a: lax.ppermute(a, 'z', O_PAIRS)  4.75 us
    ppermute x3, starting transfers between devices, local(): x3 = lambda a: lax.ppermute(a, 'x', [(i, i ^ 3) for i in range(4)])  4.49 us
  transfers between devices with their start and end apart: 24, of which 10 were waited for; matrix products, arithmetic and copies ran while one was open for 2% of the time, Pallas kernels for 19%

profile of v6, /device:TPU:1, one launch (start us, length us, event | category | flops | bytes accessed | tf_op | source)
XLA Modules:
  0.0 81.3 jit_solution(7344672895123491966)
XLA Ops:
  0.0 2.5 %collective-permute-start = (bf16[64,128]{1,0:T(8,128)(2,1)}, bf16[64,128]{1,0:T(8,128)(2,1)S(1)}, u32[]{:S(2)}, u32[]{:S(2)}) collective-permute-start(bf16[64,128]{1,0:T(8,128)(2,1)} %k_ref.1), channel_id=1, source_target_pairs={{0,4},{4,0},{8,12},{12,8},{16,20},{20,16},{24,28},{28,24},{1,5},{5... | collective-permute-start | bytes 49160 | tf_op jit(solution)/shard_map/ppermute | solution.py:284
  5.3 4.8 %collective-permute-start.2 = (bf16[128,256]{1,0:T(8,128)(2,1)S(1)}, bf16[128,256]{1,0:T(8,128)(2,1)S(1)}, u32[]{:S(2)}, u32[]{:S(2)}) collective-permute-start(bf16[128,256]{1,0:T(8,128)(2,1)S(1)} %glue.3.refs_6_), channel_id=1, source_target_pairs={{0,28},{4,8},{8,4},{12,16},{16,12},{20,24},{24,20},{28,0},{1,29},{... | collective-permute-start | bytes 196616 | tf_op jit(solution)/shard_map/ppermute | solution.py:286
  10.1 2.2 %suffix.2 = (bf16[2048,128]{1,0:T(8,128)(2,1)S(1)}, f32[2048,128]{1,0:T(8,128)S(1)}, f32[2048,256]{1,0:T(8,128)S(1)}) custom-call(bf16[64,4,1024]{2,1,0:T(4,128)(2,1)S(1)} %copy-done.2, bf16[256,128]{1,0:T(8,128)(2,1)S(1)} %bitcast.10, bf16[256,128]{1,0:T(8,128)(2,1)S(1)} %bitcast.12, bf16[4096,128]{1,0:T(8,128)(2,1)S(1)} %bitcast.6, ...), custom_call_target="tpu_custom_call" | custom-call | flops 2000000000 | bytes 3000000 | tf_op jit(solution)/shard_map/suffix/pallas_call | solution.py:140
  12.4 3.2 %collective-permute-start.3 = (bf16[128,256]{1,0:T(8,128)(2,1)S(1)}, bf16[128,256]{1,0:T(8,128)(2,1)S(1)}, u32[]{:S(2)}, u32[]{:S(2)}) collective-permute-start(bf16[128,256]{1,0:T(8,128)(2,1)S(1)} %collective-permute-done.2.refs_6_), channel_id=1, source_target_pairs={{0,4},{4,0},{8,12},{12,8},{16,20},{20,16},{24,28},{28,24},{1,5},{5... | collective-permute-start | bytes 196616 | tf_op jit(solution)/shard_map/ppermute | solution.py:284
  15.5 2.2 %suffix.3 = (bf16[2048,128]{1,0:T(8,128)(2,1)S(1)}, f32[2048,128]{1,0:T(8,128)S(1)}, f32[2048,256]{1,0:T(8,128)S(1)}) custom-call(bf16[64,4,1024]{2,1,0:T(4,128)(2,1)S(1)} %copy-done.2, bf16[256,128]{1,0:T(8,128)(2,1)S(1)} %bitcast.11, bf16[256,128]{1,0:T(8,128)(2,1)S(1)} %bitcast.13, ...), custom_call_target="tpu_custom_call", output_to_operand_aliasing={{0}: (7, {}), {1}: (8, {}), {2}: (9, {})} | custom-call | flops 2000000000 | bytes 3000000 | tf_op jit(solution)/shard_map/suffix/pallas_call | solution.py:140
  17.9 1.4 %collective-permute-start.5 = (bf16[512,256]{1,0:T(8,128)(2,1)S(1)}, bf16[512,256]{1,0:T(8,128)(2,1)S(1)}, u32[]{:S(2)}, u32[]{:S(2)}) collective-permute-start(bf16[512,256]{1,0:T(8,128)(2,1)S(1)} %pad_maximum_fusion.refs_3_), channel_id=1, source_target_pairs={{0,128},{128,0},{1,129},{129,1},{2,130},{130,2},{3,131},{131,3},{4... | collective-permute-start | bytes 786440 | tf_op jit(solution)/shard_map/ppermute | solution.py:289
  20.5 1.8 %collective-permute-start.7 = (bf16[512,256]{1,0:T(8,128)(2,1)S(1)}, bf16[512,256]{1,0:T(8,128)(2,1)S(1)}, u32[]{:S(2)}, u32[]{:S(2)}) collective-permute-start(bf16[512,256]{1,0:T(8,128)(2,1)S(1)} %pad_maximum_fusion.refs_3_), channel_id=1, source_target_pairs={{0,96},{32,64},{64,32},{96,0},{1,97},{33,65},{65,33},{97,1},{2,98}... | collective-permute-start | bytes 786440 | tf_op jit(solution)/shard_map/ppermute | solution.py:288
  22.3 1.8 %prefix.3 = (f32[2048,128]{1,0:T(8,128)S(1)}, f32[2048,256]{1,0:T(8,128)S(1)}) custom-call(bf16[2048,128]{1,0:T(8,128)(2,1)S(1)} %get-tuple-element.35.refs_0_, f32[2048,128]{1,0:T(8,128)S(1)} %get-tuple-element.36.refs_1_, f32[2048,256]{1,0:T(8,128)S(1)} %get-tuple-element.37.refs_2_, bf16[512,256]{1,0:T(8,128)(2,1)S(1)} %pad_maximum_fusion.refs_3_), custom_call_target="tpu_custom_call" | custom-call | flops 1073741824 | bytes 7000000 | tf_op jit(solution)/shard_map/prefix/pallas_call | solution.py:193
  24.6 1.7 %collective-permute-start.9 = (bf16[512,256]{1,0:T(8,128)(2,1)S(1)}, bf16[512,256]{1,0:T(8,128)(2,1)S(1)}, u32[]{:S(2)}, u32[]{:S(2)}) collective-permute-start(bf16[512,256]{1,0:T(8,128)(2,1)S(1)} %collective-permute-done.5.refs_3_), channel_id=1, source_target_pairs={{0,96},{32,64},{64,32},{96,0},{1,97},{33,65},{65,33},{97,1},{2,98}... | collective-permute-start | bytes 786440 | tf_op jit(solution)/shard_map/ppermute | solution.py:288
  26.3 2.7 %prefix.4 = (f32[2048,128]{1,0:T(8,128)S(1)}, f32[2048,256]{1,0:T(8,128)S(1)}) custom-call(bf16[2048,128]{1,0:T(8,128)(2,1)S(1)} %get-tuple-element.35.refs_0_, f32[2048,128]{1,0:T(8,128)S(1)} %get-tuple-element.39.refs_1_, f32[2048,256]{1,0:T(8,128)S(1)} %get-tuple-element.40.refs_2_, bf16[512,256]{1,0:T(8,128)(2,1)S(1)} %collective-permute-done.5.refs_3_, ...), custom_call_target="tpu_custom_call" | custom-call | flops 2147483648 | bytes 7000000 | tf_op jit(solution)/shard_map/prefix/pallas_call | solution.py:193
  29.0 3.4 %collective-permute-done.8.refs_4_ = bf16[512,256]{1,0:T(8,128)(2,1)S(1)} collective-permute-done((bf16[512,256]{1,0:T(8,128)(2,1)S(1)}, bf16[512,256]{1,0:T(8,128)(2,1)S(1)}, u32[]{:S(2)}, u32[]{:S(2)}) %collective-permute-start.8) | collective-permute-done | bytes 262176 | tf_op jit(solution)/shard_map/ppermute | solution.py:287
  33.3 3.9 %prefix.5 = (f32[2048,128]{1,0:T(8,128)S(1)}, f32[2048,256]{1,0:T(8,128)S(1)}) custom-call(bf16[2048,128]{1,0:T(8,128)(2,1)S(1)} %get-tuple-element.35.refs_0_, f32[2048,128]{1,0:T(8,128)S(1)} %get-tuple-element.41.refs_1_, f32[2048,256]{1,0:T(8,128)S(1)} %get-tuple-element.42.refs_2_, bf16[512,256]{1,0:T(8,128)(2,1)S(1)} %collective-permute-done.7.refs_3_, ...), custom_call_target="tpu_custom_call" | custom-call | flops 3221225472 | bytes 7000000 | tf_op jit(solution)/shard_map/prefix/pallas_call | solution.py:193
  38.3 1.7 %collective-permute-done.11.refs_4_ = bf16[512,256]{1,0:T(8,128)(2,1)S(1)} collective-permute-done((bf16[512,256]{1,0:T(8,128)(2,1)S(1)}, bf16[512,256]{1,0:T(8,128)(2,1)S(1)}, u32[]{:S(2)}, u32[]{:S(2)}) %collective-permute-start.11) | collective-permute-done | bytes 262176 | tf_op jit(solution)/shard_map/ppermute | solution.py:288
  40.0 2.7 %final.2 = (f32[32,4,2048]{2,1,0:T(4,128)S(1)}, bf16[32,4,2048]{2,1,0:T(4,128)(2,1)S(1)}) custom-call(bf16[2048,128]{1,0:T(8,128)(2,1)S(1)} %get-tuple-element.35.refs_0_, f32[2048,128]{1,0:T(8,128)S(1)} %get-tuple-element.44.refs_1_, f32[2048,256]{1,0:T(8,128)S(1)} %get-tuple-element.45.refs_2_, bf16[512,256]{1,0:T(8,128)(2,1)S(1)} %collective-permute-done.10.refs_3_, ...), custom_call_target="tpu_custom_call" | custom-call | flops 5368709120 | bytes 12000000 | tf_op jit(solution)/shard_map/final/pallas_call | solution.py:236
  42.6 5.2 %collective-permute-start.12 = (bf16[32,4,2048]{2,1,0:T(4,128)(2,1)S(1)}, bf16[32,4,2048]{2,1,0:T(4,128)(2,1)S(1)}, u32[]{:S(2)}, u32[]{:S(2)}) collective-permute-start(bf16[32,4,2048]{2,1,0:T(4,128)(2,1)S(1)} %get-tuple-element.49), channel_id=1, source_target_pairs={{0,1},{1,0},{2,3},{3,2},{4,5},{5,4},{6,7},{7,6},{8,9},{9,8},{10,11... | collective-permute-start | bytes 1572872 | tf_op jit(solution)/shard_map/ppermute | solution.py:290
  47.8 2.7 %final.3 = (f32[32,4,2048]{2,1,0:T(4,128)S(1)}, bf16[32,4,2048]{2,1,0:T(4,128)(2,1)S(1)}) custom-call(bf16[2048,128]{1,0:T(8,128)(2,1)S(1)} %get-tuple-element.35.refs_0_, f32[2048,128]{1,0:T(8,128)S(1)} %get-tuple-element.44.refs_1_, f32[2048,256]{1,0:T(8,128)S(1)} %get-tuple-element.45.refs_2_, bf16[512,256]{1,0:T(8,128)(2,1)S(1)} %collective-permute-done.10.refs_3_, ...), custom_call_target="tpu_custom_call" | custom-call | flops 5368709120 | bytes 12000000 | tf_op jit(solution)/shard_map/final/pallas_call | solution.py:236
  50.7 3.3 %collective-permute-start.13 = (bf16[16,4,2048]{2,1,0:T(4,128)(2,1)S(1)}, bf16[16,4,2048]{2,1,0:T(4,128)(2,1)S(1)}, u32[]{:S(2)}, u32[]{:S(2)}) collective-permute-start(bf16[16,4,2048]{2,1,0:T(4,128)(2,1)S(1)} %add_convert_fusion.2), channel_id=1, source_target_pairs={{0,2},{2,0},{1,3},{3,1},{4,6},{6,4},{5,7},{7,5},{8,10},{10,8},{9,1... | collective-permute-start | bytes 786440 | tf_op jit(solution)/shard_map/ppermute | solution.py:291
  54.7 3.0 %collective-permute-start.16 = (bf16[16,4,2048]{2,1,0:T(4,128)(2,1)S(1)}, bf16[16,4,2048]{2,1,0:T(4,128)(2,1)S(1)}, u32[]{:S(2)}, u32[]{:S(2)}) collective-permute-start(bf16[16,4,2048]{2,1,0:T(4,128)(2,1)S(1)} %slice.28), channel_id=1, source_target_pairs={{0,2},{2,0},{1,3},{3,1},{4,6},{6,4},{5,7},{7,5},{8,10},{10,8},{9,1... | collective-permute-start | bytes 786440 | tf_op jit(solution)/shard_map/ppermute | solution.py:291
  58.0 2.9 %collective-permute-start.20 = (bf16[8,4,2048]{2,1,0:T(4,128)(2,1)S(1)}, bf16[8,4,2048]{2,1,0:T(4,128)(2,1)S(1)}, u32[]{:S(2)}, u32[]{:S(2)}) collective-permute-start(bf16[8,4,2048]{2,1,0:T(4,128)(2,1)S(1)} %get-tuple-element.60), channel_id=1, source_target_pairs={{0,2},{2,0},{1,3},{3,1},{4,6},{6,4},{5,7},{7,5},{8,10},{10,8},{9,1... | collective-permute-start | bytes 393224 | tf_op jit(solution)/shard_map/ppermute | solution.py:291
  60.9 4.9 %collective-permute-done.14 = bf16[16,4,2048]{2,1,0:T(4,128)(2,1)S(1)} collective-permute-done((bf16[16,4,2048]{2,1,0:T(4,128)(2,1)S(1)}, bf16[16,4,2048]{2,1,0:T(4,128)(2,1)S(1)}, u32[]{:S(2)}, u32[]{:S(2)}) %collective-permute-start.14) | collective-permute-done | bytes 262176 | tf_op jit(solution)/shard_map/ppermute | solution.py:291
  65.9 5.6 %collective-permute-done.16 = bf16[16,4,2048]{2,1,0:T(4,128)(2,1)S(1)} collective-permute-done((bf16[16,4,2048]{2,1,0:T(4,128)(2,1)S(1)}, bf16[16,4,2048]{2,1,0:T(4,128)(2,1)S(1)}, u32[]{:S(2)}, u32[]{:S(2)}) %collective-permute-start.16) | collective-permute-done | bytes 262176 | tf_op jit(solution)/shard_map/ppermute | solution.py:291
  71.6 2.0 %collective-permute-start.17 = (bf16[16,4,2048]{2,1,0:T(4,128)(2,1)S(1)}, bf16[16,4,2048]{2,1,0:T(4,128)(2,1)S(1)}, u32[]{:S(2)}, u32[]{:S(2)}) collective-permute-start(bf16[16,4,2048]{2,1,0:T(4,128)(2,1)S(1)} %add.27.refs_0_), channel_id=1, source_target_pairs={{0,1},{1,0},{2,3},{3,2},{4,5},{5,4},{6,7},{7,6},{8,9},{9,8},{10,11... | collective-permute-start | bytes 786440 | tf_op jit(solution)/shard_map/ppermute | solution.py:290
  74.6 2.4 %collective-permute-done.20 = bf16[8,4,2048]{2,1,0:T(4,128)(2,1)S(1)} collective-permute-done((bf16[8,4,2048]{2,1,0:T(4,128)(2,1)S(1)}, bf16[8,4,2048]{2,1,0:T(4,128)(2,1)S(1)}, u32[]{:S(2)}, u32[]{:S(2)}) %collective-permute-start.20) | collective-permute-done | bytes 131104 | tf_op jit(solution)/shard_map/ppermute | solution.py:291
  79.7 1.4 %place.1 = bf16[64,4,4096]{2,1,0:T(4,128)(2,1)} custom-call(bf16[16,4,2048]{2,1,0:T(4,128)(2,1)S(1)} %add.27.refs_0_, bf16[16,4,2048]{2,1,0:T(4,128)(2,1)S(1)} %collective-permute-done.17.refs_1_, bf16[16,4,2048]{2,1,0:T(4,128)(2,1)S(1)} %add.28.refs_2_, bf16[16,4,2048]{2,1,0:T(4,128)(2,1)S(1)} %collective-permute-done.18.refs_3_, ...), custom_call_target="tpu_custom_call" | custom-call | tf_op jit(solution)/shard_map/place/pallas_call | solution.py:271
  (65 shorter events, 11.6 us)
Async XLA Ops:
  0.0 4.0 %collective-permute-start = (bf16[64,128]{1,0:T(8,128)(2,1)}, bf16[64,128]{1,0:T(8,128)(2,1)S(1)}, u32[]{:S(2)}, u32[]{:S(2)}) collective-permute-start(bf16[64,128]{1,0:T(8,128)(2,1)} %k_ref.1), channel_id=1, source_target_pairs={{0,4},{4,0},{8,12},{12,8},{16,20},{20,16},{24,28},{28,24},{1,5},{5... | collective-permute-start | bytes 49160 | tf_op jit(solution)/shard_map/ppermute | solution.py:284
  2.5 2.8 %collective-permute-start.1 = (bf16[64,128]{1,0:T(8,128)(2,1)}, bf16[64,128]{1,0:T(8,128)(2,1)S(1)}, u32[]{:S(2)}, u32[]{:S(2)}) collective-permute-start(bf16[64,128]{1,0:T(8,128)(2,1)} %v_ref.1), channel_id=1, source_target_pairs={{0,4},{4,0},{8,12},{12,8},{16,20},{20,16},{24,28},{28,24},{1,5},{5... | collective-permute-start | bytes 49160 | tf_op jit(solution)/shard_map/ppermute | solution.py:284
  5.3 7.0 %collective-permute-start.2 = (bf16[128,256]{1,0:T(8,128)(2,1)S(1)}, bf16[128,256]{1,0:T(8,128)(2,1)S(1)}, u32[]{:S(2)}, u32[]{:S(2)}) collective-permute-start(bf16[128,256]{1,0:T(8,128)(2,1)S(1)} %glue.3.refs_6_), channel_id=1, source_target_pairs={{0,28},{4,8},{8,4},{12,16},{16,12},{20,24},{24,20},{28,0},{1,29},{... | collective-permute-start | bytes 196616 | tf_op jit(solution)/shard_map/ppermute | solution.py:286
  12.3 5.5 %collective-permute-start.4 = (bf16[128,256]{1,0:T(8,128)(2,1)S(1)}, bf16[128,256]{1,0:T(8,128)(2,1)S(1)}, u32[]{:S(2)}, u32[]{:S(2)}) collective-permute-start(bf16[128,256]{1,0:T(8,128)(2,1)S(1)} %collective-permute-done.2.refs_6_), channel_id=1, source_target_pairs={{24,0},{12,4},{0,8},{20,12},{8,16},{28,20},{16,24},{4,28},{25,1},{... | collective-permute-start | bytes 196616 | tf_op jit(solution)/shard_map/ppermute | solution.py:285
  12.4 5.5 %collective-permute-start.3 = (bf16[128,256]{1,0:T(8,128)(2,1)S(1)}, bf16[128,256]{1,0:T(8,128)(2,1)S(1)}, u32[]{:S(2)}, u32[]{:S(2)}) collective-permute-start(bf16[128,256]{1,0:T(8,128)(2,1)S(1)} %collective-permute-done.2.refs_6_), channel_id=1, source_target_pairs={{0,4},{4,0},{8,12},{12,8},{16,20},{20,16},{24,28},{28,24},{1,5},{5... | collective-permute-start | bytes 196616 | tf_op jit(solution)/shard_map/ppermute | solution.py:284
  17.9 6.2 %collective-permute-start.5 = (bf16[512,256]{1,0:T(8,128)(2,1)S(1)}, bf16[512,256]{1,0:T(8,128)(2,1)S(1)}, u32[]{:S(2)}, u32[]{:S(2)}) collective-permute-start(bf16[512,256]{1,0:T(8,128)(2,1)S(1)} %pad_maximum_fusion.refs_3_), channel_id=1, source_target_pairs={{0,128},{128,0},{1,129},{129,1},{2,130},{130,2},{3,131},{131,3},{4... | collective-permute-start | bytes 786440 | tf_op jit(solution)/shard_map/ppermute | solution.py:289
  19.3 7.0 %collective-permute-start.6 = (bf16[512,256]{1,0:T(8,128)(2,1)S(1)}, bf16[512,256]{1,0:T(8,128)(2,1)S(1)}, u32[]{:S(2)}, u32[]{:S(2)}) collective-permute-start(bf16[512,256]{1,0:T(8,128)(2,1)S(1)} %pad_maximum_fusion.refs_3_), channel_id=1, source_target_pairs={{0,32},{32,0},{64,96},{96,64},{1,33},{33,1},{65,97},{97,65},{2,34}... | collective-permute-start | bytes 786440 | tf_op jit(solution)/shard_map/ppermute | solution.py:287
  20.5 8.5 %collective-permute-start.7 = (bf16[512,256]{1,0:T(8,128)(2,1)S(1)}, bf16[512,256]{1,0:T(8,128)(2,1)S(1)}, u32[]{:S(2)}, u32[]{:S(2)}) collective-permute-start(bf16[512,256]{1,0:T(8,128)(2,1)S(1)} %pad_maximum_fusion.refs_3_), channel_id=1, source_target_pairs={{0,96},{32,64},{64,32},{96,0},{1,97},{33,65},{65,33},{97,1},{2,98}... | collective-permute-start | bytes 786440 | tf_op jit(solution)/shard_map/ppermute | solution.py:288
  24.2 8.2 %collective-permute-start.8 = (bf16[512,256]{1,0:T(8,128)(2,1)S(1)}, bf16[512,256]{1,0:T(8,128)(2,1)S(1)}, u32[]{:S(2)}, u32[]{:S(2)}) collective-permute-start(bf16[512,256]{1,0:T(8,128)(2,1)S(1)} %collective-permute-done.5.refs_3_), channel_id=1, source_target_pairs={{0,32},{32,0},{64,96},{96,64},{1,33},{33,1},{65,97},{97,65},{2,34}... | collective-permute-start | bytes 786440 | tf_op jit(solution)/shard_map/ppermute | solution.py:287
  24.6 8.8 %collective-permute-start.9 = (bf16[512,256]{1,0:T(8,128)(2,1)S(1)}, bf16[512,256]{1,0:T(8,128)(2,1)S(1)}, u32[]{:S(2)}, u32[]{:S(2)}) collective-permute-start(bf16[512,256]{1,0:T(8,128)(2,1)S(1)} %collective-permute-done.5.refs_3_), channel_id=1, source_target_pairs={{0,96},{32,64},{64,32},{96,0},{1,97},{33,65},{65,33},{97,1},{2,98}... | collective-permute-start | bytes 786440 | tf_op jit(solution)/shard_map/ppermute | solution.py:288
  32.4 5.9 %collective-permute-start.10 = (bf16[512,256]{1,0:T(8,128)(2,1)S(1)}, bf16[512,256]{1,0:T(8,128)(2,1)S(1)}, u32[]{:S(2)}, u32[]{:S(2)}) collective-permute-start(bf16[512,256]{1,0:T(8,128)(2,1)S(1)} %collective-permute-done.7.refs_3_), channel_id=1, source_target_pairs={{0,32},{32,0},{64,96},{96,64},{1,33},{33,1},{65,97},{97,65},{2,34}... | collective-permute-start | bytes 786440 | tf_op jit(solution)/shard_map/ppermute | solution.py:287
  32.4 7.6 %collective-permute-start.11 = (bf16[512,256]{1,0:T(8,128)(2,1)S(1)}, bf16[512,256]{1,0:T(8,128)(2,1)S(1)}, u32[]{:S(2)}, u32[]{:S(2)}) collective-permute-start(bf16[512,256]{1,0:T(8,128)(2,1)S(1)} %collective-permute-done.8.refs_4_), channel_id=1, source_target_pairs={{0,96},{32,64},{64,32},{96,0},{1,97},{33,65},{65,33},{97,1},{2,98}... | collective-permute-start | bytes 786440 | tf_op jit(solution)/shard_map/ppermute | solution.py:288
  42.6 7.9 %collective-permute-start.12 = (bf16[32,4,2048]{2,1,0:T(4,128)(2,1)S(1)}, bf16[32,4,2048]{2,1,0:T(4,128)(2,1)S(1)}, u32[]{:S(2)}, u32[]{:S(2)}) collective-permute-start(bf16[32,4,2048]{2,1,0:T(4,128)(2,1)S(1)} %get-tuple-element.49), channel_id=1, source_target_pairs={{0,1},{1,0},{2,3},{3,2},{4,5},{5,4},{6,7},{7,6},{8,9},{9,8},{10,11... | collective-permute-start | bytes 1572872 | tf_op jit(solution)/shard_map/ppermute | solution.py:290
  50.5 3.8 %collective-permute-start.15 = (bf16[32,4,2048]{2,1,0:T(4,128)(2,1)S(1)}, bf16[32,4,2048]{2,1,0:T(4,128)(2,1)S(1)}, u32[]{:S(2)}, u32[]{:S(2)}) collective-permute-start(bf16[32,4,2048]{2,1,0:T(4,128)(2,1)S(1)} %get-tuple-element.53), channel_id=1, source_target_pairs={{0,1},{1,0},{2,3},{3,2},{4,5},{5,4},{6,7},{7,6},{8,9},{9,8},{10,11... | collective-permute-start | bytes 1572872 | tf_op jit(solution)/shard_map/ppermute | solution.py:290
  50.7 10.2 %collective-permute-start.13 = (bf16[16,4,2048]{2,1,0:T(4,128)(2,1)S(1)}, bf16[16,4,2048]{2,1,0:T(4,128)(2,1)S(1)}, u32[]{:S(2)}, u32[]{:S(2)}) collective-permute-start(bf16[16,4,2048]{2,1,0:T(4,128)(2,1)S(1)} %add_convert_fusion.2), channel_id=1, source_target_pairs={{0,2},{2,0},{1,3},{3,1},{4,6},{6,4},{5,7},{7,5},{8,10},{10,8},{9,1... | collective-permute-start | bytes 786440 | tf_op jit(solution)/shard_map/ppermute | solution.py:291
  54.2 11.7 %collective-permute-start.14 = (bf16[16,4,2048]{2,1,0:T(4,128)(2,1)S(1)}, bf16[16,4,2048]{2,1,0:T(4,128)(2,1)S(1)}, u32[]{:S(2)}, u32[]{:S(2)}) collective-permute-start(bf16[16,4,2048]{2,1,0:T(4,128)(2,1)S(1)} %add_convert_fusion.1), channel_id=1, source_target_pairs={{0,2},{2,0},{1,3},{3,1},{4,6},{6,4},{5,7},{7,5},{8,10},{10,8},{9,1... | collective-permute-start | bytes 786440 | tf_op jit(solution)/shard_map/ppermute | solution.py:291
  54.7 16.7 %collective-permute-start.16 = (bf16[16,4,2048]{2,1,0:T(4,128)(2,1)S(1)}, bf16[16,4,2048]{2,1,0:T(4,128)(2,1)S(1)}, u32[]{:S(2)}, u32[]{:S(2)}) collective-permute-start(bf16[16,4,2048]{2,1,0:T(4,128)(2,1)S(1)} %slice.28), channel_id=1, source_target_pairs={{0,2},{2,0},{1,3},{3,1},{4,6},{6,4},{5,7},{7,5},{8,10},{10,8},{9,1... | collective-permute-start | bytes 786440 | tf_op jit(solution)/shard_map/ppermute | solution.py:291
  57.9 16.8 %collective-permute-start.22 = (bf16[8,4,2048]{2,1,0:T(4,128)(2,1)S(1)}, bf16[8,4,2048]{2,1,0:T(4,128)(2,1)S(1)}, u32[]{:S(2)}, u32[]{:S(2)}) collective-permute-start(bf16[8,4,2048]{2,1,0:T(4,128)(2,1)S(1)} %get-tuple-element.59), channel_id=1, source_target_pairs={{0,2},{2,0},{1,3},{3,1},{4,6},{6,4},{5,7},{7,5},{8,10},{10,8},{9,1... | collective-permute-start | bytes 393224 | tf_op jit(solution)/shard_map/ppermute | solution.py:291
  58.0 19.1 %collective-permute-start.20 = (bf16[8,4,2048]{2,1,0:T(4,128)(2,1)S(1)}, bf16[8,4,2048]{2,1,0:T(4,128)(2,1)S(1)}, u32[]{:S(2)}, u32[]{:S(2)}) collective-permute-start(bf16[8,4,2048]{2,1,0:T(4,128)(2,1)S(1)} %get-tuple-element.60), channel_id=1, source_target_pairs={{0,2},{2,0},{1,3},{3,1},{4,6},{6,4},{5,7},{7,5},{8,10},{10,8},{9,1... | collective-permute-start | bytes 393224 | tf_op jit(solution)/shard_map/ppermute | solution.py:291
  71.6 8.1 %collective-permute-start.17 = (bf16[16,4,2048]{2,1,0:T(4,128)(2,1)S(1)}, bf16[16,4,2048]{2,1,0:T(4,128)(2,1)S(1)}, u32[]{:S(2)}, u32[]{:S(2)}) collective-permute-start(bf16[16,4,2048]{2,1,0:T(4,128)(2,1)S(1)} %add.27.refs_0_), channel_id=1, source_target_pairs={{0,1},{1,0},{2,3},{3,2},{4,5},{5,4},{6,7},{7,6},{8,9},{9,8},{10,11... | collective-permute-start | bytes 786440 | tf_op jit(solution)/shard_map/ppermute | solution.py:290
  73.8 5.9 %collective-permute-start.18 = (bf16[16,4,2048]{2,1,0:T(4,128)(2,1)S(1)}, bf16[16,4,2048]{2,1,0:T(4,128)(2,1)S(1)}, u32[]{:S(2)}, u32[]{:S(2)}) collective-permute-start(bf16[16,4,2048]{2,1,0:T(4,128)(2,1)S(1)} %add.28.refs_2_), channel_id=1, source_target_pairs={{0,1},{1,0},{2,3},{3,2},{4,5},{5,4},{6,7},{7,6},{8,9},{9,8},{10,11... | collective-permute-start | bytes 786440 | tf_op jit(solution)/shard_map/ppermute | solution.py:290
  74.1 5.7 %collective-permute-start.19 = (bf16[16,4,2048]{2,1,0:T(4,128)(2,1)S(1)}, bf16[16,4,2048]{2,1,0:T(4,128)(2,1)S(1)}, u32[]{:S(2)}, u32[]{:S(2)}) collective-permute-start(bf16[16,4,2048]{2,1,0:T(4,128)(2,1)S(1)} %slice_add_fusion.2.refs_4_), channel_id=1, source_target_pairs={{0,1},{1,0},{2,3},{3,2},{4,5},{5,4},{6,7},{7,6},{8,9},{9,8},{10,11... | collective-permute-start | bytes 786440 | tf_op jit(solution)/shard_map/ppermute | solution.py:290
  77.2 2.1 %collective-permute-start.21 = (bf16[8,4,2048]{2,1,0:T(4,128)(2,1)S(1)}, bf16[8,4,2048]{2,1,0:T(4,128)(2,1)S(1)}, u32[]{:S(2)}, u32[]{:S(2)}) collective-permute-start(bf16[8,4,2048]{2,1,0:T(4,128)(2,1)S(1)} %get-tuple-element.58.refs_6_), channel_id=1, source_target_pairs={{0,1},{1,0},{2,3},{3,2},{4,5},{5,4},{6,7},{7,6},{8,9},{9,8},{10,11... | collective-permute-start | bytes 393224 | tf_op jit(solution)/shard_map/ppermute | solution.py:290
  78.4 1.3 %collective-permute-start.23 = (bf16[8,4,2048]{2,1,0:T(4,128)(2,1)S(1)}, bf16[8,4,2048]{2,1,0:T(4,128)(2,1)S(1)}, u32[]{:S(2)}, u32[]{:S(2)}) collective-permute-start(bf16[8,4,2048]{2,1,0:T(4,128)(2,1)S(1)} %get-tuple-element.57.refs_8_), channel_id=1, source_target_pairs={{0,1},{1,0},{2,3},{3,2},{4,5},{5,4},{6,7},{7,6},{8,9},{9,8},{10,11... | collective-permute-start | bytes 393224 | tf_op jit(solution)/shard_map/ppermute | solution.py:290
  (10 other events, 58.2 us)

commit v7 on v6

--- a/solution.py
+++ b/solution.py
@@ -19,7 +19,7 @@
 
 E_PAIRS = [(i, i ^ 1) for i in range(8)]
 O_PAIRS = [(i, (i + 1) % 8 if i % 2 else (i - 1) % 8) for i in range(8)]
-SKIP_PAIRS = [((i + 2) % 8 if i % 2 else (i - 2) % 8, i) for i in range(8)]
+SKIP_PAIRS = [(i, (i - 3) % 8 if i % 2 else (i + 3) % 8) for i in range(8)]
 
 
 def dot_t(a, b):
@@ -319,7 +319,7 @@
     low = requests // 4
     pieces = [combine(mine[:low], got[:low])]
     pieces += [combine(mine[low:], after(got, pieces[0])[low:])]
-    pieces += cut(combine(mine_b, swap_core(other_b)), (16, 8, 8))
+    pieces += cut(combine(mine_b, swap_core(after(other_b, pieces[0]))), (24, 8))
     moved = [swap_y(piece) for piece in pieces]
     moved[:3] = lax.optimization_barrier(moved[:3])
     halves, lows = [], [0]

time: 81.6 us -> 80.7 us (0.989)
  starting transfers between devices: 36.7 us -> 34 us
  waiting for transfers between devices: 21.8 us -> 23.7 us
    ppermute x3, starting transfers between devices: 5.68 us -> 3.43 us  [local(): even = lambda a: lax.ppermute(a, 'z', E_PAIRS)]
    ppermute x1, starting transfers between devices: 0.08 us -> 1.72 us  [local(): skip = lambda a: lax.ppermute(a, 'z', SKIP_PAIRS)]
    ppermute x5 -> x4, waiting for transfers between devices: 13 us -> 14.6 us  [local(): swap_y = lambda a: lax.ppermute(a, 'yhi', [(0, 1), (1, 0)])]
    ppermute x5 -> x4, starting transfers between devices: 9.48 us -> 8.32 us  [local(): swap_y = lambda a: lax.ppermute(a, 'yhi', [(0, 1), (1, 0)])]
    ppermute x7 -> x6, starting transfers between devices: 9.24 us -> 8.27 us  [local(): swap_core = lambda a: lax.ppermute(a, 'core', [(0, 1), (1, 0)])]
    ppermute x1, waiting for transfers between devices: 0.01 us -> 0.88 us  [local(): skip = lambda a: lax.ppermute(a, 'z', SKIP_PAIRS)]
  transfers between devices with their start and end apart: 24 -> 22, of which waited for: 10 -> 8; matrix products, arithmetic and copies ran while one was open for 2% -> 2% of each run, Pallas kernels for 19% -> 19%
where the time goes in v7:
time: 80.7 us; the launch traced here: 80.4 us
  starting transfers between devices  34 us (42%)
  waiting for transfers between devices  23.7 us (29%)
  Pallas kernels  19.4 us (24%)
  local copies, waits for them, and re-layouts  1.68 us (2%)
  other arithmetic  1.21 us (1%)
    ppermute x4, waiting for transfers between devices, local(): swap_y = lambda a: lax.ppermute(a, 'yhi', [(0, 1), (1, 0)])  14.6 us
    pallas_call x3, Pallas kernels, prefix(): pl.pallas_call(lambda *refs: prefix_body(len(kvs), *refs), grid=(rows //...  8.38 us
    ppermute x4, starting transfers between devices, local(): swap_y = lambda a: lax.ppermute(a, 'yhi', [(0, 1), (1, 0)])  8.32 us
    ppermute x6, starting transfers between devices, local(): swap_core = lambda a: lax.ppermute(a, 'core', [(0, 1), (1, 0)])  8.27 us
    pallas_call x2, Pallas kernels, final(): pl.pallas_call(lambda *refs: final_body(len(kvs), *refs), grid=(1,), in_s...  5.31 us
    ppermute x1, starting transfers between devices, local(): odd = lambda a: lax.ppermute(a, 'z', O_PAIRS)  4.75 us
    ppermute x3, starting transfers between devices, local(): x3 = lambda a: lax.ppermute(a, 'x', [(i, i ^ 3) for i in range(4)])  4.5 us
    pallas_call x2, Pallas kernels, suffix(): pl.pallas_call(lambda *refs: suffix_body(first, *refs), grid=(grid,), in_...  4.36 us
  transfers between devices with their start and end apart: 22, of which 8 were waited for; matrix products, arithmetic and copies ran while one was open for 2% of the time, Pallas kernels for 19%

profile of v7, /device:TPU:1, one launch (start us, length us, event | category | flops | bytes accessed | tf_op | source)
XLA Modules:
  0.0 80.4 jit_solution(14165286571279752556)
XLA Ops:
  0.0 2.5 %collective-permute-start = (bf16[64,128]{1,0:T(8,128)(2,1)}, bf16[64,128]{1,0:T(8,128)(2,1)S(1)}, u32[]{:S(2)}, u32[]{:S(2)}) collective-permute-start(bf16[64,128]{1,0:T(8,128)(2,1)} %k_ref.1), channel_id=1, source_target_pairs={{0,4},{4,0},{8,12},{12,8},{16,20},{20,16},{24,28},{28,24},{1,5},{5... | collective-permute-start | bytes 49160 | tf_op jit(solution)/shard_map/ppermute | solution.py:284
  4.0 1.2 %collective-permute-done.1.v_ref = bf16[64,128]{1,0:T(8,128)(2,1)S(1)} collective-permute-done((bf16[64,128]{1,0:T(8,128)(2,1)}, bf16[64,128]{1,0:T(8,128)(2,1)S(1)}, u32[]{:S(2)}, u32[]{:S(2)}) %collective-permute-start.1) | collective-permute-done | bytes 16416 | tf_op jit(solution)/shard_map/ppermute | solution.py:284
  5.3 4.8 %collective-permute-start.2 = (bf16[128,256]{1,0:T(8,128)(2,1)S(1)}, bf16[128,256]{1,0:T(8,128)(2,1)S(1)}, u32[]{:S(2)}, u32[]{:S(2)}) collective-permute-start(bf16[128,256]{1,0:T(8,128)(2,1)S(1)} %glue.3.refs_6_), channel_id=1, source_target_pairs={{0,28},{4,8},{8,4},{12,16},{16,12},{20,24},{24,20},{28,0},{1,29},{... | collective-permute-start | bytes 196616 | tf_op jit(solution)/shard_map/ppermute | solution.py:286
  10.1 2.2 %suffix.2 = (bf16[2048,128]{1,0:T(8,128)(2,1)S(1)}, f32[2048,128]{1,0:T(8,128)S(1)}, f32[2048,256]{1,0:T(8,128)S(1)}) custom-call(bf16[64,4,1024]{2,1,0:T(4,128)(2,1)S(1)} %copy-done.2, bf16[256,128]{1,0:T(8,128)(2,1)S(1)} %bitcast.10, bf16[256,128]{1,0:T(8,128)(2,1)S(1)} %bitcast.12, bf16[4096,128]{1,0:T(8,128)(2,1)S(1)} %bitcast.6, ...), custom_call_target="tpu_custom_call" | custom-call | flops 2000000000 | bytes 3000000 | tf_op jit(solution)/shard_map/suffix/pallas_call | solution.py:140
  12.3 1.7 %collective-permute-start.4 = (bf16[128,256]{1,0:T(8,128)(2,1)S(1)}, bf16[128,256]{1,0:T(8,128)(2,1)S(1)}, u32[]{:S(2)}, u32[]{:S(2)}) collective-permute-start(bf16[128,256]{1,0:T(8,128)(2,1)S(1)} %collective-permute-done.2.refs_6_), channel_id=1, source_target_pairs={{0,12},{4,24},{8,20},{12,0},{16,28},{20,8},{24,4},{28,16},{1,13},{... | collective-permute-start | bytes 196616 | tf_op jit(solution)/shard_map/ppermute | solution.py:285
  14.9 2.2 %suffix.3 = (bf16[2048,128]{1,0:T(8,128)(2,1)S(1)}, f32[2048,128]{1,0:T(8,128)S(1)}, f32[2048,256]{1,0:T(8,128)S(1)}) custom-call(bf16[64,4,1024]{2,1,0:T(4,128)(2,1)S(1)} %copy-done.2, bf16[256,128]{1,0:T(8,128)(2,1)S(1)} %bitcast.11, bf16[256,128]{1,0:T(8,128)(2,1)S(1)} %bitcast.13, ...), custom_call_target="tpu_custom_call", output_to_operand_aliasing={{0}: (7, {}), {1}: (8, {}), {2}: (9, {})} | custom-call | flops 2000000000 | bytes 3000000 | tf_op jit(solution)/shard_map/suffix/pallas_call | solution.py:140
  18.0 1.4 %collective-permute-start.5 = (bf16[512,256]{1,0:T(8,128)(2,1)S(1)}, bf16[512,256]{1,0:T(8,128)(2,1)S(1)}, u32[]{:S(2)}, u32[]{:S(2)}) collective-permute-start(bf16[512,256]{1,0:T(8,128)(2,1)S(1)} %pad_maximum_fusion.refs_3_), channel_id=1, source_target_pairs={{0,128},{128,0},{1,129},{129,1},{2,130},{130,2},{3,131},{131,3},{4... | collective-permute-start | bytes 786440 | tf_op jit(solution)/shard_map/ppermute | solution.py:289
  20.6 1.8 %collective-permute-start.7 = (bf16[512,256]{1,0:T(8,128)(2,1)S(1)}, bf16[512,256]{1,0:T(8,128)(2,1)S(1)}, u32[]{:S(2)}, u32[]{:S(2)}) collective-permute-start(bf16[512,256]{1,0:T(8,128)(2,1)S(1)} %pad_maximum_fusion.refs_3_), channel_id=1, source_target_pairs={{0,96},{32,64},{64,32},{96,0},{1,97},{33,65},{65,33},{97,1},{2,98}... | collective-permute-start | bytes 786440 | tf_op jit(solution)/shard_map/ppermute | solution.py:288
  22.4 1.8 %prefix.3 = (f32[2048,128]{1,0:T(8,128)S(1)}, f32[2048,256]{1,0:T(8,128)S(1)}) custom-call(bf16[2048,128]{1,0:T(8,128)(2,1)S(1)} %get-tuple-element.36.refs_0_, f32[2048,128]{1,0:T(8,128)S(1)} %get-tuple-element.37.refs_1_, f32[2048,256]{1,0:T(8,128)S(1)} %get-tuple-element.38.refs_2_, bf16[512,256]{1,0:T(8,128)(2,1)S(1)} %pad_maximum_fusion.refs_3_), custom_call_target="tpu_custom_call" | custom-call | flops 1073741824 | bytes 7000000 | tf_op jit(solution)/shard_map/prefix/pallas_call | solution.py:193
  24.6 1.7 %collective-permute-start.9 = (bf16[512,256]{1,0:T(8,128)(2,1)S(1)}, bf16[512,256]{1,0:T(8,128)(2,1)S(1)}, u32[]{:S(2)}, u32[]{:S(2)}) collective-permute-start(bf16[512,256]{1,0:T(8,128)(2,1)S(1)} %collective-permute-done.5.refs_3_), channel_id=1, source_target_pairs={{0,96},{32,64},{64,32},{96,0},{1,97},{33,65},{65,33},{97,1},{2,98}... | collective-permute-start | bytes 786440 | tf_op jit(solution)/shard_map/ppermute | solution.py:288
  26.3 2.7 %prefix.4 = (f32[2048,128]{1,0:T(8,128)S(1)}, f32[2048,256]{1,0:T(8,128)S(1)}) custom-call(bf16[2048,128]{1,0:T(8,128)(2,1)S(1)} %get-tuple-element.36.refs_0_, f32[2048,128]{1,0:T(8,128)S(1)} %get-tuple-element.40.refs_1_, f32[2048,256]{1,0:T(8,128)S(1)} %get-tuple-element.41.refs_2_, bf16[512,256]{1,0:T(8,128)(2,1)S(1)} %collective-permute-done.5.refs_3_, ...), custom_call_target="tpu_custom_call" | custom-call | flops 2147483648 | bytes 7000000 | tf_op jit(solution)/shard_map/prefix/pallas_call | solution.py:193
  29.1 3.6 %collective-permute-done.8.refs_4_ = bf16[512,256]{1,0:T(8,128)(2,1)S(1)} collective-permute-done((bf16[512,256]{1,0:T(8,128)(2,1)S(1)}, bf16[512,256]{1,0:T(8,128)(2,1)S(1)}, u32[]{:S(2)}, u32[]{:S(2)}) %collective-permute-start.8) | collective-permute-done | bytes 262176 | tf_op jit(solution)/shard_map/ppermute | solution.py:287
  33.6 3.9 %prefix.5 = (f32[2048,128]{1,0:T(8,128)S(1)}, f32[2048,256]{1,0:T(8,128)S(1)}) custom-call(bf16[2048,128]{1,0:T(8,128)(2,1)S(1)} %get-tuple-element.36.refs_0_, f32[2048,128]{1,0:T(8,128)S(1)} %get-tuple-element.42.refs_1_, f32[2048,256]{1,0:T(8,128)S(1)} %get-tuple-element.43.refs_2_, bf16[512,256]{1,0:T(8,128)(2,1)S(1)} %collective-permute-done.7.refs_3_, ...), custom_call_target="tpu_custom_call" | custom-call | flops 3221225472 | bytes 7000000 | tf_op jit(solution)/shard_map/prefix/pallas_call | solution.py:193
  38.1 1.8 %collective-permute-done.11.refs_4_ = bf16[512,256]{1,0:T(8,128)(2,1)S(1)} collective-permute-done((bf16[512,256]{1,0:T(8,128)(2,1)S(1)}, bf16[512,256]{1,0:T(8,128)(2,1)S(1)}, u32[]{:S(2)}, u32[]{:S(2)}) %collective-permute-start.11) | collective-permute-done | bytes 262176 | tf_op jit(solution)/shard_map/ppermute | solution.py:288
  39.9 2.7 %final.2 = (f32[32,4,2048]{2,1,0:T(4,128)S(1)}, bf16[32,4,2048]{2,1,0:T(4,128)(2,1)S(1)}) custom-call(bf16[2048,128]{1,0:T(8,128)(2,1)S(1)} %get-tuple-element.36.refs_0_, f32[2048,128]{1,0:T(8,128)S(1)} %get-tuple-element.45.refs_1_, f32[2048,256]{1,0:T(8,128)S(1)} %get-tuple-element.46.refs_2_, bf16[512,256]{1,0:T(8,128)(2,1)S(1)} %collective-permute-done.10.refs_3_, ...), custom_call_target="tpu_custom_call" | custom-call | flops 5368709120 | bytes 12000000 | tf_op jit(solution)/shard_map/final/pallas_call | solution.py:236
  42.6 4.8 %collective-permute-start.12 = (bf16[32,4,2048]{2,1,0:T(4,128)(2,1)S(1)}, bf16[32,4,2048]{2,1,0:T(4,128)(2,1)S(1)}, u32[]{:S(2)}, u32[]{:S(2)}) collective-permute-start(bf16[32,4,2048]{2,1,0:T(4,128)(2,1)S(1)} %get-tuple-element.50), channel_id=1, source_target_pairs={{0,1},{1,0},{2,3},{3,2},{4,5},{5,4},{6,7},{7,6},{8,9},{9,8},{10,11... | collective-permute-start | bytes 1572872 | tf_op jit(solution)/shard_map/ppermute | solution.py:290
  47.4 2.7 %final.3 = (f32[32,4,2048]{2,1,0:T(4,128)S(1)}, bf16[32,4,2048]{2,1,0:T(4,128)(2,1)S(1)}) custom-call(bf16[2048,128]{1,0:T(8,128)(2,1)S(1)} %get-tuple-element.36.refs_0_, f32[2048,128]{1,0:T(8,128)S(1)} %get-tuple-element.45.refs_1_, f32[2048,256]{1,0:T(8,128)S(1)} %get-tuple-element.46.refs_2_, bf16[512,256]{1,0:T(8,128)(2,1)S(1)} %collective-permute-done.10.refs_3_, ...), custom_call_target="tpu_custom_call" | custom-call | flops 5368709120 | bytes 12000000 | tf_op jit(solution)/shard_map/final/pallas_call | solution.py:236
  50.3 3.3 %collective-permute-start.13 = (bf16[16,4,2048]{2,1,0:T(4,128)(2,1)S(1)}, bf16[16,4,2048]{2,1,0:T(4,128)(2,1)S(1)}, u32[]{:S(2)}, u32[]{:S(2)}) collective-permute-start(bf16[16,4,2048]{2,1,0:T(4,128)(2,1)S(1)} %add_convert_fusion.2), channel_id=1, source_target_pairs={{0,2},{2,0},{1,3},{3,1},{4,6},{6,4},{5,7},{7,5},{8,10},{10,8},{9,1... | collective-permute-start | bytes 786440 | tf_op jit(solution)/shard_map/ppermute | solution.py:291
  54.1 1.9 %collective-permute-start.16 = (bf16[24,4,2048]{2,1,0:T(4,128)(2,1)S(1)}, bf16[24,4,2048]{2,1,0:T(4,128)(2,1)S(1)}, u32[]{:S(2)}, u32[]{:S(2)}) collective-permute-start(bf16[24,4,2048]{2,1,0:T(4,128)(2,1)S(1)} %slice.24), channel_id=1, source_target_pairs={{0,2},{2,0},{1,3},{3,1},{4,6},{6,4},{5,7},{7,5},{8,10},{10,8},{9,1... | collective-permute-start | bytes 1179656 | tf_op jit(solution)/shard_map/ppermute | solution.py:291
  56.1 1.2 %collective-permute-start.14 = (bf16[16,4,2048]{2,1,0:T(4,128)(2,1)S(1)}, bf16[16,4,2048]{2,1,0:T(4,128)(2,1)S(1)}, u32[]{:S(2)}, u32[]{:S(2)}) collective-permute-start(bf16[16,4,2048]{2,1,0:T(4,128)(2,1)S(1)} %add_convert_fusion.1), channel_id=1, source_target_pairs={{0,2},{2,0},{1,3},{3,1},{4,6},{6,4},{5,7},{7,5},{8,10},{10,8},{9,1... | collective-permute-start | bytes 786440 | tf_op jit(solution)/shard_map/ppermute | solution.py:291
  57.4 1.9 %collective-permute-start.20 = (bf16[8,4,2048]{2,1,0:T(4,128)(2,1)S(1)}, bf16[8,4,2048]{2,1,0:T(4,128)(2,1)S(1)}, u32[]{:S(2)}, u32[]{:S(2)}) collective-permute-start(bf16[8,4,2048]{2,1,0:T(4,128)(2,1)S(1)} %slice.25), channel_id=1, source_target_pairs={{0,2},{2,0},{1,3},{3,1},{4,6},{6,4},{5,7},{7,5},{8,10},{10,8},{9,1... | collective-permute-start | bytes 393224 | tf_op jit(solution)/shard_map/ppermute | solution.py:291
  59.9 14.0 %collective-permute-done.14 = bf16[16,4,2048]{2,1,0:T(4,128)(2,1)S(1)} collective-permute-done((bf16[16,4,2048]{2,1,0:T(4,128)(2,1)S(1)}, bf16[16,4,2048]{2,1,0:T(4,128)(2,1)S(1)}, u32[]{:S(2)}, u32[]{:S(2)}) %collective-permute-start.14) | collective-permute-done | bytes 262176 | tf_op jit(solution)/shard_map/ppermute | solution.py:291
  74.1 1.6 %collective-permute-start.17 = (bf16[16,4,2048]{2,1,0:T(4,128)(2,1)S(1)}, bf16[16,4,2048]{2,1,0:T(4,128)(2,1)S(1)}, u32[]{:S(2)}, u32[]{:S(2)}) collective-permute-start(bf16[16,4,2048]{2,1,0:T(4,128)(2,1)S(1)} %add.24.refs_0_), channel_id=1, source_target_pairs={{0,1},{1,0},{2,3},{3,2},{4,5},{5,4},{6,7},{7,6},{8,9},{9,8},{10,11... | collective-permute-start | bytes 786440 | tf_op jit(solution)/shard_map/ppermute | solution.py:290
  78.9 1.4 %place.1 = bf16[64,4,4096]{2,1,0:T(4,128)(2,1)} custom-call(bf16[16,4,2048]{2,1,0:T(4,128)(2,1)S(1)} %add.24.refs_0_, bf16[16,4,2048]{2,1,0:T(4,128)(2,1)S(1)} %collective-permute-done.17.refs_1_, bf16[16,4,2048]{2,1,0:T(4,128)(2,1)S(1)} %add.25.refs_2_, bf16[16,4,2048]{2,1,0:T(4,128)(2,1)S(1)} %collective-permute-done.18.refs_3_, ...), custom_call_target="tpu_custom_call" | custom-call | tf_op jit(solution)/shard_map/place/pallas_call | solution.py:271
  (61 shorter events, 11.4 us)
Async XLA Ops:
  0.0 4.0 %collective-permute-start = (bf16[64,128]{1,0:T(8,128)(2,1)}, bf16[64,128]{1,0:T(8,128)(2,1)S(1)}, u32[]{:S(2)}, u32[]{:S(2)}) collective-permute-start(bf16[64,128]{1,0:T(8,128)(2,1)} %k_ref.1), channel_id=1, source_target_pairs={{0,4},{4,0},{8,12},{12,8},{16,20},{20,16},{24,28},{28,24},{1,5},{5... | collective-permute-start | bytes 49160 | tf_op jit(solution)/shard_map/ppermute | solution.py:284
  2.5 2.8 %collective-permute-start.1 = (bf16[64,128]{1,0:T(8,128)(2,1)}, bf16[64,128]{1,0:T(8,128)(2,1)S(1)}, u32[]{:S(2)}, u32[]{:S(2)}) collective-permute-start(bf16[64,128]{1,0:T(8,128)(2,1)} %v_ref.1), channel_id=1, source_target_pairs={{0,4},{4,0},{8,12},{12,8},{16,20},{20,16},{24,28},{28,24},{1,5},{5... | collective-permute-start | bytes 49160 | tf_op jit(solution)/shard_map/ppermute | solution.py:284
  5.3 7.0 %collective-permute-start.2 = (bf16[128,256]{1,0:T(8,128)(2,1)S(1)}, bf16[128,256]{1,0:T(8,128)(2,1)S(1)}, u32[]{:S(2)}, u32[]{:S(2)}) collective-permute-start(bf16[128,256]{1,0:T(8,128)(2,1)S(1)} %glue.3.refs_6_), channel_id=1, source_target_pairs={{0,28},{4,8},{8,4},{12,16},{16,12},{20,24},{24,20},{28,0},{1,29},{... | collective-permute-start | bytes 196616 | tf_op jit(solution)/shard_map/ppermute | solution.py:286
  12.3 5.7 %collective-permute-start.4 = (bf16[128,256]{1,0:T(8,128)(2,1)S(1)}, bf16[128,256]{1,0:T(8,128)(2,1)S(1)}, u32[]{:S(2)}, u32[]{:S(2)}) collective-permute-start(bf16[128,256]{1,0:T(8,128)(2,1)S(1)} %collective-permute-done.2.refs_6_), channel_id=1, source_target_pairs={{0,12},{4,24},{8,20},{12,0},{16,28},{20,8},{24,4},{28,16},{1,13},{... | collective-permute-start | bytes 196616 | tf_op jit(solution)/shard_map/ppermute | solution.py:285
  14.0 4.0 %collective-permute-start.3 = (bf16[128,256]{1,0:T(8,128)(2,1)S(1)}, bf16[128,256]{1,0:T(8,128)(2,1)S(1)}, u32[]{:S(2)}, u32[]{:S(2)}) collective-permute-start(bf16[128,256]{1,0:T(8,128)(2,1)S(1)} %collective-permute-done.2.refs_6_), channel_id=1, source_target_pairs={{0,4},{4,0},{8,12},{12,8},{16,20},{20,16},{24,28},{28,24},{1,5},{5... | collective-permute-start | bytes 196616 | tf_op jit(solution)/shard_map/ppermute | solution.py:284
  18.0 6.2 %collective-permute-start.5 = (bf16[512,256]{1,0:T(8,128)(2,1)S(1)}, bf16[512,256]{1,0:T(8,128)(2,1)S(1)}, u32[]{:S(2)}, u32[]{:S(2)}) collective-permute-start(bf16[512,256]{1,0:T(8,128)(2,1)S(1)} %pad_maximum_fusion.refs_3_), channel_id=1, source_target_pairs={{0,128},{128,0},{1,129},{129,1},{2,130},{130,2},{3,131},{131,3},{4... | collective-permute-start | bytes 786440 | tf_op jit(solution)/shard_map/ppermute | solution.py:289
  19.4 7.0 %collective-permute-start.6 = (bf16[512,256]{1,0:T(8,128)(2,1)S(1)}, bf16[512,256]{1,0:T(8,128)(2,1)S(1)}, u32[]{:S(2)}, u32[]{:S(2)}) collective-permute-start(bf16[512,256]{1,0:T(8,128)(2,1)S(1)} %pad_maximum_fusion.refs_3_), channel_id=1, source_target_pairs={{0,32},{32,0},{64,96},{96,64},{1,33},{33,1},{65,97},{97,65},{2,34}... | collective-permute-start | bytes 786440 | tf_op jit(solution)/shard_map/ppermute | solution.py:287
  20.6 8.5 %collective-permute-start.7 = (bf16[512,256]{1,0:T(8,128)(2,1)S(1)}, bf16[512,256]{1,0:T(8,128)(2,1)S(1)}, u32[]{:S(2)}, u32[]{:S(2)}) collective-permute-start(bf16[512,256]{1,0:T(8,128)(2,1)S(1)} %pad_maximum_fusion.refs_3_), channel_id=1, source_target_pairs={{0,96},{32,64},{64,32},{96,0},{1,97},{33,65},{65,33},{97,1},{2,98}... | collective-permute-start | bytes 786440 | tf_op jit(solution)/shard_map/ppermute | solution.py:288
  24.2 8.4 %collective-permute-start.8 = (bf16[512,256]{1,0:T(8,128)(2,1)S(1)}, bf16[512,256]{1,0:T(8,128)(2,1)S(1)}, u32[]{:S(2)}, u32[]{:S(2)}) collective-permute-start(bf16[512,256]{1,0:T(8,128)(2,1)S(1)} %collective-permute-done.5.refs_3_), channel_id=1, source_target_pairs={{0,32},{32,0},{64,96},{96,64},{1,33},{33,1},{65,97},{97,65},{2,34}... | collective-permute-start | bytes 786440 | tf_op jit(solution)/shard_map/ppermute | solution.py:287
  24.6 9.0 %collective-permute-start.9 = (bf16[512,256]{1,0:T(8,128)(2,1)S(1)}, bf16[512,256]{1,0:T(8,128)(2,1)S(1)}, u32[]{:S(2)}, u32[]{:S(2)}) collective-permute-start(bf16[512,256]{1,0:T(8,128)(2,1)S(1)} %collective-permute-done.5.refs_3_), channel_id=1, source_target_pairs={{0,96},{32,64},{64,32},{96,0},{1,97},{33,65},{65,33},{97,1},{2,98}... | collective-permute-start | bytes 786440 | tf_op jit(solution)/shard_map/ppermute | solution.py:288
  26.3 13.5 %slice-start = ((s8[8388608]{0:T(1024)(128)(4,1)}), s8[4194304]{0:T(1024)(128)(4,1)S(1)}, s32[]{:S(2)}) async-start(s8[8388608]{0:T(1024)(128)(4,1)} %bitcast.4), calls=%async_computation | async-start | bytes 8388608
  32.6 5.5 %collective-permute-start.10 = (bf16[512,256]{1,0:T(8,128)(2,1)S(1)}, bf16[512,256]{1,0:T(8,128)(2,1)S(1)}, u32[]{:S(2)}, u32[]{:S(2)}) collective-permute-start(bf16[512,256]{1,0:T(8,128)(2,1)S(1)} %collective-permute-done.7.refs_3_), channel_id=1, source_target_pairs={{0,32},{32,0},{64,96},{96,64},{1,33},{33,1},{65,97},{97,65},{2,34}... | collective-permute-start | bytes 786440 | tf_op jit(solution)/shard_map/ppermute | solution.py:287
  32.6 7.3 %collective-permute-start.11 = (bf16[512,256]{1,0:T(8,128)(2,1)S(1)}, bf16[512,256]{1,0:T(8,128)(2,1)S(1)}, u32[]{:S(2)}, u32[]{:S(2)}) collective-permute-start(bf16[512,256]{1,0:T(8,128)(2,1)S(1)} %collective-permute-done.8.refs_4_), channel_id=1, source_target_pairs={{0,96},{32,64},{64,32},{96,0},{1,97},{33,65},{65,33},{97,1},{2,98}... | collective-permute-start | bytes 786440 | tf_op jit(solution)/shard_map/ppermute | solution.py:288
  33.6 6.3 %slice-start.1 = ((s8[8388608]{0:T(1024)(128)(4,1)}), s8[4194304]{0:T(1024)(128)(4,1)S(1)}, s32[]{:S(2)}) async-start(s8[8388608]{0:T(1024)(128)(4,1)} %bitcast.4), calls=%async_computation.1 | async-start | bytes 8388608
  42.6 7.5 %collective-permute-start.12 = (bf16[32,4,2048]{2,1,0:T(4,128)(2,1)S(1)}, bf16[32,4,2048]{2,1,0:T(4,128)(2,1)S(1)}, u32[]{:S(2)}, u32[]{:S(2)}) collective-permute-start(bf16[32,4,2048]{2,1,0:T(4,128)(2,1)S(1)} %get-tuple-element.50), channel_id=1, source_target_pairs={{0,1},{1,0},{2,3},{3,2},{4,5},{5,4},{6,7},{7,6},{8,9},{9,8},{10,11... | collective-permute-start | bytes 1572872 | tf_op jit(solution)/shard_map/ppermute | solution.py:290
  50.2 3.4 %collective-permute-start.15 = (bf16[32,4,2048]{2,1,0:T(4,128)(2,1)S(1)}, bf16[32,4,2048]{2,1,0:T(4,128)(2,1)S(1)}, u32[]{:S(2)}, u32[]{:S(2)}) collective-permute-start(bf16[32,4,2048]{2,1,0:T(4,128)(2,1)S(1)} %get-tuple-element.55), channel_id=1, source_target_pairs={{0,1},{1,0},{2,3},{3,2},{4,5},{5,4},{6,7},{7,6},{8,9},{9,8},{10,11... | collective-permute-start | bytes 1572872 | tf_op jit(solution)/shard_map/ppermute | solution.py:290
  50.3 9.6 %collective-permute-start.13 = (bf16[16,4,2048]{2,1,0:T(4,128)(2,1)S(1)}, bf16[16,4,2048]{2,1,0:T(4,128)(2,1)S(1)}, u32[]{:S(2)}, u32[]{:S(2)}) collective-permute-start(bf16[16,4,2048]{2,1,0:T(4,128)(2,1)S(1)} %add_convert_fusion.2), channel_id=1, source_target_pairs={{0,2},{2,0},{1,3},{3,1},{4,6},{6,4},{5,7},{7,5},{8,10},{10,8},{9,1... | collective-permute-start | bytes 786440 | tf_op jit(solution)/shard_map/ppermute | solution.py:291
  54.1 19.8 %collective-permute-start.16 = (bf16[24,4,2048]{2,1,0:T(4,128)(2,1)S(1)}, bf16[24,4,2048]{2,1,0:T(4,128)(2,1)S(1)}, u32[]{:S(2)}, u32[]{:S(2)}) collective-permute-start(bf16[24,4,2048]{2,1,0:T(4,128)(2,1)S(1)} %slice.24), channel_id=1, source_target_pairs={{0,2},{2,0},{1,3},{3,1},{4,6},{6,4},{5,7},{7,5},{8,10},{10,8},{9,1... | collective-permute-start | bytes 1179656 | tf_op jit(solution)/shard_map/ppermute | solution.py:291
  56.1 17.8 %collective-permute-start.14 = (bf16[16,4,2048]{2,1,0:T(4,128)(2,1)S(1)}, bf16[16,4,2048]{2,1,0:T(4,128)(2,1)S(1)}, u32[]{:S(2)}, u32[]{:S(2)}) collective-permute-start(bf16[16,4,2048]{2,1,0:T(4,128)(2,1)S(1)} %add_convert_fusion.1), channel_id=1, source_target_pairs={{0,2},{2,0},{1,3},{3,1},{4,6},{6,4},{5,7},{7,5},{8,10},{10,8},{9,1... | collective-permute-start | bytes 786440 | tf_op jit(solution)/shard_map/ppermute | solution.py:291
  57.4 19.3 %collective-permute-start.20 = (bf16[8,4,2048]{2,1,0:T(4,128)(2,1)S(1)}, bf16[8,4,2048]{2,1,0:T(4,128)(2,1)S(1)}, u32[]{:S(2)}, u32[]{:S(2)}) collective-permute-start(bf16[8,4,2048]{2,1,0:T(4,128)(2,1)S(1)} %slice.25), channel_id=1, source_target_pairs={{0,2},{2,0},{1,3},{3,1},{4,6},{6,4},{5,7},{7,5},{8,10},{10,8},{9,1... | collective-permute-start | bytes 393224 | tf_op jit(solution)/shard_map/ppermute | solution.py:291
  74.1 4.8 %collective-permute-start.17 = (bf16[16,4,2048]{2,1,0:T(4,128)(2,1)S(1)}, bf16[16,4,2048]{2,1,0:T(4,128)(2,1)S(1)}, u32[]{:S(2)}, u32[]{:S(2)}) collective-permute-start(bf16[16,4,2048]{2,1,0:T(4,128)(2,1)S(1)} %add.24.refs_0_), channel_id=1, source_target_pairs={{0,1},{1,0},{2,3},{3,2},{4,5},{5,4},{6,7},{7,6},{8,9},{9,8},{10,11... | collective-permute-start | bytes 786440 | tf_op jit(solution)/shard_map/ppermute | solution.py:290
  75.9 3.0 %collective-permute-start.18 = (bf16[16,4,2048]{2,1,0:T(4,128)(2,1)S(1)}, bf16[16,4,2048]{2,1,0:T(4,128)(2,1)S(1)}, u32[]{:S(2)}, u32[]{:S(2)}) collective-permute-start(bf16[16,4,2048]{2,1,0:T(4,128)(2,1)S(1)} %add.25.refs_2_), channel_id=1, source_target_pairs={{0,1},{1,0},{2,3},{3,2},{4,5},{5,4},{6,7},{7,6},{8,9},{9,8},{10,11... | collective-permute-start | bytes 786440 | tf_op jit(solution)/shard_map/ppermute | solution.py:290
  76.2 2.7 %collective-permute-start.19 = (bf16[24,4,2048]{2,1,0:T(4,128)(2,1)S(1)}, bf16[24,4,2048]{2,1,0:T(4,128)(2,1)S(1)}, u32[]{:S(2)}, u32[]{:S(2)}) collective-permute-start(bf16[24,4,2048]{2,1,0:T(4,128)(2,1)S(1)} %slice_add_fusion.1.refs_4_), channel_id=1, source_target_pairs={{0,1},{1,0},{2,3},{3,2},{4,5},{5,4},{6,7},{7,6},{8,9},{9,8},{10,11... | collective-permute-start | bytes 1179656 | tf_op jit(solution)/shard_map/ppermute | solution.py:290
  76.8 2.0 %collective-permute-start.21 = (bf16[8,4,2048]{2,1,0:T(4,128)(2,1)S(1)}, bf16[8,4,2048]{2,1,0:T(4,128)(2,1)S(1)}, u32[]{:S(2)}, u32[]{:S(2)}) collective-permute-start(bf16[8,4,2048]{2,1,0:T(4,128)(2,1)S(1)} %slice_add_fusion.refs_6_), channel_id=1, source_target_pairs={{0,1},{1,0},{2,3},{3,2},{4,5},{5,4},{6,7},{7,6},{8,9},{9,8},{10,11... | collective-permute-start | bytes 393224 | tf_op jit(solution)/shard_map/ppermute | solution.py:290
  (8 other events, 37.9 us)

commit v8 on v7

--- a/solution.py
+++ b/solution.py
@@ -305,9 +305,9 @@
     m, acc = prefix(q, m, acc, [line])
     sent_y = after(b_y, m)
     b_yx1, b_yx3 = x1(sent_y), x3(sent_y)
-    m, acc = prefix(q, m, acc, [b_y, b_x1])
+    m, acc = prefix(q, m, acc, [b_y, b_x3])
     b_far, b_yfar = x1(after(b_x3, (b_yx1, m))), x3(after(b_yx1, m))
-    m, acc = prefix(q, m, acc, [b_x3, b_yx1, b_yx3])
+    m, acc = prefix(q, m, acc, [b_x1, b_yx1, b_yx3])
 
     shape = (requests, STEPS, out_weight.shape[1])
     last = [b_far, b_yfar]

time: 80.7 us -> 82.5 us (1.022)
  starting transfers between devices: 34 us -> 38.7 us
  waiting for transfers between devices: 23.7 us -> 20.9 us
    ppermute x6, starting transfers between devices: 8.27 us -> 11.4 us  [local(): swap_core = lambda a: lax.ppermute(a, 'core', [(0, 1), (1, 0)])]
    ppermute x3, waiting for transfers between devices: 4.2 us -> 1.36 us  [local(): x1 = lambda a: lax.ppermute(a, 'x', [(i, i ^ 1) for i in range(4)])]
    ppermute x3, starting transfers between devices: 4.5 us -> 6.26 us  [local(): x3 = lambda a: lax.ppermute(a, 'x', [(i, i ^ 3) for i in range(4)])]
  transfers between devices with their start and end apart: 22 -> 22, of which waited for: 8 -> 9; matrix products, arithmetic and copies ran while one was open for 2% -> 2% of each run, Pallas kernels for 19% -> 19%
where the time goes in v8:
time: 82.5 us; the launch traced here: 82.3 us
  starting transfers between devices  38.7 us (47%)
  waiting for transfers between devices  20.9 us (25%)
  Pallas kernels  19.4 us (24%)
  local copies, waits for them, and re-layouts  1.68 us (2%)
  other arithmetic  1.21 us (1%)
    ppermute x4, waiting for transfers between devices, local(): swap_y = lambda a: lax.ppermute(a, 'yhi', [(0, 1), (1, 0)])  14.4 us
    ppermute x6, starting transfers between devices, local(): swap_core = lambda a: lax.ppermute(a, 'core', [(0, 1), (1, 0)])  11.4 us
    pallas_call x3, Pallas kernels, prefix(): pl.pallas_call(lambda *refs: prefix_body(len(kvs), *refs), grid=(rows //...  8.38 us
    ppermute x4, starting transfers between devices, local(): swap_y = lambda a: lax.ppermute(a, 'yhi', [(0, 1), (1, 0)])  8.03 us
    ppermute x3, starting transfers between devices, local(): x3 = lambda a: lax.ppermute(a, 'x', [(i, i ^ 3) for i in range(4)])  6.26 us
    pallas_call x2, Pallas kernels, final(): pl.pallas_call(lambda *refs: final_body(len(kvs), *refs), grid=(1,), in_s...  5.31 us
    ppermute x1, starting transfers between devices, local(): odd = lambda a: lax.ppermute(a, 'z', O_PAIRS)  4.75 us
    pallas_call x2, Pallas kernels, suffix(): pl.pallas_call(lambda *refs: suffix_body(first, *refs), grid=(grid,), in_...  4.36 us
  transfers between devices with their start and end apart: 22, of which 9 were waited for; matrix products, arithmetic and copies ran while one was open for 2% of the time, Pallas kernels for 19%

profile of v8, /device:TPU:1, one launch (start us, length us, event | category | flops | bytes accessed | tf_op | source)
XLA Modules:
  0.0 82.3 jit_solution(7603354961857497330)
XLA Ops:
  0.0 2.5 %collective-permute-start = (bf16[64,128]{1,0:T(8,128)(2,1)}, bf16[64,128]{1,0:T(8,128)(2,1)S(1)}, u32[]{:S(2)}, u32[]{:S(2)}) collective-permute-start(bf16[64,128]{1,0:T(8,128)(2,1)} %k_ref.1), channel_id=1, source_target_pairs={{0,4},{4,0},{8,12},{12,8},{16,20},{20,16},{24,28},{28,24},{1,5},{5... | collective-permute-start | bytes 49160 | tf_op jit(solution)/shard_map/ppermute | solution.py:284
  4.0 1.2 %collective-permute-done.1.v_ref = bf16[64,128]{1,0:T(8,128)(2,1)S(1)} collective-permute-done((bf16[64,128]{1,0:T(8,128)(2,1)}, bf16[64,128]{1,0:T(8,128)(2,1)S(1)}, u32[]{:S(2)}, u32[]{:S(2)}) %collective-permute-start.1) | collective-permute-done | bytes 16416 | tf_op jit(solution)/shard_map/ppermute | solution.py:284
  5.3 4.8 %collective-permute-start.2 = (bf16[128,256]{1,0:T(8,128)(2,1)S(1)}, bf16[128,256]{1,0:T(8,128)(2,1)S(1)}, u32[]{:S(2)}, u32[]{:S(2)}) collective-permute-start(bf16[128,256]{1,0:T(8,128)(2,1)S(1)} %glue.3.refs_6_), channel_id=1, source_target_pairs={{0,28},{4,8},{8,4},{12,16},{16,12},{20,24},{24,20},{28,0},{1,29},{... | collective-permute-start | bytes 196616 | tf_op jit(solution)/shard_map/ppermute | solution.py:286
  10.1 2.2 %suffix.2 = (bf16[2048,128]{1,0:T(8,128)(2,1)S(1)}, f32[2048,128]{1,0:T(8,128)S(1)}, f32[2048,256]{1,0:T(8,128)S(1)}) custom-call(bf16[64,4,1024]{2,1,0:T(4,128)(2,1)S(1)} %copy-done.2, bf16[256,128]{1,0:T(8,128)(2,1)S(1)} %bitcast.10, bf16[256,128]{1,0:T(8,128)(2,1)S(1)} %bitcast.12, bf16[4096,128]{1,0:T(8,128)(2,1)S(1)} %bitcast.6, ...), custom_call_target="tpu_custom_call" | custom-call | flops 2000000000 | bytes 3000000 | tf_op jit(solution)/shard_map/suffix/pallas_call | solution.py:140
  12.3 1.7 %collective-permute-start.4 = (bf16[128,256]{1,0:T(8,128)(2,1)S(1)}, bf16[128,256]{1,0:T(8,128)(2,1)S(1)}, u32[]{:S(2)}, u32[]{:S(2)}) collective-permute-start(bf16[128,256]{1,0:T(8,128)(2,1)S(1)} %collective-permute-done.2.refs_6_), channel_id=1, source_target_pairs={{0,12},{4,24},{8,20},{12,0},{16,28},{20,8},{24,4},{28,16},{1,13},{... | collective-permute-start | bytes 196616 | tf_op jit(solution)/shard_map/ppermute | solution.py:285
  14.9 2.2 %suffix.3 = (bf16[2048,128]{1,0:T(8,128)(2,1)S(1)}, f32[2048,128]{1,0:T(8,128)S(1)}, f32[2048,256]{1,0:T(8,128)S(1)}) custom-call(bf16[64,4,1024]{2,1,0:T(4,128)(2,1)S(1)} %copy-done.2, bf16[256,128]{1,0:T(8,128)(2,1)S(1)} %bitcast.11, bf16[256,128]{1,0:T(8,128)(2,1)S(1)} %bitcast.13, ...), custom_call_target="tpu_custom_call", output_to_operand_aliasing={{0}: (7, {}), {1}: (8, {}), {2}: (9, {})} | custom-call | flops 2000000000 | bytes 3000000 | tf_op jit(solution)/shard_map/suffix/pallas_call | solution.py:140
  18.0 1.4 %collective-permute-start.5 = (bf16[512,256]{1,0:T(8,128)(2,1)S(1)}, bf16[512,256]{1,0:T(8,128)(2,1)S(1)}, u32[]{:S(2)}, u32[]{:S(2)}) collective-permute-start(bf16[512,256]{1,0:T(8,128)(2,1)S(1)} %pad_maximum_fusion.refs_3_), channel_id=1, source_target_pairs={{0,128},{128,0},{1,129},{129,1},{2,130},{130,2},{3,131},{131,3},{4... | collective-permute-start | bytes 786440 | tf_op jit(solution)/shard_map/ppermute | solution.py:289
  19.4 2.5 %collective-permute-start.6 = (bf16[512,256]{1,0:T(8,128)(2,1)S(1)}, bf16[512,256]{1,0:T(8,128)(2,1)S(1)}, u32[]{:S(2)}, u32[]{:S(2)}) collective-permute-start(bf16[512,256]{1,0:T(8,128)(2,1)S(1)} %pad_maximum_fusion.refs_3_), channel_id=1, source_target_pairs={{0,96},{32,64},{64,32},{96,0},{1,97},{33,65},{65,33},{97,1},{2,98}... | collective-permute-start | bytes 786440 | tf_op jit(solution)/shard_map/ppermute | solution.py:288
  21.9 1.8 %prefix.3 = (f32[2048,128]{1,0:T(8,128)S(1)}, f32[2048,256]{1,0:T(8,128)S(1)}) custom-call(bf16[2048,128]{1,0:T(8,128)(2,1)S(1)} %get-tuple-element.36.refs_0_, f32[2048,128]{1,0:T(8,128)S(1)} %get-tuple-element.37.refs_1_, f32[2048,256]{1,0:T(8,128)S(1)} %get-tuple-element.38.refs_2_, bf16[512,256]{1,0:T(8,128)(2,1)S(1)} %pad_maximum_fusion.refs_3_), custom_call_target="tpu_custom_call" | custom-call | flops 1073741824 | bytes 7000000 | tf_op jit(solution)/shard_map/prefix/pallas_call | solution.py:193
  25.2 2.0 %collective-permute-start.9 = (bf16[512,256]{1,0:T(8,128)(2,1)S(1)}, bf16[512,256]{1,0:T(8,128)(2,1)S(1)}, u32[]{:S(2)}, u32[]{:S(2)}) collective-permute-start(bf16[512,256]{1,0:T(8,128)(2,1)S(1)} %collective-permute-done.5.refs_3_), channel_id=1, source_target_pairs={{0,96},{32,64},{64,32},{96,0},{1,97},{33,65},{65,33},{97,1},{2,98}... | collective-permute-start | bytes 786440 | tf_op jit(solution)/shard_map/ppermute | solution.py:288
  27.3 2.7 %prefix.4 = (f32[2048,128]{1,0:T(8,128)S(1)}, f32[2048,256]{1,0:T(8,128)S(1)}) custom-call(bf16[2048,128]{1,0:T(8,128)(2,1)S(1)} %get-tuple-element.36.refs_0_, f32[2048,128]{1,0:T(8,128)S(1)} %get-tuple-element.40.refs_1_, f32[2048,256]{1,0:T(8,128)S(1)} %get-tuple-element.41.refs_2_, bf16[512,256]{1,0:T(8,128)(2,1)S(1)} %collective-permute-done.5.refs_3_, ...), custom_call_target="tpu_custom_call" | custom-call | flops 2147483648 | bytes 7000000 | tf_op jit(solution)/shard_map/prefix/pallas_call | solution.py:193
  30.1 1.8 %collective-permute-start.11 = (bf16[512,256]{1,0:T(8,128)(2,1)S(1)}, bf16[512,256]{1,0:T(8,128)(2,1)S(1)}, u32[]{:S(2)}, u32[]{:S(2)}) collective-permute-start(bf16[512,256]{1,0:T(8,128)(2,1)S(1)} %collective-permute-done.8.refs_4_), channel_id=1, source_target_pairs={{0,96},{32,64},{64,32},{96,0},{1,97},{33,65},{65,33},{97,1},{2,98}... | collective-permute-start | bytes 786440 | tf_op jit(solution)/shard_map/ppermute | solution.py:288
  32.3 1.3 %collective-permute-done.9.refs_5_ = bf16[512,256]{1,0:T(8,128)(2,1)S(1)} collective-permute-done((bf16[512,256]{1,0:T(8,128)(2,1)S(1)}, bf16[512,256]{1,0:T(8,128)(2,1)S(1)}, u32[]{:S(2)}, u32[]{:S(2)}) %collective-permute-start.9) | collective-permute-done | bytes 262176 | tf_op jit(solution)/shard_map/ppermute | solution.py:288
  33.6 3.9 %prefix.5 = (f32[2048,128]{1,0:T(8,128)S(1)}, f32[2048,256]{1,0:T(8,128)S(1)}) custom-call(bf16[2048,128]{1,0:T(8,128)(2,1)S(1)} %get-tuple-element.36.refs_0_, f32[2048,128]{1,0:T(8,128)S(1)} %get-tuple-element.42.refs_1_, f32[2048,256]{1,0:T(8,128)S(1)} %get-tuple-element.43.refs_2_, bf16[512,256]{1,0:T(8,128)(2,1)S(1)} %collective-permute-done.7.refs_3_, ...), custom_call_target="tpu_custom_call" | custom-call | flops 3221225472 | bytes 7000000 | tf_op jit(solution)/shard_map/prefix/pallas_call | solution.py:193
  39.1 2.7 %final.2 = (f32[32,4,2048]{2,1,0:T(4,128)S(1)}, bf16[32,4,2048]{2,1,0:T(4,128)(2,1)S(1)}) custom-call(bf16[2048,128]{1,0:T(8,128)(2,1)S(1)} %get-tuple-element.36.refs_0_, f32[2048,128]{1,0:T(8,128)S(1)} %get-tuple-element.45.refs_1_, f32[2048,256]{1,0:T(8,128)S(1)} %get-tuple-element.46.refs_2_, bf16[512,256]{1,0:T(8,128)(2,1)S(1)} %collective-permute-done.10.refs_3_, ...), custom_call_target="tpu_custom_call" | custom-call | flops 5368709120 | bytes 12000000 | tf_op jit(solution)/shard_map/final/pallas_call | solution.py:236
  41.8 7.7 %collective-permute-start.12 = (bf16[32,4,2048]{2,1,0:T(4,128)(2,1)S(1)}, bf16[32,4,2048]{2,1,0:T(4,128)(2,1)S(1)}, u32[]{:S(2)}, u32[]{:S(2)}) collective-permute-start(bf16[32,4,2048]{2,1,0:T(4,128)(2,1)S(1)} %get-tuple-element.50), channel_id=1, source_target_pairs={{0,1},{1,0},{2,3},{3,2},{4,5},{5,4},{6,7},{7,6},{8,9},{9,8},{10,11... | collective-permute-start | bytes 1572872 | tf_op jit(solution)/shard_map/ppermute | solution.py:290
  49.5 2.7 %final.3 = (f32[32,4,2048]{2,1,0:T(4,128)S(1)}, bf16[32,4,2048]{2,1,0:T(4,128)(2,1)S(1)}) custom-call(bf16[2048,128]{1,0:T(8,128)(2,1)S(1)} %get-tuple-element.36.refs_0_, f32[2048,128]{1,0:T(8,128)S(1)} %get-tuple-element.45.refs_1_, f32[2048,256]{1,0:T(8,128)S(1)} %get-tuple-element.46.refs_2_, bf16[512,256]{1,0:T(8,128)(2,1)S(1)} %collective-permute-done.10.refs_3_, ...), custom_call_target="tpu_custom_call" | custom-call | flops 5368709120 | bytes 12000000 | tf_op jit(solution)/shard_map/final/pallas_call | solution.py:236
  52.4 3.0 %collective-permute-start.13 = (bf16[16,4,2048]{2,1,0:T(4,128)(2,1)S(1)}, bf16[16,4,2048]{2,1,0:T(4,128)(2,1)S(1)}, u32[]{:S(2)}, u32[]{:S(2)}) collective-permute-start(bf16[16,4,2048]{2,1,0:T(4,128)(2,1)S(1)} %add_convert_fusion.2), channel_id=1, source_target_pairs={{0,2},{2,0},{1,3},{3,1},{4,6},{6,4},{5,7},{7,5},{8,10},{10,8},{9,1... | collective-permute-start | bytes 786440 | tf_op jit(solution)/shard_map/ppermute | solution.py:291
  55.9 1.9 %collective-permute-start.16 = (bf16[24,4,2048]{2,1,0:T(4,128)(2,1)S(1)}, bf16[24,4,2048]{2,1,0:T(4,128)(2,1)S(1)}, u32[]{:S(2)}, u32[]{:S(2)}) collective-permute-start(bf16[24,4,2048]{2,1,0:T(4,128)(2,1)S(1)} %slice.24), channel_id=1, source_target_pairs={{0,2},{2,0},{1,3},{3,1},{4,6},{6,4},{5,7},{7,5},{8,10},{10,8},{9,1... | collective-permute-start | bytes 1179656 | tf_op jit(solution)/shard_map/ppermute | solution.py:291
  58.0 1.3 %collective-permute-start.14 = (bf16[16,4,2048]{2,1,0:T(4,128)(2,1)S(1)}, bf16[16,4,2048]{2,1,0:T(4,128)(2,1)S(1)}, u32[]{:S(2)}, u32[]{:S(2)}) collective-permute-start(bf16[16,4,2048]{2,1,0:T(4,128)(2,1)S(1)} %add_convert_fusion.1), channel_id=1, source_target_pairs={{0,2},{2,0},{1,3},{3,1},{4,6},{6,4},{5,7},{7,5},{8,10},{10,8},{9,1... | collective-permute-start | bytes 786440 | tf_op jit(solution)/shard_map/ppermute | solution.py:291
  59.3 1.9 %collective-permute-start.20 = (bf16[8,4,2048]{2,1,0:T(4,128)(2,1)S(1)}, bf16[8,4,2048]{2,1,0:T(4,128)(2,1)S(1)}, u32[]{:S(2)}, u32[]{:S(2)}) collective-permute-start(bf16[8,4,2048]{2,1,0:T(4,128)(2,1)S(1)} %slice.25), channel_id=1, source_target_pairs={{0,2},{2,0},{1,3},{3,1},{4,6},{6,4},{5,7},{7,5},{8,10},{10,8},{9,1... | collective-permute-start | bytes 393224 | tf_op jit(solution)/shard_map/ppermute | solution.py:291
  61.5 14.0 %collective-permute-done.14 = bf16[16,4,2048]{2,1,0:T(4,128)(2,1)S(1)} collective-permute-done((bf16[16,4,2048]{2,1,0:T(4,128)(2,1)S(1)}, bf16[16,4,2048]{2,1,0:T(4,128)(2,1)S(1)}, u32[]{:S(2)}, u32[]{:S(2)}) %collective-permute-start.14) | collective-permute-done | bytes 262176 | tf_op jit(solution)/shard_map/ppermute | solution.py:291
  75.7 2.2 %collective-permute-start.17 = (bf16[16,4,2048]{2,1,0:T(4,128)(2,1)S(1)}, bf16[16,4,2048]{2,1,0:T(4,128)(2,1)S(1)}, u32[]{:S(2)}, u32[]{:S(2)}) collective-permute-start(bf16[16,4,2048]{2,1,0:T(4,128)(2,1)S(1)} %add.24.refs_0_), channel_id=1, source_target_pairs={{0,1},{1,0},{2,3},{3,2},{4,5},{5,4},{6,7},{7,6},{8,9},{9,8},{10,11... | collective-permute-start | bytes 786440 | tf_op jit(solution)/shard_map/ppermute | solution.py:290
  80.8 1.4 %place.1 = bf16[64,4,4096]{2,1,0:T(4,128)(2,1)} custom-call(bf16[16,4,2048]{2,1,0:T(4,128)(2,1)S(1)} %add.24.refs_0_, bf16[16,4,2048]{2,1,0:T(4,128)(2,1)S(1)} %collective-permute-done.17.refs_1_, bf16[16,4,2048]{2,1,0:T(4,128)(2,1)S(1)} %add.25.refs_2_, bf16[16,4,2048]{2,1,0:T(4,128)(2,1)S(1)} %collective-permute-done.18.refs_3_, ...), custom_call_target="tpu_custom_call" | custom-call | tf_op jit(solution)/shard_map/place/pallas_call | solution.py:271
  (61 shorter events, 11.3 us)
Async XLA Ops:
  0.0 4.0 %collective-permute-start = (bf16[64,128]{1,0:T(8,128)(2,1)}, bf16[64,128]{1,0:T(8,128)(2,1)S(1)}, u32[]{:S(2)}, u32[]{:S(2)}) collective-permute-start(bf16[64,128]{1,0:T(8,128)(2,1)} %k_ref.1), channel_id=1, source_target_pairs={{0,4},{4,0},{8,12},{12,8},{16,20},{20,16},{24,28},{28,24},{1,5},{5... | collective-permute-start | bytes 49160 | tf_op jit(solution)/shard_map/ppermute | solution.py:284
  2.5 2.8 %collective-permute-start.1 = (bf16[64,128]{1,0:T(8,128)(2,1)}, bf16[64,128]{1,0:T(8,128)(2,1)S(1)}, u32[]{:S(2)}, u32[]{:S(2)}) collective-permute-start(bf16[64,128]{1,0:T(8,128)(2,1)} %v_ref.1), channel_id=1, source_target_pairs={{0,4},{4,0},{8,12},{12,8},{16,20},{20,16},{24,28},{28,24},{1,5},{5... | collective-permute-start | bytes 49160 | tf_op jit(solution)/shard_map/ppermute | solution.py:284
  3.9 6.1 %copy-start = (bf16[64,64,128]{2,1,0:T(8,128)(2,1)S(1)}, bf16[64,64,128]{2,1,0:T(8,128)(2,1)}, u32[]{:S(2)}) copy-start(bf16[64,64,128]{2,1,0:T(8,128)(2,1)} %param.12) | copy-start | bytes 3145732
  5.3 7.0 %collective-permute-start.2 = (bf16[128,256]{1,0:T(8,128)(2,1)S(1)}, bf16[128,256]{1,0:T(8,128)(2,1)S(1)}, u32[]{:S(2)}, u32[]{:S(2)}) collective-permute-start(bf16[128,256]{1,0:T(8,128)(2,1)S(1)} %glue.3.refs_6_), channel_id=1, source_target_pairs={{0,28},{4,8},{8,4},{12,16},{16,12},{20,24},{24,20},{28,0},{1,29},{... | collective-permute-start | bytes 196616 | tf_op jit(solution)/shard_map/ppermute | solution.py:286
  12.3 5.7 %collective-permute-start.4 = (bf16[128,256]{1,0:T(8,128)(2,1)S(1)}, bf16[128,256]{1,0:T(8,128)(2,1)S(1)}, u32[]{:S(2)}, u32[]{:S(2)}) collective-permute-start(bf16[128,256]{1,0:T(8,128)(2,1)S(1)} %collective-permute-done.2.refs_6_), channel_id=1, source_target_pairs={{0,12},{4,24},{8,20},{12,0},{16,28},{20,8},{24,4},{28,16},{1,13},{... | collective-permute-start | bytes 196616 | tf_op jit(solution)/shard_map/ppermute | solution.py:285
  14.0 4.0 %collective-permute-start.3 = (bf16[128,256]{1,0:T(8,128)(2,1)S(1)}, bf16[128,256]{1,0:T(8,128)(2,1)S(1)}, u32[]{:S(2)}, u32[]{:S(2)}) collective-permute-start(bf16[128,256]{1,0:T(8,128)(2,1)S(1)} %collective-permute-done.2.refs_6_), channel_id=1, source_target_pairs={{0,4},{4,0},{8,12},{12,8},{16,20},{20,16},{24,28},{28,24},{1,5},{5... | collective-permute-start | bytes 196616 | tf_op jit(solution)/shard_map/ppermute | solution.py:284
  18.0 5.7 %collective-permute-start.5 = (bf16[512,256]{1,0:T(8,128)(2,1)S(1)}, bf16[512,256]{1,0:T(8,128)(2,1)S(1)}, u32[]{:S(2)}, u32[]{:S(2)}) collective-permute-start(bf16[512,256]{1,0:T(8,128)(2,1)S(1)} %pad_maximum_fusion.refs_3_), channel_id=1, source_target_pairs={{0,128},{128,0},{1,129},{129,1},{2,130},{130,2},{3,131},{131,3},{4... | collective-permute-start | bytes 786440 | tf_op jit(solution)/shard_map/ppermute | solution.py:289
  19.4 7.9 %collective-permute-start.6 = (bf16[512,256]{1,0:T(8,128)(2,1)S(1)}, bf16[512,256]{1,0:T(8,128)(2,1)S(1)}, u32[]{:S(2)}, u32[]{:S(2)}) collective-permute-start(bf16[512,256]{1,0:T(8,128)(2,1)S(1)} %pad_maximum_fusion.refs_3_), channel_id=1, source_target_pairs={{0,96},{32,64},{64,32},{96,0},{1,97},{33,65},{65,33},{97,1},{2,98}... | collective-permute-start | bytes 786440 | tf_op jit(solution)/shard_map/ppermute | solution.py:288
  23.7 6.3 %collective-permute-start.8 = (bf16[512,256]{1,0:T(8,128)(2,1)S(1)}, bf16[512,256]{1,0:T(8,128)(2,1)S(1)}, u32[]{:S(2)}, u32[]{:S(2)}) collective-permute-start(bf16[512,256]{1,0:T(8,128)(2,1)S(1)} %collective-permute-done.5.refs_3_), channel_id=1, source_target_pairs={{0,32},{32,0},{64,96},{96,64},{1,33},{33,1},{65,97},{97,65},{2,34}... | collective-permute-start | bytes 786440 | tf_op jit(solution)/shard_map/ppermute | solution.py:287
  24.5 7.7 %collective-permute-start.7 = (bf16[512,256]{1,0:T(8,128)(2,1)S(1)}, bf16[512,256]{1,0:T(8,128)(2,1)S(1)}, u32[]{:S(2)}, u32[]{:S(2)}) collective-permute-start(bf16[512,256]{1,0:T(8,128)(2,1)S(1)} %pad_maximum_fusion.refs_3_), channel_id=1, source_target_pairs={{0,32},{32,0},{64,96},{96,64},{1,33},{33,1},{65,97},{97,65},{2,34}... | collective-permute-start | bytes 786440 | tf_op jit(solution)/shard_map/ppermute | solution.py:287
  25.2 8.4 %collective-permute-start.9 = (bf16[512,256]{1,0:T(8,128)(2,1)S(1)}, bf16[512,256]{1,0:T(8,128)(2,1)S(1)}, u32[]{:S(2)}, u32[]{:S(2)}) collective-permute-start(bf16[512,256]{1,0:T(8,128)(2,1)S(1)} %collective-permute-done.5.refs_3_), channel_id=1, source_target_pairs={{0,96},{32,64},{64,32},{96,0},{1,97},{33,65},{65,33},{97,1},{2,98}... | collective-permute-start | bytes 786440 | tf_op jit(solution)/shard_map/ppermute | solution.py:288
  27.3 11.8 %slice-start = ((s8[8388608]{0:T(1024)(128)(4,1)}), s8[4194304]{0:T(1024)(128)(4,1)S(1)}, s32[]{:S(2)}) async-start(s8[8388608]{0:T(1024)(128)(4,1)} %bitcast.4), calls=%async_computation | async-start | bytes 8388608
  30.0 8.4 %collective-permute-start.10 = (bf16[512,256]{1,0:T(8,128)(2,1)S(1)}, bf16[512,256]{1,0:T(8,128)(2,1)S(1)}, u32[]{:S(2)}, u32[]{:S(2)}) collective-permute-start(bf16[512,256]{1,0:T(8,128)(2,1)S(1)} %collective-permute-done.6.refs_4_), channel_id=1, source_target_pairs={{0,32},{32,0},{64,96},{96,64},{1,33},{33,1},{65,97},{97,65},{2,34}... | collective-permute-start | bytes 786440 | tf_op jit(solution)/shard_map/ppermute | solution.py:287
  30.1 9.0 %collective-permute-start.11 = (bf16[512,256]{1,0:T(8,128)(2,1)S(1)}, bf16[512,256]{1,0:T(8,128)(2,1)S(1)}, u32[]{:S(2)}, u32[]{:S(2)}) collective-permute-start(bf16[512,256]{1,0:T(8,128)(2,1)S(1)} %collective-permute-done.8.refs_4_), channel_id=1, source_target_pairs={{0,96},{32,64},{64,32},{96,0},{1,97},{33,65},{65,33},{97,1},{2,98}... | collective-permute-start | bytes 786440 | tf_op jit(solution)/shard_map/ppermute | solution.py:288
  41.8 10.4 %collective-permute-start.12 = (bf16[32,4,2048]{2,1,0:T(4,128)(2,1)S(1)}, bf16[32,4,2048]{2,1,0:T(4,128)(2,1)S(1)}, u32[]{:S(2)}, u32[]{:S(2)}) collective-permute-start(bf16[32,4,2048]{2,1,0:T(4,128)(2,1)S(1)} %get-tuple-element.50), channel_id=1, source_target_pairs={{0,1},{1,0},{2,3},{3,2},{4,5},{5,4},{6,7},{7,6},{8,9},{9,8},{10,11... | collective-permute-start | bytes 1572872 | tf_op jit(solution)/shard_map/ppermute | solution.py:290
  52.3 3.1 %collective-permute-start.15 = (bf16[32,4,2048]{2,1,0:T(4,128)(2,1)S(1)}, bf16[32,4,2048]{2,1,0:T(4,128)(2,1)S(1)}, u32[]{:S(2)}, u32[]{:S(2)}) collective-permute-start(bf16[32,4,2048]{2,1,0:T(4,128)(2,1)S(1)} %get-tuple-element.55), channel_id=1, source_target_pairs={{0,1},{1,0},{2,3},{3,2},{4,5},{5,4},{6,7},{7,6},{8,9},{9,8},{10,11... | collective-permute-start | bytes 1572872 | tf_op jit(solution)/shard_map/ppermute | solution.py:290
  52.4 9.1 %collective-permute-start.13 = (bf16[16,4,2048]{2,1,0:T(4,128)(2,1)S(1)}, bf16[16,4,2048]{2,1,0:T(4,128)(2,1)S(1)}, u32[]{:S(2)}, u32[]{:S(2)}) collective-permute-start(bf16[16,4,2048]{2,1,0:T(4,128)(2,1)S(1)} %add_convert_fusion.2), channel_id=1, source_target_pairs={{0,2},{2,0},{1,3},{3,1},{4,6},{6,4},{5,7},{7,5},{8,10},{10,8},{9,1... | collective-permute-start | bytes 786440 | tf_op jit(solution)/shard_map/ppermute | solution.py:291
  55.9 19.6 %collective-permute-start.16 = (bf16[24,4,2048]{2,1,0:T(4,128)(2,1)S(1)}, bf16[24,4,2048]{2,1,0:T(4,128)(2,1)S(1)}, u32[]{:S(2)}, u32[]{:S(2)}) collective-permute-start(bf16[24,4,2048]{2,1,0:T(4,128)(2,1)S(1)} %slice.24), channel_id=1, source_target_pairs={{0,2},{2,0},{1,3},{3,1},{4,6},{6,4},{5,7},{7,5},{8,10},{10,8},{9,1... | collective-permute-start | bytes 1179656 | tf_op jit(solution)/shard_map/ppermute | solution.py:291
  58.0 17.6 %collective-permute-start.14 = (bf16[16,4,2048]{2,1,0:T(4,128)(2,1)S(1)}, bf16[16,4,2048]{2,1,0:T(4,128)(2,1)S(1)}, u32[]{:S(2)}, u32[]{:S(2)}) collective-permute-start(bf16[16,4,2048]{2,1,0:T(4,128)(2,1)S(1)} %add_convert_fusion.1), channel_id=1, source_target_pairs={{0,2},{2,0},{1,3},{3,1},{4,6},{6,4},{5,7},{7,5},{8,10},{10,8},{9,1... | collective-permute-start | bytes 786440 | tf_op jit(solution)/shard_map/ppermute | solution.py:291
  59.3 19.7 %collective-permute-start.20 = (bf16[8,4,2048]{2,1,0:T(4,128)(2,1)S(1)}, bf16[8,4,2048]{2,1,0:T(4,128)(2,1)S(1)}, u32[]{:S(2)}, u32[]{:S(2)}) collective-permute-start(bf16[8,4,2048]{2,1,0:T(4,128)(2,1)S(1)} %slice.25), channel_id=1, source_target_pairs={{0,2},{2,0},{1,3},{3,1},{4,6},{6,4},{5,7},{7,5},{8,10},{10,8},{9,1... | collective-permute-start | bytes 393224 | tf_op jit(solution)/shard_map/ppermute | solution.py:291
  75.7 5.0 %collective-permute-start.17 = (bf16[16,4,2048]{2,1,0:T(4,128)(2,1)S(1)}, bf16[16,4,2048]{2,1,0:T(4,128)(2,1)S(1)}, u32[]{:S(2)}, u32[]{:S(2)}) collective-permute-start(bf16[16,4,2048]{2,1,0:T(4,128)(2,1)S(1)} %add.24.refs_0_), channel_id=1, source_target_pairs={{0,1},{1,0},{2,3},{3,2},{4,5},{5,4},{6,7},{7,6},{8,9},{9,8},{10,11... | collective-permute-start | bytes 786440 | tf_op jit(solution)/shard_map/ppermute | solution.py:290
  78.0 2.7 %collective-permute-start.18 = (bf16[16,4,2048]{2,1,0:T(4,128)(2,1)S(1)}, bf16[16,4,2048]{2,1,0:T(4,128)(2,1)S(1)}, u32[]{:S(2)}, u32[]{:S(2)}) collective-permute-start(bf16[16,4,2048]{2,1,0:T(4,128)(2,1)S(1)} %add.25.refs_2_), channel_id=1, source_target_pairs={{0,1},{1,0},{2,3},{3,2},{4,5},{5,4},{6,7},{7,6},{8,9},{9,8},{10,11... | collective-permute-start | bytes 786440 | tf_op jit(solution)/shard_map/ppermute | solution.py:290
  78.3 2.4 %collective-permute-start.19 = (bf16[24,4,2048]{2,1,0:T(4,128)(2,1)S(1)}, bf16[24,4,2048]{2,1,0:T(4,128)(2,1)S(1)}, u32[]{:S(2)}, u32[]{:S(2)}) collective-permute-start(bf16[24,4,2048]{2,1,0:T(4,128)(2,1)S(1)} %slice_add_fusion.1.refs_4_), channel_id=1, source_target_pairs={{0,1},{1,0},{2,3},{3,2},{4,5},{5,4},{6,7},{7,6},{8,9},{9,8},{10,11... | collective-permute-start | bytes 1179656 | tf_op jit(solution)/shard_map/ppermute | solution.py:290
  79.0 1.7 %collective-permute-start.21 = (bf16[8,4,2048]{2,1,0:T(4,128)(2,1)S(1)}, bf16[8,4,2048]{2,1,0:T(4,128)(2,1)S(1)}, u32[]{:S(2)}, u32[]{:S(2)}) collective-permute-start(bf16[8,4,2048]{2,1,0:T(4,128)(2,1)S(1)} %slice_add_fusion.refs_6_), channel_id=1, source_target_pairs={{0,1},{1,0},{2,3},{3,2},{4,5},{5,4},{6,7},{7,6},{8,9},{9,8},{10,11... | collective-permute-start | bytes 393224 | tf_op jit(solution)/shard_map/ppermute | solution.py:290
  (8 other events, 37.3 us)
